TPU v7x, 256 devices: a whole 4x4x8 slice. The times are simulated.
256 devices in a mesh: row: 8 (over x, y_hi), col: 32 (over z, y_lo, core).
Axes of the slice: x: 4, y: 4 (y_hi: 2, y_lo: 2; y = y_hi * 2 + y_lo), z: 8, core: 2. Of those that a mesh axis runs over, the one named last changes fastest.
Arguments:
- node_features: float32 [32768, 256], P(('col', 'row')), may hold values from -6 to 6
- weight: float32 [256, 256], replicated, may hold values from -0.375 to 0.375
- bias: float32 [256], replicated, may hold values from -3 to 3
- tile_values: float32 [8, 32, 12, 128, 128], P('row', 'col'), may hold values from -0.25 to 0.25
- tile_coords: int32 [8, 32, 12, 2], P('row', 'col'), may hold values from 0 to 31, as said below
- tile_count: int32 [8, 32], P('row', 'col'), may hold values from 1 to 12, as said below
- cotangent: float32 [32768, 256], P(('row', 'col')), may hold values from -6 to 6
Outputs:
- output: float32 [32768, 256], P(('row', 'col'))
- input_grad: float32 [32768, 256], P(('col', 'row'))
- weight_grad: float32 [256, 256], replicated
- bias_grad: float32 [256], replicated
Inputs may be any that keep to these rules, and one draw needn't show every extreme that they name: tile_coords[..., 0] is a tile row within the block row of 4096 nodes, tile_coords[..., 1] a tile column within the block column of 1024 nodes, each below that block's number of tiles; a position may stand in several slots, whose blocks add. Slots 0 to tile_count - 1 of a device are live; some device has all 12 live.
All inputs are finite; a program needn't handle non-finite values.
Results may differ from a plain program's by a relative error of at most 0.0003.
Values sent between devices are 32-bit elements; how exact they have to be, the bound alone decides.
No kernel may reach another device: no remote copies, remote signals or barrier semaphores. Data moves between devices by JAX's collectives and lax.ppermute only.
A program may use at most 64 MiB of HBM per device.

v0:
```python
import math

import jax
import jax.numpy as jnp
from jax import lax
from jax.sharding import PartitionSpec as P


def body(node_features, weight, bias, tile_values, tile_coords, tile_count, cotangent):
    precise = lax.Precision.HIGHEST
    values = tile_values[0, 0]
    positions = tile_coords[0, 0]
    live_count = tile_count[0, 0]
    capacity = values.shape[0]
    tile_size = values.shape[1]
    local_nodes, features_width = node_features.shape
    row_count = lax.axis_size("row")
    col_count = lax.axis_size("col")
    row_tiles = local_nodes * col_count // tile_size
    col_tiles = local_nodes * row_count // tile_size
    live_mask = (jnp.arange(capacity, dtype=jnp.int32) < live_count).astype(jnp.float32)[
        :, None, None
    ]
    factor = 1.0 / math.sqrt(local_nodes * row_count * col_count)
    source = jnp.dot(node_features, weight, precision=precise)
    column = lax.all_gather(source, "row", axis=0, tiled=True)
    picked = jnp.take(column.reshape(col_tiles, tile_size, features_width), positions[:, 1], axis=0)
    products = jnp.einsum("kij,kjf->kif", values, picked, precision=precise) * live_mask
    partial_value = jax.ops.segment_sum(products, positions[:, 0], num_segments=row_tiles)
    partial_flat = partial_value.reshape(row_tiles * tile_size, features_width)
    summed = lax.psum_scatter(partial_flat, "col", scatter_dimension=0, tiled=True)
    pre = summed + bias
    sigma = jax.nn.sigmoid(pre)
    output = pre * sigma
    pre_grad = cotangent * (sigma * (1.0 + pre * (1.0 - sigma)))
    rows_gathered = lax.all_gather(pre_grad, "col", axis=0, tiled=True)
    back_picked = jnp.take(
        rows_gathered.reshape(row_tiles, tile_size, features_width), positions[:, 0], axis=0
    )
    back_products = jnp.einsum("kji,kjf->kif", values, back_picked, precision=precise) * live_mask
    back_partial = jax.ops.segment_sum(back_products, positions[:, 1], num_segments=col_tiles)
    back_summed = lax.psum_scatter(
        back_partial.reshape(col_tiles * tile_size, features_width),
        "row",
        scatter_dimension=0,
        tiled=True,
    )
    input_grad = jnp.dot(back_summed, weight.T, precision=precise)
    weight_term = jnp.dot(node_features.T, back_summed, precision=precise) * factor
    bias_term = jnp.sum(pre_grad, axis=0) * factor
    weight_grad, bias_grad = lax.psum((weight_term, bias_term), ("row", "col"))
    return (output, input_grad, weight_grad, bias_grad)


def solution(mesh):
    in_specs = (
        P(("col", "row"), None),
        P(),
        P(),
        P("row", "col", None, None, None),
        P("row", "col", None, None),
        P("row", "col"),
        P(("row", "col"), None),
    )
    out_specs = (P(("row", "col"), None), P(("col", "row"), None), P(), P())
    return jax.shard_map(body, mesh=mesh, in_specs=in_specs, out_specs=out_specs, check_vma=False)
```

profile of v0, /device:TPU:2, one launch (start us, length us, event | category | flops | bytes accessed | tf_op | source)
XLA Modules:
  0.0 623.7 jit_solution(6903761287918671745)
XLA Ops:
  7.2 0.0 copy-start
  7.2 0.0 all-gather.3.cloned.1.call-start
  7.2 2.0 fusion.21
  9.2 0.0 all-gather.3.cloned.1.call-update
  9.3 0.0 reduce-scatter.3.cloned.1.call-start
  10.0 0.8 fusion.19
  10.7 0.8 and_bitcast_fusion
  11.5 54.9 %all-gather.3.cloned.1.call-done = f32[1024,256]{1,0:T(8,128)} async-done(((f32[128,256]{1,0:T(8,128)}), f32[1024,256]{1,0:T(8,128)}) %all-gather.3.cloned.1.call-update) | async-done | bytes 1048592 | tf_op jit(solution)/shard_map/all_gather | solution.py:26
  66.4 1.9 gather_fusion
  68.3 0.0 copy-done
  68.3 4.2 multiply_bitcast_fusion.1
  72.5 1.9 copy.15
  74.4 2.4 broadcast_in_dim.26
  76.8 4.1 scatter_fusion
  80.8 0.0 copy-start.4
  80.8 0.0 copy-start.5
  80.8 0.0 reduce-scatter.3.cloned.1.call-update
  80.9 0.0 all-gather.5.cloned.1.call-start
  80.9 122.2 %reduce-scatter.3.cloned.1.call-done = f32[128,256]{1,0:T(8,128)} async-done(((f32[4096,256]{1,0:T(8,128)}), f32[128,256]{1,0:T(8,128)}) %reduce-scatter.3.cloned.1.call-update) | async-done | bytes 131088 | tf_op jit(solution)/shard_map/reduce_scatter | solution.py:31
  203.1 0.0 copy-done.4
  203.1 0.0 copy-done.5
  203.1 1.7 fusion.20
  204.8 0.0 all-gather.5.cloned.1.call-update
  204.8 0.0 reduce-scatter.5.cloned.1.call-start
  204.9 65.5 %all-gather.5.cloned.1.call-done = f32[4096,256]{1,0:T(8,128)} async-done(((f32[128,256]{1,0:T(8,128)}), f32[4096,256]{1,0:T(8,128)}) %all-gather.5.cloned.1.call-update) | async-done | bytes 4194320 | tf_op jit(solution)/shard_map/all_gather | solution.py:36
  270.4 2.8 gather_fusion.1
  273.3 4.2 multiply_bitcast_fusion
  277.5 1.9 copy.17
  279.3 0.1 broadcast_in_dim.29
  279.4 0.0 copy-start.3
  279.4 1.8 scatter_fusion.1
  281.3 0.0 copy-start.1
  281.3 0.0 copy-start.2
  281.3 0.9 copy-done.1
  282.3 0.0 reduce-scatter.5.cloned.1.call-update
  282.3 0.0 all-reduce.2.cloned.1.call-start
  282.3 75.9 %psum.15 = f32[256]{0:T(256)} all-reduce(f32[256]{0:T(256)S(1)} %broadcast_multiply_fusion), channel_id=1, replica_groups=mesh['row'=8,'col'=32] {'row','col'}, use_global_device_ids=true, to_apply=%region_6.7 | all-reduce | flops 256 | bytes 2048 | tf_op jit(solution)/shard_map/psum | solution.py:51
  358.2 0.8 reduce-scatter.5.cloned.1.call-done
  359.1 0.0 copy-done.3
  359.1 2.0 fusion.8
  361.1 0.0 all-reduce.2.cloned.1.call-update
  361.1 0.0 copy-done.2
  361.1 2.0 fusion.22
  363.1 252.3 %all-reduce.2.cloned.1.call-done = f32[256,256]{0,1:T(8,128)} async-done(((f32[256,256]{0,1:T(8,128)}), f32[256,256]{0,1:T(8,128)}) %all-reduce.2.cloned.1.call-update) | async-done | bytes 262160 | tf_op jit(solution)/shard_map/psum | solution.py:51
  615.4 1.8 copy.18
  (4 shorter events, 0.0 us)
Async XLA Ops:
  7.2 61.1 %copy-start = (f32[1,1,12,128,128]{4,3,2,1,0:T(8,128)S(1)}, f32[1,1,12,128,128]{4,3,2,1,0:T(8,128)}, u32[]{:S(2)}) copy-start(f32[1,1,12,128,128]{4,3,2,1,0:T(8,128)} %param.10) | copy-start | bytes 2359300
  7.2 59.2 %all-gather.3.cloned.1.call-start = ((), (), s32[]{:S(2)}) async-start(), calls=%async_computation.2 | async-start | bytes 1179648 | tf_op jit(solution)/shard_map/all_gather | solution.py:26
  9.3 193.9 %reduce-scatter.3.cloned.1.call-start = ((), (), s32[]{:S(2)}) async-start(), calls=%async_computation.3 | async-start | bytes 4325376 | tf_op jit(solution)/shard_map/reduce_scatter | solution.py:31
  80.8 122.3 %copy-start.4 = (f32[128,256]{1,0:T(8,128)S(1)}, f32[128,256]{1,0:T(8,128)}, u32[]{:S(2)}) copy-start(f32[128,256]{1,0:T(8,128)} %param.13) | copy-start | bytes 393220
  80.8 122.3 %copy-start.5 = (f32[256]{0:T(256)S(1)}, f32[256]{0:T(256)}, u32[]{:S(2)}) copy-start(f32[256]{0:T(256)} %param.9) | copy-start | bytes 3076
  80.9 189.6 %all-gather.5.cloned.1.call-start = ((), (), s32[]{:S(2)}) async-start(), calls=%async_computation.4 | async-start | bytes 4325376 | tf_op jit(solution)/shard_map/all_gather | solution.py:36
  204.8 154.2 %reduce-scatter.5.cloned.1.call-start = ((), (), s32[]{:S(2)}) async-start(), calls=%async_computation.5 | async-start | bytes 1179648 | tf_op jit(solution)/shard_map/reduce_scatter | solution.py:42
  279.4 79.6 %copy-start.3 = (f32[128,256]{1,0:T(8,128)S(1)}, f32[128,256]{1,0:T(8,128)}, u32[]{:S(2)}) copy-start(f32[128,256]{1,0:T(8,128)} %param.7) | copy-start | bytes 393220
  281.3 1.0 copy-start.1
  281.3 79.8 %copy-start.2 = (f32[256,256]{1,0:T(8,128)S(1)}, f32[256,256]{1,0:T(8,128)}, u32[]{:S(2)}) copy-start(f32[256,256]{1,0:T(8,128)} %param.8) | copy-start | bytes 786436
  282.3 333.1 %all-reduce.2.cloned.1.call-start = ((), (), s32[]{:S(2)}) async-start(), calls=%async_computation.6 | async-start | bytes 524288 | tf_op jit(solution)/shard_map/psum | solution.py:51
Sparse Core Ops, SparseCore 0:
  11.2 55.1 all-gather.2
  81.0 122.0 reduce-scatter.2
  205.6 64.8 all-gather.4
  282.4 76.6 reduce-scatter.4
  365.8 249.5 all-reduce.1
where the time goes:
time: 624 us
  waiting for transfers between devices  496 us (79%)
  blocking collectives  75.9 us (12%)
  between operations  14.5 us (2%)
  matrix products  14.4 us (2%)
  local copies, waits for them, and re-layouts  13.7 us (2%)
  other arithmetic  9.11 us (1%)
    psum x1, waiting for transfers between devices, body(): weight_grad, bias_grad = lax.psum((weight_term, bias_term), ('row', 'col'))  252 us
    reduce_scatter x1, waiting for transfers between devices, body(): lax.psum_scatter(partial_flat, 'col', scatter_dimension=0, tiled=True)  122 us
    psum x1, blocking collectives, body(): weight_grad, bias_grad = lax.psum((weight_term, bias_term), ('row', 'col'))  75.9 us
    all_gather x1, waiting for transfers between devices, body(): rows_gathered = lax.all_gather(pre_grad, 'col', axis=0, tiled=True)  65.5 us
    all_gather x1, waiting for transfers between devices, body(): column = lax.all_gather(source, 'row', axis=0, tiled=True)  54.9 us
  transfers between devices with their start and end apart: 5, of which 5 were waited for; matrix products, arithmetic and copies ran while one was open for 1% of the time, Pallas kernels for 0%

commit v1 on v0

v1 whole, which is shorter than its diff:
```python
import math

import jax
import jax.numpy as jnp
from jax import lax
from jax.experimental import pallas as pl
from jax.experimental.pallas import tpu as pltpu
from jax.sharding import PartitionSpec as P

Z, YL = 8, 2
TILE = 128


def col_pairs(move):
    pairs = []
    for z in range(Z):
        for y in range(YL):
            for core in range(2):
                a, b, c = move(z, y, core)
                pairs.append(((z * YL + y) * 2 + core, (a * YL + b) * 2 + c))
    return pairs


CORE_SWAP = col_pairs(lambda z, y, core: (z, y, 1 - core))
Y_SWAP = col_pairs(lambda z, y, core: (z, 1 - y, core))
Z_GROUPS = [[(z * YL + y) * 2 + core for z in range(Z)] for y in range(YL) for core in range(2)]


def split(value):
    high = value.astype(jnp.bfloat16)
    low = (value - high.astype(jnp.float32)).astype(jnp.bfloat16)
    return high, low


def dot3(left, right, contract):
    def one(a, b):
        return lax.dot_general(a, b, (contract, ((), ())), preferred_element_type=jnp.float32)

    return one(left[0], right[0]) + (one(left[0], right[1]) + one(left[1], right[0]))


def forward_kernel(place, count, core, values, features, keep, send, total, high, low, sems):
    total[...] = jnp.zeros_like(total)
    for j in range(features.shape[0]):
        high[j], low[j] = split(features[j])

    def slot(k, carry):
        row, col = place[k, 0], place[k, 1]
        parity = lax.rem(row, 2)
        half = jnp.where(parity == core[0], 0, 1)
        product = dot3(split(values[k]), (high[col], low[col]), ((1,), (0,)))
        index = half * keep.shape[0] + lax.div(row, 2)
        total[index] += product
        return carry

    lax.fori_loop(0, count[0], slot, 0)
    tiles = keep.shape[0]
    copies = [
        pltpu.make_async_copy(total.at[pl.ds(tiles, tiles)], send, sems.at[0]),
        pltpu.make_async_copy(total.at[pl.ds(0, tiles)], keep, sems.at[1]),
    ]
    for copy in copies:
        copy.start()
    for copy in copies:
        copy.wait()


def forward(place, count, core, values, features):
    tiles = Z * YL
    width = features.shape[-1]
    shape = jax.ShapeDtypeStruct((tiles, TILE, width), jnp.float32)
    smem = pl.BlockSpec(memory_space=pltpu.SMEM)
    vmem = pl.BlockSpec(memory_space=pltpu.VMEM)
    return pl.pallas_call(
        forward_kernel,
        out_shape=(shape, shape),
        in_specs=[smem, smem, smem, vmem, vmem],
        out_specs=(pl.BlockSpec(memory_space=pl.ANY),) * 2,
        scratch_shapes=[
            pltpu.VMEM((2 * tiles, TILE, width), jnp.float32),
            pltpu.VMEM(features.shape, jnp.bfloat16),
            pltpu.VMEM(features.shape, jnp.bfloat16),
            pltpu.SemaphoreType.DMA((2,)),
        ],
        compiler_params=pltpu.CompilerParams(vmem_limit_bytes=24 * 1024 * 1024),
        name="forward_tiles",
    )(place, count, core, values, features)


def middle_kernel(y_ref, mine, other, weight, bias, cot_own, cot_other, output, grad, extra, summed):
    y = y_ref[0]
    summed[...] = mine[...] + other[...]
    weights = split(weight[...])

    def half(start, cot):
        rows = pl.ds(pl.multiple_of(start, TILE), TILE)
        part = split(summed[rows, :])
        pre = dot3(part, weights, ((1,), (0,))) + bias[...]
        sigma = jax.nn.sigmoid(pre)
        value = cot[...] * (sigma * (1.0 + pre * (1.0 - sigma)))
        grad[rows, :] = value
        return part, pre * sigma, value

    half((1 - y) * TILE, cot_other)
    part, result, value = half(y * TILE, cot_own)
    output[...] = result
    value = split(value)
    width = weight.shape[1]
    extra[:, :width] = dot3(part, value, ((0,), (0,)))
    ones = jnp.ones((TILE, 128), jnp.bfloat16)
    first = lax.dot_general(value[0], ones, (((0,), (0,)), ((), ())), preferred_element_type=jnp.float32)
    second = lax.dot_general(value[1], ones, (((0,), (0,)), ((), ())), preferred_element_type=jnp.float32)
    extra[:, width:] = first + second


def middle(y, mine, other, weight, bias, cot_own, cot_other):
    width = weight.shape[1]
    smem = pl.BlockSpec(memory_space=pltpu.SMEM)
    vmem = pl.BlockSpec(memory_space=pltpu.VMEM)
    return pl.pallas_call(
        middle_kernel,
        out_shape=(
            jax.ShapeDtypeStruct((TILE, width), jnp.float32),
            jax.ShapeDtypeStruct((YL * TILE, width), jnp.float32),
            jax.ShapeDtypeStruct((weight.shape[0], width + 128), jnp.float32),
        ),
        in_specs=[smem] + [vmem] * 6,
        out_specs=(vmem,) * 3,
        scratch_shapes=[pltpu.VMEM((YL * TILE, weight.shape[0]), jnp.float32)],
        compiler_params=pltpu.CompilerParams(vmem_limit_bytes=16 * 1024 * 1024),
        name="middle",
    )(y, mine, other, weight, bias, cot_own, cot_other)


def backward_kernel(place, count, core, values, own, other, back):
    back[...] = jnp.zeros_like(back)

    def slot(k, carry):
        row, col = place[k, 0], place[k, 1]
        index = lax.div(row, 2)
        mine = lax.rem(row, 2) == core[0]
        block = jnp.where(mine, own[index], other[index])
        back[col] += dot3(split(values[k]), split(block), ((0,), (0,)))
        return carry

    lax.fori_loop(0, count[0], slot, 0)


def backward(place, count, core, values, own, other, tiles):
    smem = pl.BlockSpec(memory_space=pltpu.SMEM)
    vmem = pl.BlockSpec(memory_space=pltpu.VMEM)
    return pl.pallas_call(
        backward_kernel,
        out_shape=jax.ShapeDtypeStruct((tiles,) + own.shape[1:], jnp.float32),
        in_specs=[smem, smem, smem, vmem, vmem, vmem],
        out_specs=vmem,
        compiler_params=pltpu.CompilerParams(vmem_limit_bytes=24 * 1024 * 1024),
        name="backward_tiles",
    )(place, count, core, values, own, other)


def final_kernel(parts, weight, result):
    back = parts[0]
    for j in range(1, parts.shape[0]):
        back = back + parts[j]
    result[...] = dot3(split(back), split(weight[...]), ((1,), (1,)))


def final(parts, weight):
    vmem = pl.BlockSpec(memory_space=pltpu.VMEM)
    return pl.pallas_call(
        final_kernel,
        out_shape=jax.ShapeDtypeStruct((parts.shape[1], weight.shape[0]), jnp.float32),
        in_specs=[vmem, vmem],
        out_specs=vmem,
        compiler_params=pltpu.CompilerParams(vmem_limit_bytes=16 * 1024 * 1024),
        name="final",
    )(parts, weight)


def body(node_features, weight, bias, tile_values, tile_coords, tile_count, cotangent):
    values = tile_values[0, 0]
    place = tile_coords[0, 0]
    count = tile_count.reshape(1)
    local_nodes, width = node_features.shape
    row_count = lax.axis_size("row")
    col_count = lax.axis_size("col")
    device_count = row_count * col_count
    factor = 1.0 / math.sqrt(local_nodes * device_count)
    col = lax.axis_index("col")
    core = lax.rem(col, 2).reshape(1)
    y = lax.rem(lax.div(col, 2), YL).reshape(1)

    features = lax.all_to_all(
        jnp.broadcast_to(node_features[None], (row_count, local_nodes, width)), "row", 0, 0
    )
    keep, send = forward(place, count, core, values, features)
    partial = keep + lax.ppermute(send, "col", CORE_SWAP)
    summed = lax.psum_scatter(
        partial.reshape(Z * YL * TILE, width),
        "col",
        scatter_dimension=0,
        tiled=True,
        axis_index_groups=Z_GROUPS,
    )
    cot_other = lax.ppermute(cotangent, "col", Y_SWAP)
    summed, cot_other = lax.optimization_barrier((summed, cot_other))
    summed_other = lax.ppermute(summed, "col", Y_SWAP)
    output, grads, extra = middle(
        y, summed, summed_other, weight, bias.reshape(1, width), cotangent, cot_other
    )

    own = lax.all_gather(grads, "col", axis=0, tiled=True, axis_index_groups=Z_GROUPS)
    axes = ("row", "col")
    pieces = lax.all_to_all(extra.reshape(device_count, 1, -1), axes, 0, 0)
    piece = jnp.sum(pieces, axis=0, keepdims=True) * factor
    whole = lax.all_to_all(jnp.broadcast_to(piece, pieces.shape), axes, 0, 0)
    whole = whole.reshape(weight.shape[0], -1)
    weight_grad = whole[:, :width]
    bias_grad = whole[:, width]

    own, weight_grad, bias_grad = lax.optimization_barrier((own, weight_grad, bias_grad))
    own = own.reshape(Z * YL, TILE, width)
    other = lax.ppermute(own, "col", CORE_SWAP)
    back = backward(place, count, core, values, own, other, row_count)
    parts = lax.all_to_all(back, "row", 0, 0)
    input_grad = final(parts, weight)
    return (output, input_grad, weight_grad, bias_grad)


def solution(mesh):
    in_specs = (
        P(("col", "row"), None),
        P(),
        P(),
        P("row", "col", None, None, None),
        P("row", "col", None, None),
        P("row", "col"),
        P(("row", "col"), None),
    )
    out_specs = (P(("row", "col"), None), P(("col", "row"), None), P(), P())
    return jax.shard_map(body, mesh=mesh, in_specs=in_specs, out_specs=out_specs, check_vma=False)
```

time: 624 us -> 190 us (0.30)
  waiting for transfers between devices: 496 us -> 69.7 us
  matrix products: 14.4 us -> 0 us
  starting transfers between devices: 0.21 us -> 10.4 us
  other arithmetic: 9.11 us -> 2.06 us
    psum x1 -> x0, waiting for transfers between devices: 252 us -> none  [body(): weight_grad, bias_grad = lax.psum((weight_term, bias_term), ('row', 'col'))]
    all_gather x2 -> x1, waiting for transfers between devices: 120 us -> 0.01 us  [body(): lax.all_gather(grads, 'col', axis=0, tiled=True, axis_index_groups=Z_GROUPS)]
    reduce_scatter x2 -> x1, waiting for transfers between devices: 123 us -> 37.6 us  [body(): lax.psum_scatter(partial.reshape(Z * YL * TILE, width), 'col', scatter_di...]
    all_to_all x0 -> x3, blocking collectives: none -> 79.3 us  [the longest x1 32.2 us: body(): pieces = lax.all_to_all(extra.reshape(device_count, 1, -1), axes, 0, 0)]
    psum x1 -> x0, blocking collectives: 75.9 us -> none  [body(): weight_grad, bias_grad = lax.psum((weight_term, bias_term), ('row', 'col'))]
    ppermute x0 -> x4, waiting for transfers between devices: none -> 18.3 us  [the longest x1 5.24 us: body(): cot_other = lax.ppermute(cotangent, 'col', Y_SWAP)]
    dot_general x5 -> x0, matrix products: 14.4 us -> none  [the longest x1 4.18 us: body(): jnp.einsum('kij,kjf->kif', values, picked, precision=precise) * live_mask]
    all_to_all x0 -> x1, waiting for transfers between devices: none -> 13.8 us  [body(): lax.all_to_all(jnp.broadcast_to(node_features[None], (row_count, local_no...]
  transfers between devices with their start and end apart: 5 -> 7, of which waited for: 5 -> 6; matrix products, arithmetic and copies ran while one was open for 1% -> 1% of each run, Pallas kernels for 0% -> 0%
where the time goes in v1:
time: 190 us; the launch traced here: 188 us
  blocking collectives  79.3 us (42%)
  waiting for transfers between devices  69.7 us (37%)
  between operations  14.7 us (8%)
  starting transfers between devices  10.4 us (5%)
  local copies, waits for them, and re-layouts  7.56 us (4%)
  Pallas kernels  4.59 us (2%)
  other arithmetic  2.06 us (1%)
    reduce_scatter x1, waiting for transfers between devices, body(): lax.psum_scatter(partial.reshape(Z * YL * TILE, width), 'col', scatter_di...  37.6 us
    all_to_all x1, blocking collectives, body(): pieces = lax.all_to_all(extra.reshape(device_count, 1, -1), axes, 0, 0)  32.2 us
    all_to_all x1, blocking collectives, body(): whole = lax.all_to_all(jnp.broadcast_to(piece, pieces.shape), axes, 0, 0)  25.2 us
    all_to_all x1, blocking collectives, body(): parts = lax.all_to_all(back, 'row', 0, 0)  21.8 us
    all_to_all x1, waiting for transfers between devices, body(): lax.all_to_all(jnp.broadcast_to(node_features[None], (row_count, local_no...  13.8 us
    all_to_all x1, starting transfers between devices, body(): lax.all_to_all(jnp.broadcast_to(node_features[None], (row_count, local_no...  7.46 us
    ppermute x1, waiting for transfers between devices, body(): cot_other = lax.ppermute(cotangent, 'col', Y_SWAP)  5.24 us
    ppermute x1, waiting for transfers between devices, body(): summed_other = lax.ppermute(summed, 'col', Y_SWAP)  4.99 us
  transfers between devices with their start and end apart: 7, of which 6 were waited for; matrix products, arithmetic and copies ran while one was open for 1% of the time, Pallas kernels for 0%

profile of v1, /device:TPU:2, one launch (start us, length us, event | category | flops | bytes accessed | tf_op | source)
XLA Modules:
  0.0 188.3 jit_solution(11203856415608042889)
XLA Ops:
  7.2 0.0 copy-start.6
  7.2 0.0 copy-start
  7.2 2.0 %broadcast_in_dim.4 = f32[8,128,256]{2,1,0:T(8,128)} broadcast(f32[128,256]{1,0:T(8,128)} %param.7), dimensions={1,2} | broadcast | bytes 1179648 | tf_op jit(solution)/shard_map/broadcast_in_dim | solution.py:195
  9.2 7.5 %all-to-all-start = ((f32[8,128,256]{2,1,0:T(8,128)}), f32[8,128,256]{2,1,0:T(8,128)S(1)}, u32[]{:S(2)}, u32[]{:S(2)}) async-start(f32[8,128,256]{2,1,0:T(8,128)} %broadcast_in_dim.4), calls=%async_computation | async-start | bytes 2097152 | tf_op jit(solution)/shard_map/all_to_all | solution.py:194
  16.7 0.0 reduce-scatter.2.cloned.1.call-start
  16.7 0.0 copy-done.6
  16.7 0.1 copy.15.place
  17.4 13.8 %all-to-all-done.features = f32[8,128,256]{2,1,0:T(8,128)S(1)} async-done(((f32[8,128,256]{2,1,0:T(8,128)}), f32[8,128,256]{2,1,0:T(8,128)S(1)}, u32[]{:S(2)}, u32[]{:S(2)}) %all-to-all-start) | async-done | bytes 1048608 | tf_op jit(solution)/shard_map/all_to_all | solution.py:194
  31.2 0.0 copy-done
  31.2 1.6 forward_tiles.1
  32.8 0.6 collective-permute-start
  33.4 3.8 %collective-permute-done = f32[16,128,256]{2,1,0:T(8,128)S(1)} collective-permute-done((f32[16,128,256]{2,1,0:T(8,128)S(1)}, f32[16,128,256]{2,1,0:T(8,128)S(1)}, u32[]{:S(2)}, u32[]{:S(2)}) %collective-permute-start) | collective-permute-done | bytes 2097184 | tf_op jit(solution)/shard_map/ppermute | solution.py:198
  37.2 1.7 add.5
  39.0 0.0 copy-start.4
  39.0 0.0 copy-start.2
  39.0 0.0 copy-start.5
  39.0 0.0 reduce-scatter.2.cloned.1.call-update
  39.0 0.0 all-gather.2.cloned.1.call-start
  39.0 0.8 copy-done.4
  39.9 0.5 collective-permute-start.1
  40.4 5.2 %collective-permute-done.1.cot_other = f32[128,256]{1,0:T(8,128)S(1)} collective-permute-done((f32[128,256]{1,0:T(8,128)S(1)}, f32[128,256]{1,0:T(8,128)S(1)}, u32[]{:S(2)}, u32[]{:S(2)}) %collective-permute-start.1) | collective-permute-done | bytes 131104 | tf_op jit(solution)/shard_map/ppermute | solution.py:206
  45.6 37.6 %reduce-scatter.2.cloned.1.call-done.mine = f32[256,256]{1,0:T(8,128)} async-done(((f32[2048,256]{1,0:T(8,128)}), f32[256,256]{1,0:T(8,128)}) %reduce-scatter.2.cloned.1.call-update) | async-done | bytes 262160 | tf_op jit(solution)/shard_map/reduce_scatter | solution.py:199
  83.3 1.6 collective-permute-start.2
  84.9 5.0 %collective-permute-done.2.other = f32[256,256]{1,0:T(8,128)S(1)} collective-permute-done((f32[256,256]{1,0:T(8,128)}, f32[256,256]{1,0:T(8,128)S(1)}, u32[]{:S(2)}, u32[]{:S(2)}) %collective-permute-start.2) | collective-permute-done | bytes 262176 | tf_op jit(solution)/shard_map/ppermute | solution.py:208
  89.8 0.0 copy-done.2
  89.8 0.0 copy-done.5
  89.8 0.0 copy-start.3
  89.9 0.9 copy-done.3
  90.8 1.1 middle.1
  91.9 0.0 all-gather.2.cloned.1.call-update
  91.9 0.4 copy.16
  92.3 32.2 %all_to_all.20 = f32[256,1,384]{2,1,0:T(1,128)S(1)} all-to-all(f32[256,1,384]{2,1,0:T(1,128)S(1)} %copy.16), channel_id=1, replica_groups=mesh['row'=8,'col'=32] {'row','col'}, dimensions={0} | all-to-all | bytes 786432 | tf_op jit(solution)/shard_map/all_to_all | solution.py:215
  124.6 0.3 reduce_sum.9
  124.9 0.2 broadcast_in_dim.5
  125.1 25.2 %all_to_all.21 = f32[256,1,384]{2,1,0:T(1,128)S(1)} all-to-all(f32[256,1,384]{2,1,0:T(1,128)S(1)} %broadcast_in_dim.5), channel_id=1, replica_groups=mesh['row'=8,'col'=32] {'row','col'}, dimensions={0} | all-to-all | bytes 786432 | tf_op jit(solution)/shard_map/all_to_all | solution.py:217
  150.3 0.7 slice.8
  151.1 0.7 slice_reduce_fusion
  151.7 0.0 all-gather.2.cloned.1.call-done
  151.7 0.1 collective-permute-start.3
  151.9 4.3 %collective-permute-done.3.other = f32[16,128,256]{2,1,0:T(8,128)S(1)} collective-permute-done((f32[16,128,256]{2,1,0:T(8,128)}, f32[16,128,256]{2,1,0:T(8,128)S(1)}, u32[]{:S(2)}, u32[]{:S(2)}) %collective-permute-start.3) | collective-permute-done | bytes 2097184 | tf_op jit(solution)/shard_map/ppermute | solution.py:224
  156.1 0.0 copy-start.1
  156.1 1.6 copy-done.1
  157.7 1.0 backward_tiles.1
  158.7 21.8 %all_to_all.22.parts = f32[8,128,256]{2,1,0:T(8,128)S(1)} all-to-all(f32[8,128,256]{2,1,0:T(8,128)S(1)} %backward_tiles.1), channel_id=1, replica_groups=mesh['row'=8,'col'=32] {'row'}, dimensions={0} | all-to-all | bytes 2097152 | tf_op jit(solution)/shard_map/all_to_all | solution.py:226
  180.5 0.9 final.1
  (2 shorter events, 0.0 us)
Async XLA Ops:
  7.2 9.5 %copy-start.6 = (s32[1,1,12,2]{2,3,1,0:T(2,128)S(1)}, s32[1,1,12,2]{2,3,1,0:T(2,128)}, u32[]{:S(2)}) copy-start(s32[1,1,12,2]{2,3,1,0:T(2,128)} %param.11) | copy-start | bytes 292
  7.2 24.1 %copy-start = (f32[1,1,12,128,128]{4,3,2,1,0:T(8,128)S(1)}, f32[1,1,12,128,128]{4,3,2,1,0:T(8,128)}, u32[]{:S(2)}) copy-start(f32[1,1,12,128,128]{4,3,2,1,0:T(8,128)} %param.10) | copy-start | bytes 2359300
  9.2 22.0 %all-to-all-start = ((f32[8,128,256]{2,1,0:T(8,128)}), f32[8,128,256]{2,1,0:T(8,128)S(1)}, u32[]{:S(2)}, u32[]{:S(2)}) async-start(f32[8,128,256]{2,1,0:T(8,128)} %broadcast_in_dim.4), calls=%async_computation | async-start | bytes 2097152 | tf_op jit(solution)/shard_map/all_to_all | solution.py:194
  16.7 66.6 %reduce-scatter.2.cloned.1.call-start = ((), (), s32[]{:S(2)}) async-start(), calls=%async_computation.5 | async-start | bytes 2359296 | tf_op jit(solution)/shard_map/reduce_scatter | solution.py:199
  32.8 4.4 %collective-permute-start = (f32[16,128,256]{2,1,0:T(8,128)S(1)}, f32[16,128,256]{2,1,0:T(8,128)S(1)}, u32[]{:S(2)}, u32[]{:S(2)}) collective-permute-start(f32[16,128,256]{2,1,0:T(8,128)S(1)} %get-tuple-element.15), channel_id=1, source_target_pairs={{0,1},{1,0},{2,3},{3,2},{4,5},{5,4},{6,7},{7,6},{8,9},{9,8},{10,11... | collective-permute-start | bytes 6291464 | tf_op jit(solution)/shard_map/ppermute | solution.py:198
  39.0 0.9 copy-start.4
  39.0 50.9 %copy-start.2 = (f32[256,256]{1,0:T(8,128)S(1)}, f32[256,256]{1,0:T(8,128)}, u32[]{:S(2)}) copy-start(f32[256,256]{1,0:T(8,128)} %weight.3) | copy-start | bytes 786436
  39.0 50.9 %copy-start.5 = (f32[256]{0:T(256)S(1)}, f32[256]{0:T(256)}, u32[]{:S(2)}) copy-start(f32[256]{0:T(256)} %param.9) | copy-start | bytes 3076
  39.0 112.8 %all-gather.2.cloned.1.call-start = ((), (), s32[]{:S(2)}) async-start(), calls=%async_computation.6 | async-start | bytes 2359296 | tf_op jit(solution)/shard_map/all_gather | solution.py:213
  39.9 5.8 %collective-permute-start.1 = (f32[128,256]{1,0:T(8,128)S(1)}, f32[128,256]{1,0:T(8,128)S(1)}, u32[]{:S(2)}, u32[]{:S(2)}) collective-permute-start(f32[128,256]{1,0:T(8,128)S(1)} %copy-done.4), channel_id=1, source_target_pairs={{0,2},{1,3},{2,0},{3,1},{4,6},{5,7},{6,4},{7,5},{8,10},{9,11},{10,... | collective-permute-start | bytes 393224 | tf_op jit(solution)/shard_map/ppermute | solution.py:206
  83.3 6.6 %collective-permute-start.2 = (f32[256,256]{1,0:T(8,128)}, f32[256,256]{1,0:T(8,128)S(1)}, u32[]{:S(2)}, u32[]{:S(2)}) collective-permute-start(f32[256,256]{1,0:T(8,128)} %reduce-scatter.2.cloned.1.call-done.mine), channel_id=1, source_target_pairs={{0,2},{1,3},{2,0},{3,1},{4,6},{5,7},{6,4},{7,5},{8,10},{9,11},{10,... | collective-permute-start | bytes 786440 | tf_op jit(solution)/shard_map/ppermute | solution.py:208
  89.8 1.0 copy-start.3
  151.7 4.4 %collective-permute-start.3 = (f32[16,128,256]{2,1,0:T(8,128)}, f32[16,128,256]{2,1,0:T(8,128)S(1)}, u32[]{:S(2)}, u32[]{:S(2)}) collective-permute-start(f32[16,128,256]{2,1,0:T(8,128)} %bitcast.16), channel_id=1, source_target_pairs={{0,1},{1,0},{2,3},{3,2},{4,5},{5,4},{6,7},{7,6},{8,9},{9,8},{10,11... | collective-permute-start | bytes 6291464 | tf_op jit(solution)/shard_map/ppermute | solution.py:224
  156.1 1.6 copy-start.1
Sparse Core Ops, SparseCore 0:
  39.1 44.1 reduce-scatter.1
  92.0 53.2 all-gather.1

commit v2 on v1

v2 whole, which is shorter than its diff:
```python
import math

import jax
import jax.numpy as jnp
from jax import lax
from jax.experimental import pallas as pl
from jax.experimental.pallas import tpu as pltpu
from jax.sharding import PartitionSpec as P

Z, YL = 8, 2
TILE = 128
PAIR = YL * TILE
NEAR = (0, 1, 2, 6, 7)
FAR = (3, 4, 5)


def col_pairs(move):
    pairs = []
    for z in range(Z):
        for y in range(YL):
            for core in range(2):
                a, b, c = move(z, y, core)
                pairs.append(((z * YL + y) * 2 + core, (a * YL + b) * 2 + c))
    return pairs


CORE_SWAP = col_pairs(lambda z, y, core: (z, y, 1 - core))
Y_SWAP = col_pairs(lambda z, y, core: (z, 1 - y, core))
Z_GROUPS = [[(z * YL + y) * 2 + core for z in range(Z)] for y in range(YL) for core in range(2)]


def z_shift(value, distance):
    return lax.ppermute(value, "col", col_pairs(lambda z, y, core: ((z + distance) % Z, y, core)))


SMEM = pl.BlockSpec(memory_space=pltpu.SMEM)
VMEM = pl.BlockSpec(memory_space=pltpu.VMEM)


def params(mib):
    return pltpu.CompilerParams(vmem_limit_bytes=mib * 1024 * 1024)


def shaped(*shape):
    return jax.ShapeDtypeStruct(shape, jnp.float32)


def split(value):
    high = value.astype(jnp.bfloat16)
    low = (value - high.astype(jnp.float32)).astype(jnp.bfloat16)
    return high, low


def dot3(left, right, contract):
    def one(a, b):
        return lax.dot_general(a, b, (contract, ((), ())), preferred_element_type=jnp.float32)

    return one(left[0], right[0]) + (one(left[0], right[1]) + one(left[1], right[0]))


def locate(tile, where):
    mine = lax.rem(tile, 2) == where[2]
    distance = lax.rem(lax.div(tile, 2 * YL) - where[0] + Z, Z)
    return mine, distance, lax.rem(lax.div(tile, 2), YL)


def forward_kernel(place, count, where, values, features, keep, send, total, high, low, sems):
    total[...] = jnp.zeros_like(total)
    for j in range(features.shape[0]):
        high[j], low[j] = split(features[j])

    def slot(k, carry):
        col = place[k, 1]
        mine, distance, y = locate(place[k, 0], where)
        product = dot3(split(values[k]), (high[col], low[col]), ((1,), (0,)))
        total[jnp.where(mine, 0, Z * YL) + distance * YL + y] += product
        return carry

    lax.fori_loop(0, count[0], slot, 0)
    tiles = keep.shape[0]
    copies = [
        pltpu.make_async_copy(total.at[pl.ds(tiles, tiles)], send, sems.at[0]),
        pltpu.make_async_copy(total.at[pl.ds(0, tiles)], keep, sems.at[1]),
    ]
    for copy in copies:
        copy.start()
    for copy in copies:
        copy.wait()


def forward(place, count, where, values, features):
    tiles = Z * YL
    width = features.shape[-1]
    return pl.pallas_call(
        forward_kernel,
        out_shape=(shaped(tiles, TILE, width),) * 2,
        in_specs=[SMEM, SMEM, SMEM, VMEM, VMEM],
        out_specs=(pl.BlockSpec(memory_space=pl.ANY),) * 2,
        scratch_shapes=[
            pltpu.VMEM((2 * tiles, TILE, width), jnp.float32),
            pltpu.VMEM(features.shape, jnp.bfloat16),
            pltpu.VMEM(features.shape, jnp.bfloat16),
            pltpu.SemaphoreType.DMA((2,)),
        ],
        compiler_params=params(24),
        name="forward_tiles",
    )(place, count, where, values, features)


def add_cores_kernel(first, second, own, one, two, three, four_up, four_down, five, six, seven):
    def total(tile):
        return first[tile] + second[tile]

    for distance, out in ((3, three), (5, five), (0, own), (1, one), (2, two), (6, six), (7, seven)):
        for y in range(YL):
            out[y * TILE : (y + 1) * TILE, :] = total(distance * YL + y)
    four_up[...] = total(4 * YL)
    four_down[...] = total(4 * YL + 1)


def add_cores(first, second):
    width = first.shape[-1]
    whole, half = shaped(PAIR, width), shaped(TILE, width)
    return pl.pallas_call(
        add_cores_kernel,
        out_shape=(whole,) * 4 + (half,) * 2 + (whole,) * 3,
        in_specs=[VMEM] * 2,
        out_specs=(VMEM,) * 9,
        compiler_params=params(16),
        name="add_cores",
    )(first, second)


def relay_kernel(two, three, four_up, six, five, four_down, up, down):
    up[:TILE, :] = two[:TILE, :] + three[:TILE, :] + four_up[...]
    up[TILE:, :] = two[TILE:, :] + three[TILE:, :]
    down[:TILE, :] = six[:TILE, :] + five[:TILE, :]
    down[TILE:, :] = six[TILE:, :] + five[TILE:, :] + four_down[...]


def relay(*operands):
    return pl.pallas_call(
        relay_kernel,
        out_shape=(jax.ShapeDtypeStruct(operands[0].shape, jnp.float32),) * 2,
        in_specs=[VMEM] * 6,
        out_specs=(VMEM,) * 2,
        compiler_params=params(16),
        name="relay",
    )(*operands)


def scatter_z(own, one, two, three, four_up, four_down, five, six, seven):
    from_three, from_five = z_shift(three, 1), z_shift(five, -1)
    from_up, from_down = z_shift(four_up, 2), z_shift(four_down, -2)
    from_one, from_seven = z_shift(one, 1), z_shift(seven, -1)
    up, down = relay(two, from_three, from_up, six, from_five, from_down)
    from_two, from_six = z_shift(up, 2), z_shift(down, -2)
    return ((own + from_one) + from_seven) + (from_two + from_six)


def middle_kernel(y_ref, mine, other, weight, bias, cot_own, cot_other, output, grad, extra, cots):
    y = y_ref[1]
    cots[y] = cot_own[...]
    cots[1 - y] = cot_other[...]
    cot = cots[...].reshape(grad.shape)
    part = split(mine[...] + other[...])
    pre = dot3(part, split(weight[...]), ((1,), (0,))) + bias[...]
    sigma = jax.nn.sigmoid(pre)
    value = cot * (sigma * (1.0 + pre * (1.0 - sigma)))
    grad[...] = value
    cots[...] = (pre * sigma).reshape(cots.shape)
    output[...] = cots[y]
    sums = jnp.broadcast_to(jnp.sum(value, axis=0, keepdims=True), (8, value.shape[1]))
    product = dot3(part, split(value), ((0,), (0,)))
    pieces = extra.shape[0]
    rows = product.shape[0] // pieces
    for j in range(pieces):
        extra[j, :rows, :] = product[j * rows : (j + 1) * rows, :]
        extra[j, rows:, :] = sums


def middle(where, mine, other, weight, bias, cot_own, cot_other, pieces):
    width = weight.shape[1]
    return pl.pallas_call(
        middle_kernel,
        out_shape=(
            shaped(TILE, width),
            shaped(PAIR, width),
            shaped(pieces, weight.shape[0] // pieces + 8, width),
        ),
        in_specs=[SMEM] + [VMEM] * 6,
        out_specs=(VMEM,) * 3,
        scratch_shapes=[pltpu.VMEM((YL, TILE, width), jnp.float32)],
        compiler_params=params(16),
        name="middle",
    )(where, mine, other, weight, bias, cot_own, cot_other)


def gather_z(block):
    one, seven = z_shift(block, -1), z_shift(block, 1)
    two, six = z_shift(block, -2), z_shift(block, 2)
    return one, two, six, seven


def gather_z_far(two, six):
    three, five = z_shift(two, -1), z_shift(six, 1)
    low, high = z_shift(six[:TILE], 2), z_shift(two[TILE:], -2)
    return jnp.concatenate([three, low, high, five])


def backward_kernel(
    place, count, where, values, own_near, other_near, own_far, other_far, piece, back, held, total
):
    total[...] = jnp.zeros_like(total)

    def slot(k, carry):
        mine, distance, y = locate(place[k, 0], where)
        far = (distance >= FAR[0]) & (distance <= FAR[-1])
        index = jnp.where(distance < FAR[0], distance, distance - len(FAR)) * YL + y
        for source, good in (
            (own_near, mine & ~far),
            (other_near, ~mine & ~far),
            (own_far, mine & far),
            (other_far, ~mine & far),
        ):

            @pl.when(good)
            def _():
                held[...] = source[index]

        total[place[k, 1]] += dot3(split(values[k]), split(held[...]), ((0,), (0,)))
        return carry

    lax.fori_loop(0, count[0], slot, 0)
    for j in range(back.shape[0]):
        back[j, :TILE, :] = total[j]
        back[j, TILE:, :] = piece[...]


def backward(place, count, where, values, near, other_near, far, other_far, piece, tiles):
    width = near.shape[-1]
    return pl.pallas_call(
        backward_kernel,
        out_shape=shaped(tiles, TILE + piece.shape[0], width),
        in_specs=[SMEM] * 3 + [VMEM] * 6,
        out_specs=VMEM,
        scratch_shapes=[
            pltpu.VMEM((TILE, width), jnp.float32),
            pltpu.VMEM((tiles, TILE, width), jnp.float32),
        ],
        compiler_params=params(24),
        name="backward_tiles",
    )(place, count, where, values, near, other_near, far, other_far, piece)


def final_kernel(parts, weight, result, weight_grad, bias_grad):
    back = parts[0, :TILE, :]
    for j in range(1, parts.shape[0]):
        back = back + parts[j, :TILE, :]
    result[...] = dot3(split(back), split(weight[...]), ((1,), (1,)))
    rows = parts.shape[1] - TILE - 8
    for j in range(parts.shape[0]):
        weight_grad[j * rows : (j + 1) * rows, :] = parts[j, TILE : TILE + rows, :]
    bias_grad[...] = parts[0, TILE + rows : TILE + rows + 1, :]


def final(parts, weight):
    return pl.pallas_call(
        final_kernel,
        out_shape=(
            shaped(TILE, weight.shape[0]),
            shaped(*weight.shape),
            shaped(1, weight.shape[1]),
        ),
        in_specs=[VMEM, VMEM],
        out_specs=(VMEM,) * 3,
        compiler_params=params(16),
        name="final",
    )(parts, weight)


def body(node_features, weight, bias, tile_values, tile_coords, tile_count, cotangent):
    values = tile_values[0, 0]
    place = tile_coords[0, 0]
    count = tile_count.reshape(1)
    local_nodes, width = node_features.shape
    row_count = lax.axis_size("row")
    col_count = lax.axis_size("col")
    factor = 1.0 / math.sqrt(local_nodes * row_count * col_count)
    col = lax.axis_index("col")
    where = jnp.stack([lax.div(col, 2 * YL), lax.rem(lax.div(col, 2), YL), lax.rem(col, 2)])

    features = lax.all_to_all(
        jnp.broadcast_to(node_features[None], (row_count, local_nodes, width)), "row", 0, 0
    )
    keep, send = forward(place, count, where, values, features)
    cot_other = lax.ppermute(cotangent, "col", Y_SWAP)
    summed = scatter_z(*add_cores(keep, lax.ppermute(send, "col", CORE_SWAP)))
    summed, cot_other = lax.optimization_barrier((summed, cot_other))
    summed_other = lax.ppermute(summed, "col", Y_SWAP)
    output, grads, extra = middle(
        where, summed, summed_other, weight, bias.reshape(1, width), cotangent, cot_other, row_count
    )

    one, two, six, seven = gather_z(grads)
    piece = jnp.sum(lax.all_to_all(extra, "row", 0, 0), axis=0)
    piece, one, two, six, seven = lax.optimization_barrier((piece, one, two, six, seven))
    far = gather_z_far(two, six)
    near = jnp.concatenate([grads, one, two, six, seven])
    other_near = lax.ppermute(near, "col", CORE_SWAP)
    piece = piece + lax.ppermute(piece, "col", CORE_SWAP)
    pieces = jnp.broadcast_to(piece[None], (Z,) + piece.shape)
    pieces = lax.all_to_all(pieces, "col", 0, 0, axis_index_groups=Z_GROUPS)
    piece = jnp.sum(pieces, axis=0) * factor
    piece, far = lax.optimization_barrier((piece, far))
    other_far = lax.ppermute(far, "col", CORE_SWAP)

    def tiles(value):
        return value.reshape(-1, TILE, width)

    back = backward(
        place, count, where, values, tiles(near), tiles(other_near), tiles(far), tiles(other_far),
        piece, row_count,
    )
    parts = lax.all_to_all(back, "row", 0, 0)
    input_grad, weight_grad, bias_grad = final(parts, weight)
    return (output, input_grad, weight_grad, bias_grad.reshape(width))


def solution(mesh):
    in_specs = (
        P(("col", "row"), None),
        P(),
        P(),
        P("row", "col", None, None, None),
        P("row", "col", None, None),
        P("row", "col"),
        P(("row", "col"), None),
    )
    out_specs = (P(("row", "col"), None), P(("col", "row"), None), P(), P())
    return jax.shard_map(body, mesh=mesh, in_specs=in_specs, out_specs=out_specs, check_vma=False)
```

time: 190 us -> 173 us (0.911)
  blocking collectives: 79.3 us -> 25.2 us
  starting transfers between devices: 10.4 us -> 48.8 us
  between operations: 14.7 us -> 1.48 us
  Pallas kernels: 4.59 us -> 11.9 us
  waiting for transfers between devices: 69.7 us -> 76.3 us
    all_to_all x2 -> x0, blocking collectives: 57.5 us -> none  [the longest x1 32.2 us: body(): pieces = lax.all_to_all(extra.reshape(device_count, 1, -1), axes, 0, 0)]
    ppermute x2 -> x20, waiting for transfers between devices: 8.04 us -> 55.6 us  [the longest x16 49.2 us: z_shift(): lax.ppermute(value, 'col', col_pairs(lambda z, y, core: ((z + distance) %...]
    reduce_scatter x1 -> x0, waiting for transfers between devices: 37.6 us -> none  [body(): lax.psum_scatter(partial.reshape(Z * YL * TILE, width), 'col', scatter_di...]
    ppermute x2 -> x20, starting transfers between devices: 0.72 us -> 25.1 us  [the longest x16 24.9 us: z_shift(): lax.ppermute(value, 'col', col_pairs(lambda z, y, core: ((z + distance) %...]
    all_to_all x0 -> x2, starting transfers between devices: none -> 13.3 us  [the longest x1 7.25 us: body(): piece = jnp.sum(lax.all_to_all(extra, 'row', 0, 0), axis=0)]
    pallas_call x4 -> x6, Pallas kernels: 4.59 us -> 11.9 us  [the longest x1 4.77 us: backward(): pl.pallas_call(backward_kernel, out_shape=shaped(tiles, TILE + piece.shap...]
    ppermute x1, waiting for transfers between devices: 5.24 us -> 0.01 us  [body(): cot_other = lax.ppermute(cotangent, 'col', Y_SWAP)]
    all_to_all x1, blocking collectives: 21.8 us -> 25.2 us  [body(): parts = lax.all_to_all(back, 'row', 0, 0)]
  transfers between devices with their start and end apart: 7 -> 25, of which waited for: 6 -> 15; matrix products, arithmetic and copies ran while one was open for 1% -> 3% of each run, Pallas kernels for 0% -> 0%
where the time goes in v2:
time: 173 us; the launch traced here: 171 us
  waiting for transfers between devices  76.3 us (44%)
  starting transfers between devices  48.8 us (28%)
  blocking collectives  25.2 us (15%)
  Pallas kernels  11.9 us (7%)
  local copies, waits for them, and re-layouts  5.75 us (3%)
    ppermute x16, waiting for transfers between devices, z_shift(): lax.ppermute(value, 'col', col_pairs(lambda z, y, core: ((z + distance) %...  49.2 us
    all_to_all x1, blocking collectives, body(): parts = lax.all_to_all(back, 'row', 0, 0)  25.2 us
    ppermute x16, starting transfers between devices, z_shift(): lax.ppermute(value, 'col', col_pairs(lambda z, y, core: ((z + distance) %...  24.9 us
    all_to_all x1, waiting for transfers between devices, body(): lax.all_to_all(jnp.broadcast_to(node_features[None], (row_count, local_no...  13.7 us
    all_to_all x1, starting transfers between devices, body(): lax.all_to_all(jnp.broadcast_to(node_features[None], (row_count, local_no...  7.59 us
    all_to_all x1, starting transfers between devices, body(): piece = jnp.sum(lax.all_to_all(extra, 'row', 0, 0), axis=0)  7.25 us
    all_to_all x1, starting transfers between devices, body(): pieces = lax.all_to_all(pieces, 'col', 0, 0, axis_index_groups=Z_GROUPS)  6.03 us
    ppermute x1, waiting for transfers between devices, body(): summed_other = lax.ppermute(summed, 'col', Y_SWAP)  5.04 us
  transfers between devices with their start and end apart: 25, of which 15 were waited for; matrix products, arithmetic and copies ran while one was open for 3% of the time, Pallas kernels for 0%

profile of v2, /device:TPU:2, one launch (start us, length us, event | category | flops | bytes accessed | tf_op | source)
XLA Modules:
  0.0 170.7 jit_solution(5185389305823617764)
XLA Ops:
  0.6 2.0 %broadcast_in_dim.4 = f32[8,128,256]{2,1,0:T(8,128)} broadcast(f32[128,256]{1,0:T(8,128)} %param.7), dimensions={1,2} | broadcast | bytes 1179648 | tf_op jit(solution)/shard_map/broadcast_in_dim | solution.py:294
  2.6 7.6 %all-to-all-start = ((f32[8,128,256]{2,1,0:T(8,128)}), f32[8,128,256]{2,1,0:T(8,128)S(1)}, u32[]{:S(2)}, u32[]{:S(2)}) async-start(f32[8,128,256]{2,1,0:T(8,128)} %broadcast_in_dim.4), calls=%async_computation | async-start | bytes 2097152 | tf_op jit(solution)/shard_map/all_to_all | solution.py:293
  10.2 0.1 copy.13.place
  10.9 0.1 pad_add_fusion.where.y_ref
  11.0 13.7 %all-to-all-done.features = f32[8,128,256]{2,1,0:T(8,128)S(1)} async-done(((f32[8,128,256]{2,1,0:T(8,128)}), f32[8,128,256]{2,1,0:T(8,128)S(1)}, u32[]{:S(2)}, u32[]{:S(2)}) %all-to-all-start) | async-done | bytes 1048608 | tf_op jit(solution)/shard_map/all_to_all | solution.py:293
  24.7 3.8 %forward_tiles.1 = (f32[16,128,256]{2,1,0:T(8,128)S(1)}, f32[16,128,256]{2,1,0:T(8,128)S(1)}) custom-call(s32[12,2]{1,0:T(8,128)S(1)} %copy.13.place, s32[1]{0:T(128)} %bitcast.12.count, s32[3]{0:T(128)S(1)} %pad_add_fusion.where.y_ref, f32[12,128,128]{2,1,0:T(8,128)S(1)} %bitcast.14, f32[8,128,256]{2,1,0:T(8,128)S(1)} %all-to-all-done.features), custom_call_target="tpu_custom_call" | custom-call | tf_op jit(solution)/shard_map/forward_tiles/pallas_call | solution.py:94
  28.6 0.1 collective-permute-start
  28.7 4.1 %collective-permute-done.second = f32[16,128,256]{2,1,0:T(8,128)S(1)} collective-permute-done((f32[16,128,256]{2,1,0:T(8,128)S(1)}, f32[16,128,256]{2,1,0:T(8,128)S(1)}, u32[]{:S(2)}, u32[]{:S(2)}) %collective-permute-start) | collective-permute-done | bytes 2097184 | tf_op jit(solution)/shard_map/ppermute | solution.py:298
  32.8 0.3 add_cores.1
  33.1 0.0 copy-start.2
  33.2 0.3 collective-permute-start.3
  33.5 4.5 %collective-permute-start.5 = (f32[256,256]{1,0:T(8,128)S(1)}, f32[256,256]{1,0:T(8,128)S(1)}, u32[]{:S(2)}, u32[]{:S(2)}) collective-permute-start(f32[256,256]{1,0:T(8,128)S(1)} %get-tuple-element.41), channel_id=1, source_target_pairs={{0,28},{1,29},{2,30},{3,31},{4,0},{5,1},{6,2},{7,3},{8,4},{9,5},{1... | collective-permute-start | bytes 786440 | tf_op jit(solution)/shard_map/ppermute | solution.py:33
  37.9 0.2 collective-permute-start.4
  38.1 4.0 %collective-permute-start.6 = (f32[128,256]{1,0:T(8,128)S(1)}, f32[128,256]{1,0:T(8,128)S(1)}, u32[]{:S(2)}, u32[]{:S(2)}) collective-permute-start(f32[128,256]{1,0:T(8,128)S(1)} %get-tuple-element.42), channel_id=1, source_target_pairs={{0,24},{1,25},{2,26},{3,27},{4,28},{5,29},{6,30},{7,31},{8,0},{9,1... | collective-permute-start | bytes 393224 | tf_op jit(solution)/shard_map/ppermute | solution.py:33
  42.1 0.7 collective-permute-start.2
  42.8 8.5 %collective-permute-done.4.four_up = f32[128,256]{1,0:T(8,128)S(1)} collective-permute-done((f32[128,256]{1,0:T(8,128)S(1)}, f32[128,256]{1,0:T(8,128)S(1)}, u32[]{:S(2)}, u32[]{:S(2)}) %collective-permute-start.4) | collective-permute-done | bytes 131104 | tf_op jit(solution)/shard_map/ppermute | solution.py:33
  51.3 0.0 collective-permute-done.6.four_down
  51.3 0.0 collective-permute-done.3.three
  51.3 0.0 collective-permute-done.5.five
  51.3 0.0 copy-start.1
  51.3 0.0 copy-start.3
  51.3 0.1 relay.1
  51.4 4.5 %collective-permute-start.7 = (f32[256,256]{1,0:T(8,128)S(1)}, f32[256,256]{1,0:T(8,128)S(1)}, u32[]{:S(2)}, u32[]{:S(2)}) collective-permute-start(f32[256,256]{1,0:T(8,128)S(1)} %get-tuple-element.43), channel_id=1, source_target_pairs={{0,8},{1,9},{2,10},{3,11},{4,12},{5,13},{6,14},{7,15},{8,16},{9,17... | collective-permute-start | bytes 786440 | tf_op jit(solution)/shard_map/ppermute | solution.py:33
  56.0 0.0 collective-permute-start.8
  56.0 1.2 collective-permute-start.9
  57.2 2.9 %collective-permute-done.2 = f32[256,256]{1,0:T(8,128)S(1)} collective-permute-done((f32[256,256]{1,0:T(8,128)S(1)}, f32[256,256]{1,0:T(8,128)S(1)}, u32[]{:S(2)}, u32[]{:S(2)}) %collective-permute-start.2) | collective-permute-done | bytes 262176 | tf_op jit(solution)/shard_map/ppermute | solution.py:33
  60.1 3.4 %collective-permute-done.1 = f32[256,256]{1,0:T(8,128)S(1)} collective-permute-done((f32[256,256]{1,0:T(8,128)S(1)}, f32[256,256]{1,0:T(8,128)S(1)}, u32[]{:S(2)}, u32[]{:S(2)}) %collective-permute-start.1) | collective-permute-done | bytes 262176 | tf_op jit(solution)/shard_map/ppermute | solution.py:33
  63.5 6.0 %collective-permute-done.7 = f32[256,256]{1,0:T(8,128)S(1)} collective-permute-done((f32[256,256]{1,0:T(8,128)S(1)}, f32[256,256]{1,0:T(8,128)S(1)}, u32[]{:S(2)}, u32[]{:S(2)}) %collective-permute-start.7) | collective-permute-done | bytes 262176 | tf_op jit(solution)/shard_map/ppermute | solution.py:33
  69.5 0.0 collective-permute-done.8
  69.5 0.1 add_add_fusion.mine
  69.6 1.6 collective-permute-start.10
  71.2 5.0 %collective-permute-done.10.other = f32[256,256]{1,0:T(8,128)S(1)} collective-permute-done((f32[256,256]{1,0:T(8,128)S(1)}, f32[256,256]{1,0:T(8,128)S(1)}, u32[]{:S(2)}, u32[]{:S(2)}) %collective-permute-start.10) | collective-permute-done | bytes 262176 | tf_op jit(solution)/shard_map/ppermute | solution.py:300
  76.2 2.0 %middle.1 = (f32[128,256]{1,0:T(8,128)}, f32[256,256]{1,0:T(8,128)S(1)}, f32[8,40,256]{2,1,0:T(8,128)}) custom-call(s32[3]{0:T(128)S(1)} %pad_add_fusion.where.y_ref, f32[256,256]{1,0:T(8,128)S(1)} %add_add_fusion.mine, f32[256,256]{1,0:T(8,128)S(1)} %collective-permute-done.10.other, f32[256,256]{1,0:T(8,128)S(1)} %copy-done.1, f32[1,256]{1,0:T(1,128)S(1)} %bitcast.19, ...), custom_call_target="tpu_custom_call" | custom-call | tf_op jit(solution)/shard_map/middle/pallas_call | solution.py:184
  78.2 7.3 %all-to-all-start.1 = ((f32[8,40,256]{2,1,0:T(8,128)}), f32[8,40,256]{2,1,0:T(8,128)S(1)}, u32[]{:S(2)}, u32[]{:S(2)}) async-start(f32[8,40,256]{2,1,0:T(8,128)} %get-tuple-element.49), calls=%async_computation.1 | async-start | bytes 655360 | tf_op jit(solution)/shard_map/all_to_all | solution.py:306
  85.4 0.7 collective-permute-start.11
  86.2 1.9 %collective-permute-start.12 = (f32[256,256]{1,0:T(8,128)S(1)}, f32[256,256]{1,0:T(8,128)}, u32[]{:S(2)}, u32[]{:S(2)}) collective-permute-start(f32[256,256]{1,0:T(8,128)S(1)} %get-tuple-element.48), channel_id=1, source_target_pairs={{0,24},{1,25},{2,26},{3,27},{4,28},{5,29},{6,30},{7,31},{8,0},{9,1... | collective-permute-start | bytes 786440 | tf_op jit(solution)/shard_map/ppermute | solution.py:33
  88.0 1.1 collective-permute-start.13
  89.1 1.4 collective-permute-start.14
  90.5 1.9 %all-to-all-done.1 = f32[8,40,256]{2,1,0:T(8,128)S(1)} async-done(((f32[8,40,256]{2,1,0:T(8,128)}), f32[8,40,256]{2,1,0:T(8,128)S(1)}, u32[]{:S(2)}, u32[]{:S(2)}) %all-to-all-start.1) | async-done | bytes 327712 | tf_op jit(solution)/shard_map/all_to_all | solution.py:306
  92.4 5.6 %collective-permute-done.11 = f32[256,256]{1,0:T(8,128)} collective-permute-done((f32[256,256]{1,0:T(8,128)S(1)}, f32[256,256]{1,0:T(8,128)}, u32[]{:S(2)}, u32[]{:S(2)}) %collective-permute-start.11) | collective-permute-done | bytes 262176 | tf_op jit(solution)/shard_map/ppermute | solution.py:33
  98.0 2.4 %collective-permute-done.12 = f32[256,256]{1,0:T(8,128)} collective-permute-done((f32[256,256]{1,0:T(8,128)S(1)}, f32[256,256]{1,0:T(8,128)}, u32[]{:S(2)}, u32[]{:S(2)}) %collective-permute-start.12) | collective-permute-done | bytes 262176 | tf_op jit(solution)/shard_map/ppermute | solution.py:33
  100.5 3.1 %collective-permute-done.13 = f32[256,256]{1,0:T(8,128)S(1)} collective-permute-done((f32[256,256]{1,0:T(8,128)S(1)}, f32[256,256]{1,0:T(8,128)S(1)}, u32[]{:S(2)}, u32[]{:S(2)}) %collective-permute-start.13) | collective-permute-done | bytes 262176 | tf_op jit(solution)/shard_map/ppermute | solution.py:33
  103.6 2.7 %collective-permute-done.14 = f32[256,256]{1,0:T(8,128)S(1)} collective-permute-done((f32[256,256]{1,0:T(8,128)S(1)}, f32[256,256]{1,0:T(8,128)S(1)}, u32[]{:S(2)}, u32[]{:S(2)}) %collective-permute-start.14) | collective-permute-done | bytes 262176 | tf_op jit(solution)/shard_map/ppermute | solution.py:33
  106.3 0.0 collective-permute-start.16
  106.3 0.6 collective-permute-start.17
  106.9 1.0 constant_dynamic-update-slice_fusion.3
  107.9 0.0 collective-permute-done.16
  107.9 0.7 broadcast_in_dim.5
  108.7 6.0 %all-to-all-start.2 = ((f32[8,40,256]{2,1,0:T(8,128)}), f32[8,40,256]{2,1,0:T(8,128)S(1)}, u32[]{:S(2)}, u32[]{:S(2)}) async-start(f32[8,40,256]{2,1,0:T(8,128)} %broadcast_in_dim.5), calls=%async_computation.2 | async-start | bytes 655360 | tf_op jit(solution)/shard_map/all_to_all | solution.py:313
  114.7 1.0 constant_dynamic-update-slice_fusion.2
  115.7 2.1 %collective-permute-start.20 = (f32[256,256]{1,0:T(8,128)S(1)}, f32[256,256]{1,0:T(8,128)S(1)}, u32[]{:S(2)}, u32[]{:S(2)}) collective-permute-start(f32[256,256]{1,0:T(8,128)S(1)} %collective-permute-done.13), channel_id=1, source_target_pairs={{0,4},{1,5},{2,6},{3,7},{4,8},{5,9},{6,10},{7,11},{8,12},{9,13},{1... | collective-permute-start | bytes 786440 | tf_op jit(solution)/shard_map/ppermute | solution.py:33
  117.8 0.1 collective-permute-start.15
  117.9 0.9 slice.7
  118.9 2.8 %collective-permute-start.19 = (f32[128,256]{1,0:T(8,128)S(1)}, f32[128,256]{1,0:T(8,128)S(1)}, u32[]{:S(2)}, u32[]{:S(2)}) collective-permute-start(f32[128,256]{1,0:T(8,128)S(1)} %slice.7), channel_id=1, source_target_pairs={{0,24},{1,25},{2,26},{3,27},{4,28},{5,29},{6,30},{7,31},{8,0},{9,1... | collective-permute-start | bytes 393224 | tf_op jit(solution)/shard_map/ppermute | solution.py:33
  121.6 0.2 collective-permute-start.18
  121.9 8.7 %collective-permute-done.19 = f32[128,256]{1,0:T(8,128)S(1)} collective-permute-done((f32[128,256]{1,0:T(8,128)S(1)}, f32[128,256]{1,0:T(8,128)S(1)}, u32[]{:S(2)}, u32[]{:S(2)}) %collective-permute-start.19) | collective-permute-done | bytes 131104 | tf_op jit(solution)/shard_map/ppermute | solution.py:33
  130.6 5.7 %collective-permute-done.18 = f32[128,256]{1,0:T(8,128)S(1)} collective-permute-done((f32[128,256]{1,0:T(8,128)S(1)}, f32[128,256]{1,0:T(8,128)S(1)}, u32[]{:S(2)}, u32[]{:S(2)}) %collective-permute-start.18) | collective-permute-done | bytes 131104 | tf_op jit(solution)/shard_map/ppermute | solution.py:33
  136.3 1.0 pad_maximum_fusion
  137.3 0.0 all-to-all-done.2
  137.4 0.1 collective-permute-start.21
  137.5 2.3 %collective-permute-done.21 = f32[768,256]{1,0:T(8,128)S(1)} collective-permute-done((f32[768,256]{1,0:T(8,128)S(1)}, f32[768,256]{1,0:T(8,128)S(1)}, u32[]{:S(2)}, u32[]{:S(2)}) %collective-permute-start.21) | collective-permute-done | bytes 786464 | tf_op jit(solution)/shard_map/ppermute | solution.py:316
  139.7 4.8 %backward_tiles.1 = f32[8,168,256]{2,1,0:T(8,128)S(1)} custom-call(s32[12,2]{1,0:T(8,128)S(1)} %copy.13.place, s32[1]{0:T(128)} %bitcast.13.count, s32[3]{0:T(128)S(1)} %pad_add_fusion.where.y_ref, f32[12,128,128]{2,1,0:T(8,128)S(1)} %bitcast.15, f32[10,128,256]{2,1,0:T(8,128)S(1)} %bitcast.17, f32[10,128,256]{2,1,0:T(8,128)} %bitcast.8.other_near, ...), custom_call_target="tpu_custom_call" | custom-call | tf_op jit(solution)/shard_map/backward_tiles/pallas_call | solution.py:242
  144.5 25.2 %all_to_all.20.parts = f32[8,168,256]{2,1,0:T(8,128)S(1)} all-to-all(f32[8,168,256]{2,1,0:T(8,128)S(1)} %backward_tiles.1), channel_id=1, replica_groups=mesh['row'=8,'col'=32] {'row'}, dimensions={0} | all-to-all | bytes 2752512 | tf_op jit(solution)/shard_map/all_to_all | solution.py:325
  169.7 1.0 final.1
  (20 shorter events, 0.2 us)
Async XLA Ops:
  2.6 7.6 %copy-start.4 = (s32[1,1,12,2]{2,3,1,0:T(2,128)S(1)}, s32[1,1,12,2]{2,3,1,0:T(2,128)}, u32[]{:S(2)}) copy-start(s32[1,1,12,2]{2,3,1,0:T(2,128)} %param.11) | copy-start | bytes 292
  2.6 22.1 %copy-start = (f32[1,1,12,128,128]{4,3,2,1,0:T(8,128)S(1)}, f32[1,1,12,128,128]{4,3,2,1,0:T(8,128)}, u32[]{:S(2)}) copy-start(f32[1,1,12,128,128]{4,3,2,1,0:T(8,128)} %param.10) | copy-start | bytes 2359300
  2.6 22.1 %all-to-all-start = ((f32[8,128,256]{2,1,0:T(8,128)}), f32[8,128,256]{2,1,0:T(8,128)S(1)}, u32[]{:S(2)}, u32[]{:S(2)}) async-start(f32[8,128,256]{2,1,0:T(8,128)} %broadcast_in_dim.4), calls=%async_computation | async-start | bytes 2097152 | tf_op jit(solution)/shard_map/all_to_all | solution.py:293
  28.6 4.2 %collective-permute-start = (f32[16,128,256]{2,1,0:T(8,128)S(1)}, f32[16,128,256]{2,1,0:T(8,128)S(1)}, u32[]{:S(2)}, u32[]{:S(2)}) collective-permute-start(f32[16,128,256]{2,1,0:T(8,128)S(1)} %get-tuple-element.33), channel_id=1, source_target_pairs={{0,1},{1,0},{2,3},{3,2},{4,5},{5,4},{6,7},{7,6},{8,9},{9,8},{10,11... | collective-permute-start | bytes 6291464 | tf_op jit(solution)/shard_map/ppermute | solution.py:298
  33.1 22.8 %copy-start.2 = (f32[128,256]{1,0:T(8,128)S(1)}, f32[128,256]{1,0:T(8,128)}, u32[]{:S(2)}) copy-start(f32[128,256]{1,0:T(8,128)} %cot_own.1) | copy-start | bytes 393220
  33.2 18.2 %collective-permute-start.3 = (f32[256,256]{1,0:T(8,128)S(1)}, f32[256,256]{1,0:T(8,128)S(1)}, u32[]{:S(2)}, u32[]{:S(2)}) collective-permute-start(f32[256,256]{1,0:T(8,128)S(1)} %get-tuple-element.38), channel_id=1, source_target_pairs={{0,4},{1,5},{2,6},{3,7},{4,8},{5,9},{6,10},{7,11},{8,12},{9,13},{1... | collective-permute-start | bytes 786440 | tf_op jit(solution)/shard_map/ppermute | solution.py:33
  33.5 17.9 %collective-permute-start.5 = (f32[256,256]{1,0:T(8,128)S(1)}, f32[256,256]{1,0:T(8,128)S(1)}, u32[]{:S(2)}, u32[]{:S(2)}) collective-permute-start(f32[256,256]{1,0:T(8,128)S(1)} %get-tuple-element.41), channel_id=1, source_target_pairs={{0,28},{1,29},{2,30},{3,31},{4,0},{5,1},{6,2},{7,3},{8,4},{9,5},{1... | collective-permute-start | bytes 786440 | tf_op jit(solution)/shard_map/ppermute | solution.py:33
  37.9 13.4 %collective-permute-start.4 = (f32[128,256]{1,0:T(8,128)S(1)}, f32[128,256]{1,0:T(8,128)S(1)}, u32[]{:S(2)}, u32[]{:S(2)}) collective-permute-start(f32[128,256]{1,0:T(8,128)S(1)} %get-tuple-element.39), channel_id=1, source_target_pairs={{0,8},{1,9},{2,10},{3,11},{4,12},{5,13},{6,14},{7,15},{8,16},{9,17... | collective-permute-start | bytes 393224 | tf_op jit(solution)/shard_map/ppermute | solution.py:33
  38.1 13.2 %collective-permute-start.6 = (f32[128,256]{1,0:T(8,128)S(1)}, f32[128,256]{1,0:T(8,128)S(1)}, u32[]{:S(2)}, u32[]{:S(2)}) collective-permute-start(f32[128,256]{1,0:T(8,128)S(1)} %get-tuple-element.42), channel_id=1, source_target_pairs={{0,24},{1,25},{2,26},{3,27},{4,28},{5,29},{6,30},{7,31},{8,0},{9,1... | collective-permute-start | bytes 393224 | tf_op jit(solution)/shard_map/ppermute | solution.py:33
  42.1 18.0 %collective-permute-start.2 = (f32[256,256]{1,0:T(8,128)S(1)}, f32[256,256]{1,0:T(8,128)S(1)}, u32[]{:S(2)}, u32[]{:S(2)}) collective-permute-start(f32[256,256]{1,0:T(8,128)S(1)} %get-tuple-element.36), channel_id=1, source_target_pairs={{0,28},{1,29},{2,30},{3,31},{4,0},{5,1},{6,2},{7,3},{8,4},{9,5},{1... | collective-permute-start | bytes 786440 | tf_op jit(solution)/shard_map/ppermute | solution.py:33
  51.3 12.2 %collective-permute-start.1 = (f32[256,256]{1,0:T(8,128)S(1)}, f32[256,256]{1,0:T(8,128)S(1)}, u32[]{:S(2)}, u32[]{:S(2)}) collective-permute-start(f32[256,256]{1,0:T(8,128)S(1)} %get-tuple-element.35), channel_id=1, source_target_pairs={{0,4},{1,5},{2,6},{3,7},{4,8},{5,9},{6,10},{7,11},{8,12},{9,13},{1... | collective-permute-start | bytes 786440 | tf_op jit(solution)/shard_map/ppermute | solution.py:33
  51.3 24.9 %copy-start.1 = (f32[256,256]{1,0:T(8,128)S(1)}, f32[256,256]{1,0:T(8,128)}, u32[]{:S(2)}) copy-start(f32[256,256]{1,0:T(8,128)} %weight.3) | copy-start | bytes 786436
  51.3 24.9 %copy-start.3 = (f32[256]{0:T(256)S(1)}, f32[256]{0:T(256)}, u32[]{:S(2)}) copy-start(f32[256]{0:T(256)} %param.9) | copy-start | bytes 3076
  51.4 18.0 %collective-permute-start.7 = (f32[256,256]{1,0:T(8,128)S(1)}, f32[256,256]{1,0:T(8,128)S(1)}, u32[]{:S(2)}, u32[]{:S(2)}) collective-permute-start(f32[256,256]{1,0:T(8,128)S(1)} %get-tuple-element.43), channel_id=1, source_target_pairs={{0,8},{1,9},{2,10},{3,11},{4,12},{5,13},{6,14},{7,15},{8,16},{9,17... | collective-permute-start | bytes 786440 | tf_op jit(solution)/shard_map/ppermute | solution.py:33
  56.0 13.5 %collective-permute-start.8 = (f32[256,256]{1,0:T(8,128)S(1)}, f32[256,256]{1,0:T(8,128)S(1)}, u32[]{:S(2)}, u32[]{:S(2)}) collective-permute-start(f32[256,256]{1,0:T(8,128)S(1)} %get-tuple-element.44), channel_id=1, source_target_pairs={{0,24},{1,25},{2,26},{3,27},{4,28},{5,29},{6,30},{7,31},{8,0},{9,1... | collective-permute-start | bytes 786440 | tf_op jit(solution)/shard_map/ppermute | solution.py:33
  56.0 13.6 %collective-permute-start.9 = (f32[128,256]{1,0:T(8,128)S(1)}, f32[128,256]{1,0:T(8,128)S(1)}, u32[]{:S(2)}, u32[]{:S(2)}) collective-permute-start(f32[128,256]{1,0:T(8,128)S(1)} %copy-done.2), channel_id=1, source_target_pairs={{0,2},{1,3},{2,0},{3,1},{4,6},{5,7},{6,4},{7,5},{8,10},{9,11},{10,... | collective-permute-start | bytes 393224 | tf_op jit(solution)/shard_map/ppermute | solution.py:297
  69.6 6.6 %collective-permute-start.10 = (f32[256,256]{1,0:T(8,128)S(1)}, f32[256,256]{1,0:T(8,128)S(1)}, u32[]{:S(2)}, u32[]{:S(2)}) collective-permute-start(f32[256,256]{1,0:T(8,128)S(1)} %add_add_fusion.mine), channel_id=1, source_target_pairs={{0,2},{1,3},{2,0},{3,1},{4,6},{5,7},{6,4},{7,5},{8,10},{9,11},{10,... | collective-permute-start | bytes 786440 | tf_op jit(solution)/shard_map/ppermute | solution.py:300
  78.2 14.2 %all-to-all-start.1 = ((f32[8,40,256]{2,1,0:T(8,128)}), f32[8,40,256]{2,1,0:T(8,128)S(1)}, u32[]{:S(2)}, u32[]{:S(2)}) async-start(f32[8,40,256]{2,1,0:T(8,128)} %get-tuple-element.49), calls=%async_computation.1 | async-start | bytes 655360 | tf_op jit(solution)/shard_map/all_to_all | solution.py:306
  85.4 12.6 %collective-permute-start.11 = (f32[256,256]{1,0:T(8,128)S(1)}, f32[256,256]{1,0:T(8,128)}, u32[]{:S(2)}, u32[]{:S(2)}) collective-permute-start(f32[256,256]{1,0:T(8,128)S(1)} %get-tuple-element.48), channel_id=1, source_target_pairs={{0,28},{1,29},{2,30},{3,31},{4,0},{5,1},{6,2},{7,3},{8,4},{9,5},{1... | collective-permute-start | bytes 786440 | tf_op jit(solution)/shard_map/ppermute | solution.py:33
  86.2 14.3 %collective-permute-start.12 = (f32[256,256]{1,0:T(8,128)S(1)}, f32[256,256]{1,0:T(8,128)}, u32[]{:S(2)}, u32[]{:S(2)}) collective-permute-start(f32[256,256]{1,0:T(8,128)S(1)} %get-tuple-element.48), channel_id=1, source_target_pairs={{0,24},{1,25},{2,26},{3,27},{4,28},{5,29},{6,30},{7,31},{8,0},{9,1... | collective-permute-start | bytes 786440 | tf_op jit(solution)/shard_map/ppermute | solution.py:33
  88.0 15.6 %collective-permute-start.13 = (f32[256,256]{1,0:T(8,128)S(1)}, f32[256,256]{1,0:T(8,128)S(1)}, u32[]{:S(2)}, u32[]{:S(2)}) collective-permute-start(f32[256,256]{1,0:T(8,128)S(1)} %get-tuple-element.48), channel_id=1, source_target_pairs={{0,8},{1,9},{2,10},{3,11},{4,12},{5,13},{6,14},{7,15},{8,16},{9,17... | collective-permute-start | bytes 786440 | tf_op jit(solution)/shard_map/ppermute | solution.py:33
  89.1 17.3 %collective-permute-start.14 = (f32[256,256]{1,0:T(8,128)S(1)}, f32[256,256]{1,0:T(8,128)S(1)}, u32[]{:S(2)}, u32[]{:S(2)}) collective-permute-start(f32[256,256]{1,0:T(8,128)S(1)} %get-tuple-element.48), channel_id=1, source_target_pairs={{0,4},{1,5},{2,6},{3,7},{4,8},{5,9},{6,10},{7,11},{8,12},{9,13},{1... | collective-permute-start | bytes 786440 | tf_op jit(solution)/shard_map/ppermute | solution.py:33
  106.3 1.6 collective-permute-start.16
  106.3 30.0 %collective-permute-start.17 = (f32[256,256]{1,0:T(8,128)}, f32[256,256]{1,0:T(8,128)}, u32[]{:S(2)}, u32[]{:S(2)}) collective-permute-start(f32[256,256]{1,0:T(8,128)} %collective-permute-done.12), channel_id=1, source_target_pairs={{0,28},{1,29},{2,30},{3,31},{4,0},{5,1},{6,2},{7,3},{8,4},{9,5},{1... | collective-permute-start | bytes 786440 | tf_op jit(solution)/shard_map/ppermute | solution.py:33
  108.7 28.6 %all-to-all-start.2 = ((f32[8,40,256]{2,1,0:T(8,128)}), f32[8,40,256]{2,1,0:T(8,128)S(1)}, u32[]{:S(2)}, u32[]{:S(2)}) async-start(f32[8,40,256]{2,1,0:T(8,128)} %broadcast_in_dim.5), calls=%async_computation.2 | async-start | bytes 655360 | tf_op jit(solution)/shard_map/all_to_all | solution.py:313
  115.7 20.6 %collective-permute-start.20 = (f32[256,256]{1,0:T(8,128)S(1)}, f32[256,256]{1,0:T(8,128)S(1)}, u32[]{:S(2)}, u32[]{:S(2)}) collective-permute-start(f32[256,256]{1,0:T(8,128)S(1)} %collective-permute-done.13), channel_id=1, source_target_pairs={{0,4},{1,5},{2,6},{3,7},{4,8},{5,9},{6,10},{7,11},{8,12},{9,13},{1... | collective-permute-start | bytes 786440 | tf_op jit(solution)/shard_map/ppermute | solution.py:33
  117.8 19.6 %collective-permute-start.15 = (f32[1280,256]{1,0:T(8,128)S(1)}, f32[1280,256]{1,0:T(8,128)}, u32[]{:S(2)}, u32[]{:S(2)}) collective-permute-start(f32[1280,256]{1,0:T(8,128)S(1)} %constant_dynamic-update-slice_fusion), channel_id=1, source_target_pairs={{0,1},{1,0},{2,3},{3,2},{4,5},{5,4},{6,7},{7,6},{8,9},{9,8},{10,11... | collective-permute-start | bytes 3932168 | tf_op jit(solution)/shard_map/ppermute | solution.py:310
  118.9 11.7 %collective-permute-start.19 = (f32[128,256]{1,0:T(8,128)S(1)}, f32[128,256]{1,0:T(8,128)S(1)}, u32[]{:S(2)}, u32[]{:S(2)}) collective-permute-start(f32[128,256]{1,0:T(8,128)S(1)} %slice.7), channel_id=1, source_target_pairs={{0,24},{1,25},{2,26},{3,27},{4,28},{5,29},{6,30},{7,31},{8,0},{9,1... | collective-permute-start | bytes 393224 | tf_op jit(solution)/shard_map/ppermute | solution.py:33
  121.6 14.7 %collective-permute-start.18 = (f32[128,256]{1,0:T(8,128)S(1)}, f32[128,256]{1,0:T(8,128)S(1)}, u32[]{:S(2)}, u32[]{:S(2)}) collective-permute-start(f32[128,256]{1,0:T(8,128)S(1)} %slice.6), channel_id=1, source_target_pairs={{0,8},{1,9},{2,10},{3,11},{4,12},{5,13},{6,14},{7,15},{8,16},{9,17... | collective-permute-start | bytes 393224 | tf_op jit(solution)/shard_map/ppermute | solution.py:33
  137.4 2.4 %collective-permute-start.21 = (f32[768,256]{1,0:T(8,128)S(1)}, f32[768,256]{1,0:T(8,128)S(1)}, u32[]{:S(2)}, u32[]{:S(2)}) collective-permute-start(f32[768,256]{1,0:T(8,128)S(1)} %pad_maximum_fusion), channel_id=1, source_target_pairs={{0,1},{1,0},{2,3},{3,2},{4,5},{5,4},{6,7},{7,6},{8,9},{9,8},{10,11... | collective-permute-start | bytes 2359304 | tf_op jit(solution)/shard_map/ppermute | solution.py:316

commit v3 on v2

v3 whole, which is shorter than its diff:
```python
import functools
import math

import jax
import jax.numpy as jnp
from jax import lax
from jax.experimental import pallas as pl
from jax.experimental.pallas import tpu as pltpu
from jax.sharding import PartitionSpec as P

Z, YL = 8, 2
TILE = 128
PAIR = YL * TILE
JOIN_COST = 10**12
HALVES_COST = 10**12


def col_pairs(move):
    pairs = []
    for z in range(Z):
        for y in range(YL):
            for core in range(2):
                a, b, c = move(z, y, core)
                pairs.append(((z * YL + y) * 2 + core, (a * YL + b) * 2 + c))
    return pairs


CORE_SWAP = col_pairs(lambda z, y, core: (z, y, 1 - core))
Y_SWAP = col_pairs(lambda z, y, core: (z, 1 - y, core))
Z_GROUPS = [[(z * YL + y) * 2 + core for z in range(Z)] for y in range(YL) for core in range(2)]


def z_shift(value, distance):
    return lax.ppermute(value, "col", col_pairs(lambda z, y, core: ((z + distance) % Z, y, core)))


SMEM = pl.BlockSpec(memory_space=pltpu.SMEM)
VMEM = pl.BlockSpec(memory_space=pltpu.VMEM)


def params(mib):
    return pltpu.CompilerParams(vmem_limit_bytes=mib * 1024 * 1024)


def shaped(*shape):
    return jax.ShapeDtypeStruct(shape, jnp.float32)


def split(value):
    high = value.astype(jnp.bfloat16)
    low = (value - high.astype(jnp.float32)).astype(jnp.bfloat16)
    return high, low


def dot3(left, right, contract):
    def one(a, b):
        return lax.dot_general(a, b, (contract, ((), ())), preferred_element_type=jnp.float32)

    return one(left[0], right[0]) + (one(left[0], right[1]) + one(left[1], right[0]))


def locate(tile, where):
    mine = lax.rem(tile, 2) == where[2]
    distance = lax.rem(lax.div(tile, 2 * YL) - where[0] + Z, Z)
    return mine, distance, lax.rem(lax.div(tile, 2), YL)


def broadcast_kernel(block, out):
    for j in range(out.shape[0]):
        out[j] = block[...]


def broadcast(block, copies):
    return pl.pallas_call(
        broadcast_kernel,
        out_shape=shaped(copies, *block.shape),
        in_specs=[VMEM],
        out_specs=VMEM,
        compiler_params=params(3),
        name="broadcast_rows",
    )(block)


def forward_kernel(place, count, where, values, features, keep, send, high, low):
    keep[...] = jnp.zeros_like(keep)
    send[...] = jnp.zeros_like(send)
    for j in range(features.shape[0]):
        high[j], low[j] = split(features[j])
    for k in range(values.shape[0]):
        col = place[k, 1]
        mine, distance, y = locate(place[k, 0], where)
        live = k < count[0]
        product = dot3(split(values[k]), (high[col], low[col]), ((1,), (0,)))
        index = distance * YL + y
        keep[index] += jnp.where(live & mine, product, 0.0)
        send[index] += jnp.where(live & ~mine, product, 0.0)


def forward(place, count, where, values, features):
    tiles = Z * YL
    width = features.shape[-1]
    return pl.pallas_call(
        forward_kernel,
        out_shape=(shaped(tiles, TILE, width),) * 2,
        in_specs=[SMEM, SMEM, SMEM, VMEM, VMEM],
        out_specs=(VMEM,) * 2,
        scratch_shapes=[
            pltpu.VMEM(features.shape, jnp.bfloat16),
            pltpu.VMEM(features.shape, jnp.bfloat16),
        ],
        compiler_params=params(12),
        name="forward_tiles",
    )(place, count, where, values, features)


def add_cores_kernel(first, second, own, one, two, three, four_up, four_down, five, six, seven):
    def total(tile):
        return first[tile] + second[tile]

    for distance, out in ((3, three), (5, five), (0, own), (1, one), (2, two), (6, six), (7, seven)):
        for y in range(YL):
            out[y * TILE : (y + 1) * TILE, :] = total(distance * YL + y)
    four_up[...] = total(4 * YL)
    four_down[...] = total(4 * YL + 1)


def add_cores(first, second):
    width = first.shape[-1]
    whole, half = shaped(PAIR, width), shaped(TILE, width)
    return pl.pallas_call(
        add_cores_kernel,
        out_shape=(whole,) * 4 + (half,) * 2 + (whole,) * 3,
        in_specs=[VMEM] * 2,
        out_specs=(VMEM,) * 9,
        compiler_params=params(10),
        name="add_cores",
    )(first, second)


def relay_kernel(two, three, four_up, six, five, four_down, up, down):
    up[:TILE, :] = two[:TILE, :] + three[:TILE, :] + four_up[...]
    up[TILE:, :] = two[TILE:, :] + three[TILE:, :]
    down[:TILE, :] = six[:TILE, :] + five[:TILE, :]
    down[TILE:, :] = six[TILE:, :] + five[TILE:, :] + four_down[...]


def relay(*operands):
    return pl.pallas_call(
        relay_kernel,
        out_shape=(jax.ShapeDtypeStruct(operands[0].shape, jnp.float32),) * 2,
        in_specs=[VMEM] * 6,
        out_specs=(VMEM,) * 2,
        compiler_params=params(5),
        name="relay",
    )(*operands)


def scatter_z(own, one, two, three, four_up, four_down, five, six, seven):
    from_three, from_five = z_shift(three, 1), z_shift(five, -1)
    from_up, from_down = z_shift(four_up, 2), z_shift(four_down, -2)
    from_one, from_seven = z_shift(one, 1), z_shift(seven, -1)
    up, down = relay(two, from_three, from_up, six, from_five, from_down)
    from_two, from_six = z_shift(up, 2), z_shift(down, -2)
    return ((own + from_one) + from_seven) + (from_two + from_six)


def middle_kernel(where, mine, other, weight, bias, cot_own, cot_other, output, grad, total, cots):
    y = where[1]
    cots[y] = cot_own[...]
    cots[1 - y] = cot_other[...]
    cot = cots[...].reshape(grad.shape)
    summed = mine[...] + other[...]
    total[...] = summed
    pre = dot3(split(summed), split(weight[...]), ((1,), (0,))) + bias[...]
    sigma = jax.nn.sigmoid(pre)
    grad[...] = cot * (sigma * (1.0 + pre * (1.0 - sigma)))
    cots[...] = (pre * sigma).reshape(cots.shape)
    output[...] = cots[y]


def middle(where, mine, other, weight, bias, cot_own, cot_other):
    width = weight.shape[1]
    return pl.pallas_call(
        middle_kernel,
        out_shape=(shaped(TILE, width), shaped(PAIR, width), shaped(PAIR, weight.shape[0])),
        in_specs=[SMEM] + [VMEM] * 6,
        out_specs=(VMEM,) * 3,
        scratch_shapes=[pltpu.VMEM((YL, TILE, width), jnp.float32)],
        compiler_params=params(6),
        name="middle",
    )(where, mine, other, weight, bias, cot_own, cot_other)


def outer_kernel(total, grad, extra):
    value = grad[...]
    sums = jnp.broadcast_to(jnp.sum(value, axis=0, keepdims=True), (8, value.shape[1]))
    product = dot3(split(total[...]), split(value), ((0,), (0,)))
    pieces = extra.shape[0]
    rows = product.shape[0] // pieces
    for j in range(pieces):
        extra[j, :rows, :] = product[j * rows : (j + 1) * rows, :]
        extra[j, rows:, :] = sums


def outer(total, grad, pieces):
    return pl.pallas_call(
        outer_kernel,
        out_shape=shaped(pieces, total.shape[1] // pieces + 8, grad.shape[1]),
        in_specs=[VMEM] * 2,
        out_specs=VMEM,
        compiler_params=params(4),
        name="outer",
    )(total, grad)


def spread_kernel(parts, out):
    piece = parts[0]
    for j in range(1, parts.shape[0]):
        piece = piece + parts[j]
    for j in range(out.shape[0]):
        out[j] = piece


def spread(parts, copies):
    return pl.pallas_call(
        spread_kernel,
        out_shape=shaped(copies, *parts.shape[1:]),
        in_specs=[VMEM],
        out_specs=VMEM,
        compiler_params=params(3),
        name="spread",
    )(parts)


def halves_kernel(two, six, low, high):
    low[...] = six[:TILE, :]
    high[...] = two[TILE:, :]


def halves(two, six):
    return pl.pallas_call(
        halves_kernel,
        out_shape=(shaped(TILE, two.shape[1]),) * 2,
        in_specs=[VMEM] * 2,
        out_specs=(VMEM,) * 2,
        compiler_params=params(3),
        cost_estimate=pl.CostEstimate(flops=HALVES_COST, bytes_accessed=0, transcendentals=0),
        name="halves",
    )(two, six)


def join_kernel(*refs):
    out = refs[-1]
    start = 0
    for part in refs[:-1]:
        out[start : start + part.shape[0], :] = part[...]
        start += part.shape[0]


def join(*blocks):
    rows, width = sum(block.shape[0] for block in blocks), blocks[0].shape[1]
    return pl.pallas_call(
        join_kernel,
        out_shape=shaped(rows, width),
        in_specs=[VMEM] * len(blocks),
        out_specs=VMEM,
        compiler_params=params(8),
        cost_estimate=pl.CostEstimate(flops=JOIN_COST, bytes_accessed=0, transcendentals=0),
        name="join",
    )(*blocks)


def total_kernel(parts, out, *, factor):
    piece = parts[0]
    for j in range(1, parts.shape[0]):
        piece = piece + parts[j]
    out[...] = piece * factor


def total_of(parts, factor):
    return pl.pallas_call(
        functools.partial(total_kernel, factor=factor),
        out_shape=shaped(*parts.shape[1:]),
        in_specs=[VMEM],
        out_specs=VMEM,
        compiler_params=params(3),
        name="total",
    )(parts)


def backward_kernel(place, count, where, values, own, other, piece, piece_other, back):
    back[...] = jnp.zeros_like(back)
    for k in range(values.shape[0]):
        mine, distance, y = locate(place[k, 0], where)
        rows = pl.ds(pl.multiple_of((distance * YL + y) * TILE, TILE), TILE)
        block = jnp.where(mine, own[rows, :], other[rows, :])
        product = dot3(split(values[k]), split(block), ((0,), (0,)))
        back[place[k, 1], :TILE, :] += jnp.where(k < count[0], product, 0.0)
    both = piece[...] + piece_other[...]
    for j in range(back.shape[0]):
        back[j, TILE:, :] = both


def backward(place, count, where, values, own, other, piece, piece_other, tiles):
    return pl.pallas_call(
        backward_kernel,
        out_shape=shaped(tiles, TILE + piece.shape[0], own.shape[1]),
        in_specs=[SMEM] * 3 + [VMEM] * 5,
        out_specs=VMEM,
        compiler_params=params(12),
        name="backward_tiles",
    )(place, count, where, values, own, other, piece, piece_other)


def final_kernel(parts, weight, result, weight_grad, bias_grad):
    back = parts[0, :TILE, :]
    for j in range(1, parts.shape[0]):
        back = back + parts[j, :TILE, :]
    result[...] = dot3(split(back), split(weight[...]), ((1,), (1,)))
    rows = parts.shape[1] - TILE - 8
    for j in range(parts.shape[0]):
        weight_grad[j * rows : (j + 1) * rows, :] = parts[j, TILE : TILE + rows, :]
    bias_grad[...] = parts[0, TILE + rows : TILE + rows + 1, :]


def final(parts, weight):
    return pl.pallas_call(
        final_kernel,
        out_shape=(
            shaped(TILE, weight.shape[0]),
            shaped(*weight.shape),
            shaped(1, weight.shape[1]),
        ),
        in_specs=[VMEM, VMEM],
        out_specs=(VMEM,) * 3,
        compiler_params=params(5),
        name="final",
    )(parts, weight)


def body(node_features, weight, bias, tile_values, tile_coords, tile_count, cotangent):
    values = tile_values[0, 0]
    local_nodes, width = node_features.shape
    row_count = lax.axis_size("row")
    col_count = lax.axis_size("col")
    factor = 1.0 / math.sqrt(local_nodes * row_count * col_count)

    features = lax.all_to_all(broadcast(node_features, row_count), "row", 0, 0)
    features, tile_coords, tile_count, col = lax.optimization_barrier(
        (features, tile_coords, tile_count, lax.axis_index("col"))
    )
    place, count = tile_coords[0, 0], tile_count.reshape(1)
    where = jnp.stack([lax.div(col, 2 * YL), lax.rem(lax.div(col, 2), YL), lax.rem(col, 2)])
    keep, send = forward(place, count, where, values, features)
    cot_other = lax.ppermute(cotangent, "col", Y_SWAP)
    summed = scatter_z(*add_cores(keep, lax.ppermute(send, "col", CORE_SWAP)))
    summed, cot_other = lax.optimization_barrier((summed, cot_other))
    summed_other = lax.ppermute(summed, "col", Y_SWAP)
    output, grads, total = middle(
        where, summed, summed_other, weight, bias.reshape(1, width), cotangent, cot_other
    )

    two, six = z_shift(grads, -2), z_shift(grads, 2)
    one, seven = z_shift(grads, -1), z_shift(grads, 1)
    parts = lax.all_to_all(outer(total, grads, row_count), "row", 0, 0)
    parts = lax.all_to_all(spread(parts, Z), "col", 0, 0, axis_index_groups=Z_GROUPS)
    three, five = z_shift(two, -1), z_shift(six, 1)
    low, high = halves(two, six)
    low, high = z_shift(low, 2), z_shift(high, -2)
    own = join(grads, one, two, three, low, high, five, six, seven)
    piece = total_of(parts, factor)
    own, piece = lax.optimization_barrier((own, piece))
    other = lax.ppermute(own, "col", CORE_SWAP)
    piece_other = lax.ppermute(piece, "col", CORE_SWAP)
    back = backward(place, count, where, values, own, other, piece, piece_other, row_count)
    parts = lax.all_to_all(back, "row", 0, 0)
    input_grad, weight_grad, bias_grad = final(parts, weight)
    return (output, input_grad, weight_grad, bias_grad.reshape(width))


def solution(mesh):
    in_specs = (
        P(("col", "row"), None),
        P(),
        P(),
        P("row", "col", None, None, None),
        P("row", "col", None, None),
        P("row", "col"),
        P(("row", "col"), None),
    )
    out_specs = (P(("row", "col"), None), P(("col", "row"), None), P(), P())
    return jax.shard_map(body, mesh=mesh, in_specs=in_specs, out_specs=out_specs, check_vma=False)
```

time: 173 us -> 152 us (0.88)
  waiting for transfers between devices: 76.3 us -> 60.6 us
  local copies, waits for them, and re-layouts: 5.75 us -> 1.11 us
  Pallas kernels: 11.9 us -> 14.8 us
    ppermute x16, waiting for transfers between devices: 49.2 us -> 31.1 us  [z_shift(): lax.ppermute(value, 'col', col_pairs(lambda z, y, core: ((z + distance) %...]
    pallas_call x0 -> x6, Pallas kernels: none -> 8.44 us  [the longest x1 2.03 us: outer(): pl.pallas_call(outer_kernel, out_shape=shaped(pieces, total.shape[1] // p...]
    all_to_all x3, starting transfers between devices: 20.9 us -> 17 us  [the longest x1 7.46 us: body(): features = lax.all_to_all(broadcast(node_features, row_count), 'row', 0, 0)]
    ppermute x16, starting transfers between devices: 24.9 us -> 28.3 us  [z_shift(): lax.ppermute(value, 'col', col_pairs(lambda z, y, core: ((z + distance) %...]
    pallas_call x1, Pallas kernels: 4.77 us -> 1.63 us  [backward(): pl.pallas_call(backward_kernel, out_shape=shaped(tiles, TILE + piece.shap...]
    broadcast_in_dim x2 -> x0, local copies, waits for them, and re-layouts: 2.71 us -> none  [the longest x1 1.97 us: body(): jnp.broadcast_to(node_features[None], (row_count, local_nodes, width))]
    pallas_call x1, Pallas kernels: 3.84 us -> 1.89 us  [forward(): pl.pallas_call(forward_kernel, out_shape=(shaped(tiles, TILE, width),) *...]
    ppermute x3 -> x2, waiting for transfers between devices: 2.27 us -> 3.71 us  [the longest x1 3.71 us: body(): piece_other = lax.ppermute(piece, 'col', CORE_SWAP)]
  transfers between devices with their start and end apart: 25 -> 24, of which waited for: 15 -> 12; matrix products, arithmetic and copies ran while one was open for 3% -> 0% of each run, Pallas kernels for 0% -> 4%
where the time goes in v3:
time: 152 us; the launch traced here: 151 us
  waiting for transfers between devices  60.6 us (40%)
  starting transfers between devices  47.4 us (31%)
  blocking collectives  25 us (16%)
  Pallas kernels  14.8 us (10%)
    ppermute x16, waiting for transfers between devices, z_shift(): lax.ppermute(value, 'col', col_pairs(lambda z, y, core: ((z + distance) %...  31.1 us
    ppermute x16, starting transfers between devices, z_shift(): lax.ppermute(value, 'col', col_pairs(lambda z, y, core: ((z + distance) %...  28.3 us
    all_to_all x1, blocking collectives, body(): parts = lax.all_to_all(back, 'row', 0, 0)  25 us
    all_to_all x1, waiting for transfers between devices, body(): features = lax.all_to_all(broadcast(node_features, row_count), 'row', 0, 0)  13.9 us
    all_to_all x1, starting transfers between devices, body(): features = lax.all_to_all(broadcast(node_features, row_count), 'row', 0, 0)  7.46 us
    ppermute x1, waiting for transfers between devices, body(): summed_other = lax.ppermute(summed, 'col', Y_SWAP)  6.35 us
    all_to_all x1, starting transfers between devices, body(): parts = lax.all_to_all(outer(total, grads, row_count), 'row', 0, 0)  5.44 us
    ppermute x1, waiting for transfers between devices, body(): summed = scatter_z(*add_cores(keep, lax.ppermute(send, 'col', CORE_SWAP)))  4.15 us
  transfers between devices with their start and end apart: 24, of which 12 were waited for; matrix products, arithmetic and copies ran while one was open for 0% of the time, Pallas kernels for 4%

profile of v3, /device:TPU:2, one launch (start us, length us, event | category | flops | bytes accessed | tf_op | source)
XLA Modules:
  0.0 150.6 jit_solution(14442060396273099007)
XLA Ops:
  0.7 1.0 copy-done.3
  1.6 1.1 broadcast_rows.1
  2.7 7.5 %all-to-all-start = ((f32[8,128,256]{2,1,0:T(8,128)}), f32[8,128,256]{2,1,0:T(8,128)S(1)}, u32[]{:S(2)}, u32[]{:S(2)}) async-start(f32[8,128,256]{2,1,0:T(8,128)} %broadcast_rows.1), calls=%async_computation | async-start | bytes 2097152 | tf_op jit(solution)/shard_map/all_to_all | solution.py:348
  10.8 13.9 %all-to-all-done.features = f32[8,128,256]{2,1,0:T(8,128)S(1)} async-done(((f32[8,128,256]{2,1,0:T(8,128)}), f32[8,128,256]{2,1,0:T(8,128)S(1)}, u32[]{:S(2)}, u32[]{:S(2)}) %all-to-all-start) | async-done | bytes 1048608 | tf_op jit(solution)/shard_map/all_to_all | solution.py:348
  24.7 0.1 copy.11.place
  24.8 0.1 pad_add_fusion.where
  24.9 1.9 %forward_tiles.1 = (f32[16,128,256]{2,1,0:T(8,128)S(1)}, f32[16,128,256]{2,1,0:T(8,128)S(1)}) custom-call(s32[12,2]{1,0:T(8,128)S(1)} %copy.11.place, s32[1]{0:T(128)} %bitcast.8.count, s32[3]{0:T(128)S(1)} %pad_add_fusion.where, f32[12,128,128]{2,1,0:T(8,128)S(1)} %bitcast.10, f32[8,128,256]{2,1,0:T(8,128)S(1)} %all-to-all-done.features), custom_call_target="tpu_custom_call" | custom-call | tf_op jit(solution)/shard_map/forward_tiles/pallas_call | solution.py:102
  26.8 0.1 collective-permute-start
  26.9 4.1 %collective-permute-done.second = f32[16,128,256]{2,1,0:T(8,128)S(1)} collective-permute-done((f32[16,128,256]{2,1,0:T(8,128)S(1)}, f32[16,128,256]{2,1,0:T(8,128)S(1)}, u32[]{:S(2)}, u32[]{:S(2)}) %collective-permute-start) | collective-permute-done | bytes 2097184 | tf_op jit(solution)/shard_map/ppermute | solution.py:356
  31.0 0.2 add_cores.1
  31.2 0.0 copy-start.1
  31.2 0.0 copy-start.9
  31.3 2.0 %collective-permute-start.3 = (f32[256,256]{1,0:T(8,128)S(1)}, f32[256,256]{1,0:T(8,128)S(1)}, u32[]{:S(2)}, u32[]{:S(2)}) collective-permute-start(f32[256,256]{1,0:T(8,128)S(1)} %get-tuple-element.43), channel_id=1, source_target_pairs={{0,4},{1,5},{2,6},{3,7},{4,8},{5,9},{6,10},{7,11},{8,12},{9,13},{1... | collective-permute-start | bytes 786440 | tf_op jit(solution)/shard_map/ppermute | solution.py:34
  33.3 4.0 %collective-permute-start.5 = (f32[256,256]{1,0:T(8,128)S(1)}, f32[256,256]{1,0:T(8,128)S(1)}, u32[]{:S(2)}, u32[]{:S(2)}) collective-permute-start(f32[256,256]{1,0:T(8,128)S(1)} %get-tuple-element.46), channel_id=1, source_target_pairs={{0,28},{1,29},{2,30},{3,31},{4,0},{5,1},{6,2},{7,3},{8,4},{9,5},{1... | collective-permute-start | bytes 786440 | tf_op jit(solution)/shard_map/ppermute | solution.py:34
  37.3 0.0 collective-permute-start.4
  37.3 4.1 %collective-permute-start.6 = (f32[128,256]{1,0:T(8,128)S(1)}, f32[128,256]{1,0:T(8,128)S(1)}, u32[]{:S(2)}, u32[]{:S(2)}) collective-permute-start(f32[128,256]{1,0:T(8,128)S(1)} %get-tuple-element.47), channel_id=1, source_target_pairs={{0,24},{1,25},{2,26},{3,27},{4,28},{5,29},{6,30},{7,31},{8,0},{9,1... | collective-permute-start | bytes 393224 | tf_op jit(solution)/shard_map/ppermute | solution.py:34
  41.4 0.0 collective-permute-start.1
  41.4 9.5 %collective-permute-done.4.four_up = f32[128,256]{1,0:T(8,128)S(1)} collective-permute-done((f32[128,256]{1,0:T(8,128)S(1)}, f32[128,256]{1,0:T(8,128)S(1)}, u32[]{:S(2)}, u32[]{:S(2)}) %collective-permute-start.4) | collective-permute-done | bytes 131104 | tf_op jit(solution)/shard_map/ppermute | solution.py:34
  50.9 1.5 collective-permute-start.2
  52.4 0.0 collective-permute-done.6.four_down
  52.4 0.1 relay.1
  52.5 2.3 %collective-permute-start.7 = (f32[256,256]{1,0:T(8,128)S(1)}, f32[256,256]{1,0:T(8,128)S(1)}, u32[]{:S(2)}, u32[]{:S(2)}) collective-permute-start(f32[256,256]{1,0:T(8,128)S(1)} %get-tuple-element.48), channel_id=1, source_target_pairs={{0,8},{1,9},{2,10},{3,11},{4,12},{5,13},{6,14},{7,15},{8,16},{9,17... | collective-permute-start | bytes 786440 | tf_op jit(solution)/shard_map/ppermute | solution.py:34
  54.8 1.9 %collective-permute-start.8 = (f32[256,256]{1,0:T(8,128)S(1)}, f32[256,256]{1,0:T(8,128)S(1)}, u32[]{:S(2)}, u32[]{:S(2)}) collective-permute-start(f32[256,256]{1,0:T(8,128)S(1)} %get-tuple-element.49), channel_id=1, source_target_pairs={{0,24},{1,25},{2,26},{3,27},{4,28},{5,29},{6,30},{7,31},{8,0},{9,1... | collective-permute-start | bytes 786440 | tf_op jit(solution)/shard_map/ppermute | solution.py:34
  56.7 0.7 collective-permute-start.9
  57.4 0.0 collective-permute-done.1
  57.4 4.5 %collective-permute-done.2 = f32[256,256]{1,0:T(8,128)S(1)} collective-permute-done((f32[256,256]{1,0:T(8,128)S(1)}, f32[256,256]{1,0:T(8,128)S(1)}, u32[]{:S(2)}, u32[]{:S(2)}) %collective-permute-start.2) | collective-permute-done | bytes 262176 | tf_op jit(solution)/shard_map/ppermute | solution.py:34
  61.9 4.3 %collective-permute-done.7 = f32[256,256]{1,0:T(8,128)S(1)} collective-permute-done((f32[256,256]{1,0:T(8,128)S(1)}, f32[256,256]{1,0:T(8,128)S(1)}, u32[]{:S(2)}, u32[]{:S(2)}) %collective-permute-start.7) | collective-permute-done | bytes 262176 | tf_op jit(solution)/shard_map/ppermute | solution.py:34
  66.3 2.7 %collective-permute-done.8 = f32[256,256]{1,0:T(8,128)S(1)} collective-permute-done((f32[256,256]{1,0:T(8,128)S(1)}, f32[256,256]{1,0:T(8,128)S(1)}, u32[]{:S(2)}, u32[]{:S(2)}) %collective-permute-start.8) | collective-permute-done | bytes 262176 | tf_op jit(solution)/shard_map/ppermute | solution.py:34
  68.9 0.1 add_add_fusion.mine
  69.0 0.8 collective-permute-start.10
  69.8 6.3 %collective-permute-done.10.other = f32[256,256]{1,0:T(8,128)S(1)} collective-permute-done((f32[256,256]{1,0:T(8,128)S(1)}, f32[256,256]{1,0:T(8,128)S(1)}, u32[]{:S(2)}, u32[]{:S(2)}) %collective-permute-start.10) | collective-permute-done | bytes 262176 | tf_op jit(solution)/shard_map/ppermute | solution.py:358
  76.2 1.6 %middle.1 = (f32[128,256]{1,0:T(8,128)}, f32[256,256]{1,0:T(8,128)}, f32[256,256]{1,0:T(8,128)S(1)}) custom-call(s32[3]{0:T(128)S(1)} %pad_add_fusion.where, f32[256,256]{1,0:T(8,128)S(1)} %add_add_fusion.mine, f32[256,256]{1,0:T(8,128)S(1)} %collective-permute-done.10.other, f32[256,256]{1,0:T(8,128)S(1)} %copy-done.1, f32[1,256]{1,0:T(1,128)S(1)} %bitcast.12, ...), custom_call_target="tpu_custom_call" | custom-call | tf_op jit(solution)/shard_map/middle/pallas_call | solution.py:183
  77.8 2.9 %collective-permute-start.12 = (f32[256,256]{1,0:T(8,128)}, f32[256,256]{1,0:T(8,128)}, u32[]{:S(2)}, u32[]{:S(2)}) collective-permute-start(f32[256,256]{1,0:T(8,128)} %get-tuple-element.53.refs_0_.grad), channel_id=1, source_target_pairs={{0,24},{1,25},{2,26},{3,27},{4,28},{5,29},{6,30},{7,31},{8,0},{9,1... | collective-permute-start | bytes 786440 | tf_op jit(solution)/shard_map/ppermute | solution.py:34
  80.7 0.1 collective-permute-start.14
  80.7 1.2 collective-permute-start.11
  81.9 0.8 collective-permute-start.18
  82.7 2.0 %outer.1 = f32[8,40,256]{2,1,0:T(8,128)} custom-call(f32[256,256]{1,0:T(8,128)S(1)} %get-tuple-element.56.total, f32[256,256]{1,0:T(8,128)} %get-tuple-element.53.refs_0_.grad), custom_call_target="tpu_custom_call" | custom-call | tf_op jit(solution)/shard_map/outer/pallas_call | solution.py:206
  84.8 5.4 %all-to-all-start.1 = ((f32[8,40,256]{2,1,0:T(8,128)}), f32[8,40,256]{2,1,0:T(8,128)}, u32[]{:S(2)}, u32[]{:S(2)}) async-start(f32[8,40,256]{2,1,0:T(8,128)} %outer.1), calls=%async_computation.1 | async-start | bytes 655360 | tf_op jit(solution)/shard_map/all_to_all | solution.py:365
  90.2 0.0 collective-permute-done.12.two.refs_2_
  90.2 4.5 %collective-permute-start.13 = (f32[256,256]{1,0:T(8,128)}, f32[256,256]{1,0:T(8,128)}, u32[]{:S(2)}, u32[]{:S(2)}) collective-permute-start(f32[256,256]{1,0:T(8,128)} %collective-permute-done.12.two.refs_2_), channel_id=1, source_target_pairs={{0,28},{1,29},{2,30},{3,31},{4,0},{5,1},{6,2},{7,3},{8,4},{9,5},{1... | collective-permute-start | bytes 786440 | tf_op jit(solution)/shard_map/ppermute | solution.py:34
  94.7 0.6 collective-permute-done.14.six.refs_7_
  95.3 1.0 halves.1
  96.4 0.1 collective-permute-start.15
  96.5 1.1 collective-permute-done.11.refs_1_
  97.6 2.9 %collective-permute-start.16 = (f32[128,256]{1,0:T(8,128)S(1)}, f32[128,256]{1,0:T(8,128)S(1)}, u32[]{:S(2)}, u32[]{:S(2)}) collective-permute-start(f32[128,256]{1,0:T(8,128)S(1)} %get-tuple-element.55), channel_id=1, source_target_pairs={{0,24},{1,25},{2,26},{3,27},{4,28},{5,29},{6,30},{7,31},{8,0},{9,1... | collective-permute-start | bytes 393224 | tf_op jit(solution)/shard_map/ppermute | solution.py:34
  100.6 1.7 %spread.1 = f32[8,40,256]{2,1,0:T(8,128)} custom-call(f32[8,40,256]{2,1,0:T(8,128)} %all-to-all-done.1.parts), custom_call_target="tpu_custom_call" | custom-call | tf_op jit(solution)/shard_map/spread/pallas_call | solution.py:225
  102.3 4.1 %all-to-all-start.2 = ((f32[8,40,256]{2,1,0:T(8,128)}), f32[8,40,256]{2,1,0:T(8,128)}, u32[]{:S(2)}, u32[]{:S(2)}) async-start(f32[8,40,256]{2,1,0:T(8,128)} %spread.1), calls=%async_computation.2 | async-start | bytes 655360 | tf_op jit(solution)/shard_map/all_to_all | solution.py:366
  106.4 0.0 collective-permute-done.18.refs_8_
  106.4 8.3 %collective-permute-done.15.refs_4_ = f32[128,256]{1,0:T(8,128)S(1)} collective-permute-done((f32[128,256]{1,0:T(8,128)S(1)}, f32[128,256]{1,0:T(8,128)S(1)}, u32[]{:S(2)}, u32[]{:S(2)}) %collective-permute-start.15) | collective-permute-done | bytes 131104 | tf_op jit(solution)/shard_map/ppermute | solution.py:34
  114.7 0.0 collective-permute-done.16.refs_5_
  114.7 0.0 collective-permute-done.13.refs_3_
  114.7 0.0 collective-permute-done.17.refs_6_
  114.7 0.0 copy-start.6
  114.7 0.0 copy-start.8
  114.7 1.6 %join.1.own = f32[2048,256]{1,0:T(8,128)S(1)} custom-call(f32[256,256]{1,0:T(8,128)} %get-tuple-element.53.refs_0_.grad, f32[256,256]{1,0:T(8,128)} %collective-permute-done.11.refs_1_, f32[256,256]{1,0:T(8,128)} %collective-permute-done.12.two.refs_2_, f32[256,256]{1,0:T(8,128)} %collective-permute-done.13.refs_3_, ...), custom_call_target="tpu_custom_call" | custom-call | flops 999999995904 | tf_op jit(solution)/shard_map/join/pallas_call | solution.py:262
  116.3 1.3 all-to-all-done.2.parts
  117.6 1.0 total.1.piece
  118.6 0.1 collective-permute-start.19
  118.7 0.5 collective-permute-start.20
  119.2 3.7 %collective-permute-done.20.piece_other = f32[40,256]{1,0:T(8,128)S(1)} collective-permute-done((f32[40,256]{1,0:T(8,128)S(1)}, f32[40,256]{1,0:T(8,128)S(1)}, u32[]{:S(2)}, u32[]{:S(2)}) %collective-permute-start.20) | collective-permute-done | bytes 40992 | tf_op jit(solution)/shard_map/ppermute | solution.py:374
  122.9 1.6 %backward_tiles.1 = f32[8,168,256]{2,1,0:T(8,128)S(1)} custom-call(s32[12,2]{1,0:T(8,128)S(1)} %copy-done.6, s32[1]{0:T(128)} %bitcast.9.count, s32[3]{0:T(128)S(1)} %copy-done.8, f32[12,128,128]{2,1,0:T(8,128)S(1)} %bitcast.11, f32[2048,256]{1,0:T(8,128)S(1)} %join.1.own, f32[2048,256]{1,0:T(8,128)S(1)} %collective-permute-done.19.other, ...), custom_call_target="tpu_custom_call" | custom-call | tf_op jit(solution)/shard_map/backward_tiles/pallas_call | solution.py:305
  124.6 0.0 copy-start.2
  124.6 25.0 %all_to_all.20.parts = f32[8,168,256]{2,1,0:T(8,128)S(1)} all-to-all(f32[8,168,256]{2,1,0:T(8,128)S(1)} %backward_tiles.1), channel_id=1, replica_groups=mesh['row'=8,'col'=32] {'row'}, dimensions={0} | all-to-all | bytes 2752512 | tf_op jit(solution)/shard_map/all_to_all | solution.py:376
  149.6 1.0 final.1
  (22 shorter events, 0.0 us)
Async XLA Ops:
  0.6 24.2 %copy-start = (f32[1,1,12,128,128]{4,3,2,1,0:T(8,128)S(1)}, f32[1,1,12,128,128]{4,3,2,1,0:T(8,128)}, u32[]{:S(2)}) copy-start(f32[1,1,12,128,128]{4,3,2,1,0:T(8,128)} %param.10) | copy-start | bytes 2359300
  0.6 1.0 copy-start.3
  1.6 23.1 %copy-start.10 = (s32[1,1,12,2]{2,3,1,0:T(2,128)S(1)}, s32[1,1,12,2]{2,3,1,0:T(2,128)}, u32[]{:S(2)}) copy-start(s32[1,1,12,2]{2,3,1,0:T(2,128)} %param.11) | copy-start | bytes 292
  2.7 22.0 %all-to-all-start = ((f32[8,128,256]{2,1,0:T(8,128)}), f32[8,128,256]{2,1,0:T(8,128)S(1)}, u32[]{:S(2)}, u32[]{:S(2)}) async-start(f32[8,128,256]{2,1,0:T(8,128)} %broadcast_rows.1), calls=%async_computation | async-start | bytes 2097152 | tf_op jit(solution)/shard_map/all_to_all | solution.py:348
  24.8 6.4 %copy-start.5 = (s32[12,2]{1,0:T(8,128)}, s32[12,2]{1,0:T(8,128)S(1)}, u32[]{:S(2)}) copy-start(s32[12,2]{1,0:T(8,128)S(1)} %copy.11.place) | copy-start | bytes 292
  24.9 51.3 %copy-start.7 = (s32[3]{0:T(128)}, s32[3]{0:T(128)S(1)}, u32[]{:S(2)}) copy-start(s32[3]{0:T(128)S(1)} %pad_add_fusion.where) | copy-start | bytes 40
  26.8 4.2 %collective-permute-start = (f32[16,128,256]{2,1,0:T(8,128)S(1)}, f32[16,128,256]{2,1,0:T(8,128)S(1)}, u32[]{:S(2)}, u32[]{:S(2)}) collective-permute-start(f32[16,128,256]{2,1,0:T(8,128)S(1)} %get-tuple-element.38), channel_id=1, source_target_pairs={{0,1},{1,0},{2,3},{3,2},{4,5},{5,4},{6,7},{7,6},{8,9},{9,8},{10,11... | collective-permute-start | bytes 6291464 | tf_op jit(solution)/shard_map/ppermute | solution.py:356
  31.0 25.7 %copy-start.4 = (f32[128,256]{1,0:T(8,128)S(1)}, f32[128,256]{1,0:T(8,128)}, u32[]{:S(2)}) copy-start(f32[128,256]{1,0:T(8,128)} %cot_own.1) | copy-start | bytes 393220
  31.2 44.9 %copy-start.1 = (f32[256,256]{1,0:T(8,128)S(1)}, f32[256,256]{1,0:T(8,128)}, u32[]{:S(2)}) copy-start(f32[256,256]{1,0:T(8,128)} %weight.3) | copy-start | bytes 786436
  31.2 44.9 %copy-start.9 = (f32[256]{0:T(256)S(1)}, f32[256]{0:T(256)}, u32[]{:S(2)}) copy-start(f32[256]{0:T(256)} %param.9) | copy-start | bytes 3076
  31.3 21.2 %collective-permute-start.3 = (f32[256,256]{1,0:T(8,128)S(1)}, f32[256,256]{1,0:T(8,128)S(1)}, u32[]{:S(2)}, u32[]{:S(2)}) collective-permute-start(f32[256,256]{1,0:T(8,128)S(1)} %get-tuple-element.43), channel_id=1, source_target_pairs={{0,4},{1,5},{2,6},{3,7},{4,8},{5,9},{6,10},{7,11},{8,12},{9,13},{1... | collective-permute-start | bytes 786440 | tf_op jit(solution)/shard_map/ppermute | solution.py:34
  33.3 19.2 %collective-permute-start.5 = (f32[256,256]{1,0:T(8,128)S(1)}, f32[256,256]{1,0:T(8,128)S(1)}, u32[]{:S(2)}, u32[]{:S(2)}) collective-permute-start(f32[256,256]{1,0:T(8,128)S(1)} %get-tuple-element.46), channel_id=1, source_target_pairs={{0,28},{1,29},{2,30},{3,31},{4,0},{5,1},{6,2},{7,3},{8,4},{9,5},{1... | collective-permute-start | bytes 786440 | tf_op jit(solution)/shard_map/ppermute | solution.py:34
  37.3 13.7 %collective-permute-start.4 = (f32[128,256]{1,0:T(8,128)S(1)}, f32[128,256]{1,0:T(8,128)S(1)}, u32[]{:S(2)}, u32[]{:S(2)}) collective-permute-start(f32[128,256]{1,0:T(8,128)S(1)} %get-tuple-element.44), channel_id=1, source_target_pairs={{0,8},{1,9},{2,10},{3,11},{4,12},{5,13},{6,14},{7,15},{8,16},{9,17... | collective-permute-start | bytes 393224 | tf_op jit(solution)/shard_map/ppermute | solution.py:34
  37.3 15.1 %collective-permute-start.6 = (f32[128,256]{1,0:T(8,128)S(1)}, f32[128,256]{1,0:T(8,128)S(1)}, u32[]{:S(2)}, u32[]{:S(2)}) collective-permute-start(f32[128,256]{1,0:T(8,128)S(1)} %get-tuple-element.47), channel_id=1, source_target_pairs={{0,24},{1,25},{2,26},{3,27},{4,28},{5,29},{6,30},{7,31},{8,0},{9,1... | collective-permute-start | bytes 393224 | tf_op jit(solution)/shard_map/ppermute | solution.py:34
  41.4 16.0 %collective-permute-start.1 = (f32[256,256]{1,0:T(8,128)S(1)}, f32[256,256]{1,0:T(8,128)S(1)}, u32[]{:S(2)}, u32[]{:S(2)}) collective-permute-start(f32[256,256]{1,0:T(8,128)S(1)} %get-tuple-element.40), channel_id=1, source_target_pairs={{0,4},{1,5},{2,6},{3,7},{4,8},{5,9},{6,10},{7,11},{8,12},{9,13},{1... | collective-permute-start | bytes 786440 | tf_op jit(solution)/shard_map/ppermute | solution.py:34
  50.9 11.0 %collective-permute-start.2 = (f32[256,256]{1,0:T(8,128)S(1)}, f32[256,256]{1,0:T(8,128)S(1)}, u32[]{:S(2)}, u32[]{:S(2)}) collective-permute-start(f32[256,256]{1,0:T(8,128)S(1)} %get-tuple-element.41), channel_id=1, source_target_pairs={{0,28},{1,29},{2,30},{3,31},{4,0},{5,1},{6,2},{7,3},{8,4},{9,5},{1... | collective-permute-start | bytes 786440 | tf_op jit(solution)/shard_map/ppermute | solution.py:34
  52.5 13.8 %collective-permute-start.7 = (f32[256,256]{1,0:T(8,128)S(1)}, f32[256,256]{1,0:T(8,128)S(1)}, u32[]{:S(2)}, u32[]{:S(2)}) collective-permute-start(f32[256,256]{1,0:T(8,128)S(1)} %get-tuple-element.48), channel_id=1, source_target_pairs={{0,8},{1,9},{2,10},{3,11},{4,12},{5,13},{6,14},{7,15},{8,16},{9,17... | collective-permute-start | bytes 786440 | tf_op jit(solution)/shard_map/ppermute | solution.py:34
  54.8 14.2 %collective-permute-start.8 = (f32[256,256]{1,0:T(8,128)S(1)}, f32[256,256]{1,0:T(8,128)S(1)}, u32[]{:S(2)}, u32[]{:S(2)}) collective-permute-start(f32[256,256]{1,0:T(8,128)S(1)} %get-tuple-element.49), channel_id=1, source_target_pairs={{0,24},{1,25},{2,26},{3,27},{4,28},{5,29},{6,30},{7,31},{8,0},{9,1... | collective-permute-start | bytes 786440 | tf_op jit(solution)/shard_map/ppermute | solution.py:34
  56.7 12.3 %collective-permute-start.9 = (f32[128,256]{1,0:T(8,128)S(1)}, f32[128,256]{1,0:T(8,128)S(1)}, u32[]{:S(2)}, u32[]{:S(2)}) collective-permute-start(f32[128,256]{1,0:T(8,128)S(1)} %copy-done.4), channel_id=1, source_target_pairs={{0,2},{1,3},{2,0},{3,1},{4,6},{5,7},{6,4},{7,5},{8,10},{9,11},{10,... | collective-permute-start | bytes 393224 | tf_op jit(solution)/shard_map/ppermute | solution.py:355
  69.0 7.1 %collective-permute-start.10 = (f32[256,256]{1,0:T(8,128)S(1)}, f32[256,256]{1,0:T(8,128)S(1)}, u32[]{:S(2)}, u32[]{:S(2)}) collective-permute-start(f32[256,256]{1,0:T(8,128)S(1)} %add_add_fusion.mine), channel_id=1, source_target_pairs={{0,2},{1,3},{2,0},{3,1},{4,6},{5,7},{6,4},{7,5},{8,10},{9,11},{10,... | collective-permute-start | bytes 786440 | tf_op jit(solution)/shard_map/ppermute | solution.py:358
  77.8 12.4 %collective-permute-start.12 = (f32[256,256]{1,0:T(8,128)}, f32[256,256]{1,0:T(8,128)}, u32[]{:S(2)}, u32[]{:S(2)}) collective-permute-start(f32[256,256]{1,0:T(8,128)} %get-tuple-element.53.refs_0_.grad), channel_id=1, source_target_pairs={{0,24},{1,25},{2,26},{3,27},{4,28},{5,29},{6,30},{7,31},{8,0},{9,1... | collective-permute-start | bytes 786440 | tf_op jit(solution)/shard_map/ppermute | solution.py:34
  80.7 14.6 %collective-permute-start.14 = (f32[256,256]{1,0:T(8,128)}, f32[256,256]{1,0:T(8,128)}, u32[]{:S(2)}, u32[]{:S(2)}) collective-permute-start(f32[256,256]{1,0:T(8,128)} %get-tuple-element.53.refs_0_.grad), channel_id=1, source_target_pairs={{0,8},{1,9},{2,10},{3,11},{4,12},{5,13},{6,14},{7,15},{8,16},{9,17... | collective-permute-start | bytes 786440 | tf_op jit(solution)/shard_map/ppermute | solution.py:34
  80.7 16.9 %collective-permute-start.11 = (f32[256,256]{1,0:T(8,128)}, f32[256,256]{1,0:T(8,128)}, u32[]{:S(2)}, u32[]{:S(2)}) collective-permute-start(f32[256,256]{1,0:T(8,128)} %get-tuple-element.53.refs_0_.grad), channel_id=1, source_target_pairs={{0,28},{1,29},{2,30},{3,31},{4,0},{5,1},{6,2},{7,3},{8,4},{9,5},{1... | collective-permute-start | bytes 786440 | tf_op jit(solution)/shard_map/ppermute | solution.py:34
  81.9 24.5 %collective-permute-start.18 = (f32[256,256]{1,0:T(8,128)}, f32[256,256]{1,0:T(8,128)}, u32[]{:S(2)}, u32[]{:S(2)}) collective-permute-start(f32[256,256]{1,0:T(8,128)} %get-tuple-element.53.refs_0_.grad), channel_id=1, source_target_pairs={{0,4},{1,5},{2,6},{3,7},{4,8},{5,9},{6,10},{7,11},{8,12},{9,13},{1... | collective-permute-start | bytes 786440 | tf_op jit(solution)/shard_map/ppermute | solution.py:34
  84.8 15.8 %all-to-all-start.1 = ((f32[8,40,256]{2,1,0:T(8,128)}), f32[8,40,256]{2,1,0:T(8,128)}, u32[]{:S(2)}, u32[]{:S(2)}) async-start(f32[8,40,256]{2,1,0:T(8,128)} %outer.1), calls=%async_computation.1 | async-start | bytes 655360 | tf_op jit(solution)/shard_map/all_to_all | solution.py:365
  90.2 24.5 %collective-permute-start.13 = (f32[256,256]{1,0:T(8,128)}, f32[256,256]{1,0:T(8,128)}, u32[]{:S(2)}, u32[]{:S(2)}) collective-permute-start(f32[256,256]{1,0:T(8,128)} %collective-permute-done.12.two.refs_2_), channel_id=1, source_target_pairs={{0,28},{1,29},{2,30},{3,31},{4,0},{5,1},{6,2},{7,3},{8,4},{9,5},{1... | collective-permute-start | bytes 786440 | tf_op jit(solution)/shard_map/ppermute | solution.py:34
  95.3 19.4 %collective-permute-start.17 = (f32[256,256]{1,0:T(8,128)}, f32[256,256]{1,0:T(8,128)}, u32[]{:S(2)}, u32[]{:S(2)}) collective-permute-start(f32[256,256]{1,0:T(8,128)} %collective-permute-done.14.six.refs_7_), channel_id=1, source_target_pairs={{0,4},{1,5},{2,6},{3,7},{4,8},{5,9},{6,10},{7,11},{8,12},{9,13},{1... | collective-permute-start | bytes 786440 | tf_op jit(solution)/shard_map/ppermute | solution.py:34
  96.4 18.4 %collective-permute-start.15 = (f32[128,256]{1,0:T(8,128)S(1)}, f32[128,256]{1,0:T(8,128)S(1)}, u32[]{:S(2)}, u32[]{:S(2)}) collective-permute-start(f32[128,256]{1,0:T(8,128)S(1)} %get-tuple-element.54), channel_id=1, source_target_pairs={{0,8},{1,9},{2,10},{3,11},{4,12},{5,13},{6,14},{7,15},{8,16},{9,17... | collective-permute-start | bytes 393224 | tf_op jit(solution)/shard_map/ppermute | solution.py:34
  97.6 17.1 %collective-permute-start.16 = (f32[128,256]{1,0:T(8,128)S(1)}, f32[128,256]{1,0:T(8,128)S(1)}, u32[]{:S(2)}, u32[]{:S(2)}) collective-permute-start(f32[128,256]{1,0:T(8,128)S(1)} %get-tuple-element.55), channel_id=1, source_target_pairs={{0,24},{1,25},{2,26},{3,27},{4,28},{5,29},{6,30},{7,31},{8,0},{9,1... | collective-permute-start | bytes 393224 | tf_op jit(solution)/shard_map/ppermute | solution.py:34
  102.3 15.3 %all-to-all-start.2 = ((f32[8,40,256]{2,1,0:T(8,128)}), f32[8,40,256]{2,1,0:T(8,128)}, u32[]{:S(2)}, u32[]{:S(2)}) async-start(f32[8,40,256]{2,1,0:T(8,128)} %spread.1), calls=%async_computation.2 | async-start | bytes 655360 | tf_op jit(solution)/shard_map/all_to_all | solution.py:366
  114.7 8.2 %copy-start.6 = (s32[12,2]{1,0:T(8,128)S(1)}, s32[12,2]{1,0:T(8,128)}, u32[]{:S(2)}) copy-start(s32[12,2]{1,0:T(8,128)} %copy-done.5) | copy-start | bytes 292
  114.7 8.2 %copy-start.8 = (s32[3]{0:T(128)S(1)}, s32[3]{0:T(128)}, u32[]{:S(2)}) copy-start(s32[3]{0:T(128)} %copy-done.7) | copy-start | bytes 40
  118.6 4.3 %collective-permute-start.19 = (f32[2048,256]{1,0:T(8,128)S(1)}, f32[2048,256]{1,0:T(8,128)S(1)}, u32[]{:S(2)}, u32[]{:S(2)}) collective-permute-start(f32[2048,256]{1,0:T(8,128)S(1)} %join.1.own), channel_id=1, source_target_pairs={{0,1},{1,0},{2,3},{3,2},{4,5},{5,4},{6,7},{7,6},{8,9},{9,8},{10,11... | collective-permute-start | bytes 6291464 | tf_op jit(solution)/shard_map/ppermute | solution.py:373
  118.7 4.2 %collective-permute-start.20 = (f32[40,256]{1,0:T(8,128)S(1)}, f32[40,256]{1,0:T(8,128)S(1)}, u32[]{:S(2)}, u32[]{:S(2)}) collective-permute-start(f32[40,256]{1,0:T(8,128)S(1)} %total.1.piece), channel_id=1, source_target_pairs={{0,1},{1,0},{2,3},{3,2},{4,5},{5,4},{6,7},{7,6},{8,9},{9,8},{10,11... | collective-permute-start | bytes 122888 | tf_op jit(solution)/shard_map/ppermute | solution.py:374
  124.6 25.0 %copy-start.2 = (f32[256,256]{1,0:T(8,128)S(1)}, f32[256,256]{1,0:T(8,128)}, u32[]{:S(2)}) copy-start(f32[256,256]{1,0:T(8,128)} %weight.3) | copy-start | bytes 786436

commit v4 on v3

--- a/solution.py
+++ b/solution.py
@@ -9,10 +9,15 @@
 from jax.sharding import PartitionSpec as P
 
 Z, YL = 8, 2
+X, YH = 4, 2
 TILE = 128
 PAIR = YL * TILE
 JOIN_COST = 10**12
 HALVES_COST = 10**12
+ROWS_COST = 10**12
+UNPACK_COST = 10**10
+SUMS_COST = 10**10
+JOIN_PARTS = 4
 
 
 def col_pairs(move):
@@ -34,6 +39,23 @@
     return lax.ppermute(value, "col", col_pairs(lambda z, y, core: ((z + distance) % Z, y, core)))
 
 
+def row_pairs(move):
+    pairs = []
+    for x in range(X):
+        for h in range(YH):
+            a, b = move(x, h)
+            pairs.append((x * YH + h, (a % X) * YH + b))
+    return pairs
+
+
+def x_shift(value, distance):
+    return lax.ppermute(value, "row", row_pairs(lambda x, h: (x + distance, h)))
+
+
+def h_swap(value):
+    return lax.ppermute(value, "row", row_pairs(lambda x, h: (x, 1 - h)))
+
+
 SMEM = pl.BlockSpec(memory_space=pltpu.SMEM)
 VMEM = pl.BlockSpec(memory_space=pltpu.VMEM)
 
@@ -65,29 +87,38 @@
     return mine, distance, lax.rem(lax.div(tile, 2), YL)
 
 
-def broadcast_kernel(block, out):
-    for j in range(out.shape[0]):
-        out[j] = block[...]
-
-
-def broadcast(block, copies):
-    return pl.pallas_call(
-        broadcast_kernel,
-        out_shape=shaped(copies, *block.shape),
-        in_specs=[VMEM],
-        out_specs=VMEM,
+def halve_kernel(*refs):
+    count = len(refs) - 2
+    for j in range(count):
+        refs[count][j], refs[count + 1][j] = split(refs[j][...])
+
+
+def halve(*blocks):
+    shape = jax.ShapeDtypeStruct((len(blocks),) + blocks[0].shape, jnp.bfloat16)
+    return pl.pallas_call(
+        halve_kernel,
+        out_shape=(shape, shape),
+        in_specs=[VMEM] * len(blocks),
+        out_specs=(VMEM,) * 2,
         compiler_params=params(3),
-        name="broadcast_rows",
-    )(block)
-
-
-def forward_kernel(place, count, where, values, features, keep, send, high, low):
+        cost_estimate=pl.CostEstimate(flops=ROWS_COST, bytes_accessed=0, transcendentals=0),
+        name="halve",
+    )(*blocks)
+
+
+def row_index(tile, where):
+    across = lax.rem(lax.rem(tile, YH) + where[4], YH)
+    return across * X + lax.rem(lax.div(tile, YH) - where[3] + X, X)
+
+
+def forward_kernel(place, count, where, values, near_high, near_low, a, b, c, d, keep, send, high, low):
     keep[...] = jnp.zeros_like(keep)
     send[...] = jnp.zeros_like(send)
-    for j in range(features.shape[0]):
-        high[j], low[j] = split(features[j])
+    for j, part in enumerate((a, b, c, d)):
+        high[j], low[j] = near_high[j], near_low[j]
+        high[X + j], low[X + j] = split(part[...])
     for k in range(values.shape[0]):
-        col = place[k, 1]
+        col = row_index(place[k, 1], where)
         mine, distance, y = locate(place[k, 0], where)
         live = k < count[0]
         product = dot3(split(values[k]), (high[col], low[col]), ((1,), (0,)))
@@ -96,21 +127,19 @@
         send[index] += jnp.where(live & ~mine, product, 0.0)
 
 
-def forward(place, count, where, values, features):
+def forward(place, count, where, values, near, far):
     tiles = Z * YL
-    width = features.shape[-1]
+    width = far[0].shape[-1]
+    parts = pltpu.VMEM((X * YH, TILE, width), jnp.bfloat16)
     return pl.pallas_call(
         forward_kernel,
         out_shape=(shaped(tiles, TILE, width),) * 2,
-        in_specs=[SMEM, SMEM, SMEM, VMEM, VMEM],
+        in_specs=[SMEM, SMEM, SMEM] + [VMEM] * 7,
         out_specs=(VMEM,) * 2,
-        scratch_shapes=[
-            pltpu.VMEM(features.shape, jnp.bfloat16),
-            pltpu.VMEM(features.shape, jnp.bfloat16),
-        ],
+        scratch_shapes=[parts, parts],
         compiler_params=params(12),
         name="forward_tiles",
-    )(place, count, where, values, features)
+    )(place, count, where, values, *near, *far)
 
 
 def add_cores_kernel(first, second, own, one, two, three, four_up, four_down, five, six, seven):
@@ -250,20 +279,21 @@
 
 
 def join_kernel(*refs):
-    out = refs[-1]
-    start = 0
-    for part in refs[:-1]:
-        out[start : start + part.shape[0], :] = part[...]
-        start += part.shape[0]
+    parts, outs = refs[:-JOIN_PARTS], refs[-JOIN_PARTS:]
+    rows, start = outs[0].shape[0], 0
+    for part in parts:
+        size = part.shape[0]
+        outs[start // rows][start % rows : start % rows + size, :] = part[...]
+        start += size
 
 
 def join(*blocks):
     rows, width = sum(block.shape[0] for block in blocks), blocks[0].shape[1]
     return pl.pallas_call(
         join_kernel,
-        out_shape=shaped(rows, width),
+        out_shape=(shaped(rows // JOIN_PARTS, width),) * JOIN_PARTS,
         in_specs=[VMEM] * len(blocks),
-        out_specs=VMEM,
+        out_specs=(VMEM,) * JOIN_PARTS,
         compiler_params=params(8),
         cost_estimate=pl.CostEstimate(flops=JOIN_COST, bytes_accessed=0, transcendentals=0),
         name="join",
@@ -288,54 +318,116 @@
     )(parts)
 
 
-def backward_kernel(place, count, where, values, own, other, piece, piece_other, back):
-    back[...] = jnp.zeros_like(back)
+def backward_kernel(place, count, where, values, *refs):
+    own, other = refs[:JOIN_PARTS], refs[JOIN_PARTS : 2 * JOIN_PARTS]
+    outs, total = refs[2 * JOIN_PARTS : -1], refs[-1]
+    total[...] = jnp.zeros_like(total)
+    tiles = own[0].shape[0] // TILE
     for k in range(values.shape[0]):
         mine, distance, y = locate(place[k, 0], where)
-        rows = pl.ds(pl.multiple_of((distance * YL + y) * TILE, TILE), TILE)
-        block = jnp.where(mine, own[rows, :], other[rows, :])
+        index = distance * YL + y
+        rows = pl.ds(pl.multiple_of(lax.rem(index, tiles) * TILE, TILE), TILE)
+        block = jnp.where(mine, own[0][rows, :], other[0][rows, :])
+        for j in range(1, JOIN_PARTS):
+            later = jnp.where(mine, own[j][rows, :], other[j][rows, :])
+            block = jnp.where(index >= j * tiles, later, block)
         product = dot3(split(values[k]), split(block), ((0,), (0,)))
-        back[place[k, 1], :TILE, :] += jnp.where(k < count[0], product, 0.0)
-    both = piece[...] + piece_other[...]
-    for j in range(back.shape[0]):
-        back[j, TILE:, :] = both
-
-
-def backward(place, count, where, values, own, other, piece, piece_other, tiles):
+        total[row_index(place[k, 1], where)] += jnp.where(k < count[0], product, 0.0)
+    for j, out in enumerate(outs):
+        out[...] = total[j]
+
+
+def backward(place, count, where, values, own, other):
+    width = own[0].shape[1]
     return pl.pallas_call(
         backward_kernel,
-        out_shape=shaped(tiles, TILE + piece.shape[0], own.shape[1]),
-        in_specs=[SMEM] * 3 + [VMEM] * 5,
-        out_specs=VMEM,
+        out_shape=(shaped(TILE, width),) * (X * YH),
+        in_specs=[SMEM] * 3 + [VMEM] * (1 + 2 * JOIN_PARTS),
+        out_specs=(VMEM,) * (X * YH),
+        scratch_shapes=[pltpu.VMEM((X * YH, TILE, width), jnp.float32)],
         compiler_params=params(12),
         name="backward_tiles",
-    )(place, count, where, values, own, other, piece, piece_other)
-
-
-def final_kernel(parts, weight, result, weight_grad, bias_grad):
-    back = parts[0, :TILE, :]
-    for j in range(1, parts.shape[0]):
-        back = back + parts[j, :TILE, :]
-    result[...] = dot3(split(back), split(weight[...]), ((1,), (1,)))
-    rows = parts.shape[1] - TILE - 8
-    for j in range(parts.shape[0]):
-        weight_grad[j * rows : (j + 1) * rows, :] = parts[j, TILE : TILE + rows, :]
-    bias_grad[...] = parts[0, TILE + rows : TILE + rows + 1, :]
-
-
-def final(parts, weight):
-    return pl.pallas_call(
-        final_kernel,
-        out_shape=(
-            shaped(TILE, weight.shape[0]),
-            shaped(*weight.shape),
-            shaped(1, weight.shape[1]),
-        ),
-        in_specs=[VMEM, VMEM],
+    )(place, count, where, values, *own, *other)
+
+
+def pack_kernel(one, two, three, piece, piece_across, *outs):
+    rows = piece.shape[0]
+    for part, out in zip((one, two, three), outs):
+        out[:TILE, :] = part[...]
+        out[TILE : TILE + rows, :] = piece[...]
+        out[TILE + rows :, :] = piece_across[...]
+
+
+def pack(one, two, three, piece, piece_across):
+    rows, width = one.shape[0] + 2 * piece.shape[0], one.shape[1]
+    return pl.pallas_call(
+        pack_kernel,
+        out_shape=(shaped(rows, width),) * 3,
+        in_specs=[VMEM] * 5,
+        out_specs=(VMEM,) * 3,
+        compiler_params=params(4),
+        name="pack",
+    )(one, two, three, piece, piece_across)
+
+
+def gather_sums_kernel(cross, one, two, three, out):
+    out[...] = (cross[...] + one[...]) + (two[...] + three[...])
+
+
+def gather_sums(*parts):
+    return pl.pallas_call(
+        gather_sums_kernel,
+        out_shape=shaped(*parts[0].shape),
+        in_specs=[VMEM] * 4,
+        out_specs=VMEM,
+        compiler_params=params(3),
+        cost_estimate=pl.CostEstimate(flops=SUMS_COST, bytes_accessed=0, transcendentals=0),
+        name="gather_sums",
+    )(*parts)
+
+
+def unpack_kernel(where, home, one, two, three, piece, piece_across, back, weight_grad, bias_grad):
+    back[...] = (home[...] + one[:TILE, :]) + (two[:TILE, :] + three[:TILE, :])
+    rows = weight_grad.shape[0] // (X * YH)
+    step = rows + 8
+    for distance, source in enumerate((None, three, two, one)):
+        x = lax.rem(where[3] + distance, X)
+        for across in range(YH):
+            if source is None:
+                value = (piece, piece_across)[across][:rows, :]
+            else:
+                start = TILE + across * step
+                value = source[start : start + rows, :]
+            index = x * YH + lax.rem(where[4] + across, YH)
+            weight_grad[pl.ds(pl.multiple_of(index * rows, rows), rows), :] = value
+    bias_grad[...] = piece[rows : rows + 1, :]
+
+
+def unpack(where, home, one, two, three, piece, piece_across, shape):
+    return pl.pallas_call(
+        unpack_kernel,
+        out_shape=(shaped(*home.shape), shaped(*shape), shaped(1, shape[1])),
+        in_specs=[SMEM] + [VMEM] * 6,
         out_specs=(VMEM,) * 3,
         compiler_params=params(5),
+        cost_estimate=pl.CostEstimate(flops=UNPACK_COST, bytes_accessed=0, transcendentals=0),
+        name="unpack",
+    )(where, home, one, two, three, piece, piece_across)
+
+
+def final_kernel(back, partner, weight, result):
+    result[...] = dot3(split(back[...] + partner[...]), split(weight[...]), ((1,), (1,)))
+
+
+def final(back, partner, weight):
+    return pl.pallas_call(
+        final_kernel,
+        out_shape=shaped(TILE, weight.shape[0]),
+        in_specs=[VMEM] * 3,
+        out_specs=VMEM,
+        compiler_params=params(3),
         name="final",
-    )(parts, weight)
+    )(back, partner, weight)
 
 
 def body(node_features, weight, bias, tile_values, tile_coords, tile_count, cotangent):
@@ -345,13 +437,27 @@
     col_count = lax.axis_size("col")
     factor = 1.0 / math.sqrt(local_nodes * row_count * col_count)
 
-    features = lax.all_to_all(broadcast(node_features, row_count), "row", 0, 0)
-    features, tile_coords, tile_count, col = lax.optimization_barrier(
-        (features, tile_coords, tile_count, lax.axis_index("col"))
+    place, count = tile_coords[0, 0], tile_count.reshape(1)
+    row, col = lax.axis_index("row"), lax.axis_index("col")
+    where = jnp.stack(
+        [
+            lax.div(col, 2 * YL),
+            lax.rem(lax.div(col, 2), YL),
+            lax.rem(col, 2),
+            lax.div(row, YH),
+            lax.rem(row, YH),
+        ]
     )
-    place, count = tile_coords[0, 0], tile_count.reshape(1)
-    where = jnp.stack([lax.div(col, 2 * YL), lax.rem(lax.div(col, 2), YL), lax.rem(col, 2)])
-    keep, send = forward(place, count, where, values, features)
+
+    partner = h_swap(node_features)
+    near = halve(
+        node_features,
+        x_shift(node_features, -1),
+        x_shift(node_features, 2),
+        x_shift(node_features, 1),
+    )
+    far = (partner, x_shift(partner, -1), x_shift(partner, 2), x_shift(partner, 1))
+    keep, send = forward(place, count, where, values, near, far)
     cot_other = lax.ppermute(cotangent, "col", Y_SWAP)
     summed = scatter_z(*add_cores(keep, lax.ppermute(send, "col", CORE_SWAP)))
     summed, cot_other = lax.optimization_barrier((summed, cot_other))
@@ -368,13 +474,16 @@
     low, high = halves(two, six)
     low, high = z_shift(low, 2), z_shift(high, -2)
     own = join(grads, one, two, three, low, high, five, six, seven)
+    other = [lax.ppermute(part, "col", CORE_SWAP) for part in own]
     piece = total_of(parts, factor)
-    own, piece = lax.optimization_barrier((own, piece))
-    other = lax.ppermute(own, "col", CORE_SWAP)
-    piece_other = lax.ppermute(piece, "col", CORE_SWAP)
-    back = backward(place, count, where, values, own, other, piece, piece_other, row_count)
-    parts = lax.all_to_all(back, "row", 0, 0)
-    input_grad, weight_grad, bias_grad = final(parts, weight)
+    piece = piece + lax.ppermute(piece, "col", CORE_SWAP)
+    piece_across = h_swap(piece)
+    home, *near, cross, one, two, three = backward(place, count, where, values, own, other)
+    near = pack(*near, piece, piece_across)
+    sums = gather_sums(cross, x_shift(one, 1), x_shift(two, 2), x_shift(three, -1))
+    near = [x_shift(part, distance) for part, distance in zip(near, (1, 2, -1))]
+    back, weight_grad, bias_grad = unpack(where, home, *near, piece, piece_across, weight.shape)
+    input_grad = final(back, h_swap(sums), weight)
     return (output, input_grad, weight_grad, bias_grad.reshape(width))
 
 

time: 152 us -> 140 us (0.921)
  blocking collectives: 25 us -> 0 us
  starting transfers between devices: 47.4 us -> 66.7 us
  waiting for transfers between devices: 60.6 us -> 53 us
    all_to_all x1 -> x0, blocking collectives: 25 us -> none  [body(): parts = lax.all_to_all(back, 'row', 0, 0)]
    ppermute x2 -> x20, starting transfers between devices: 0.59 us -> 24.3 us  [the longest x12 18 us: x_shift(): return lax.ppermute(value, 'row', row_pairs(lambda x, h: (x + distance, h)))]
    ppermute x2 -> x20, waiting for transfers between devices: 3.71 us -> 21.5 us  [the longest x12 12.5 us: x_shift(): return lax.ppermute(value, 'row', row_pairs(lambda x, h: (x + distance, h)))]
    all_to_all x1 -> x0, waiting for transfers between devices: 13.9 us -> none  [body(): features = lax.all_to_all(broadcast(node_features, row_count), 'row', 0, 0)]
    ppermute x16, waiting for transfers between devices: 31.1 us -> 21.4 us  [z_shift(): lax.ppermute(value, 'col', col_pairs(lambda z, y, core: ((z + distance) %...]
    all_to_all x1 -> x0, starting transfers between devices: 7.46 us -> none  [body(): features = lax.all_to_all(broadcast(node_features, row_count), 'row', 0, 0)]
    pallas_call x4 -> x7, Pallas kernels: 5.23 us -> 6.08 us  [the longest x1 2.07 us: backward(): pl.pallas_call(backward_kernel, out_shape=(shaped(TILE, width),) * (X * Y...]
  transfers between devices with their start and end apart: 24 -> 41, of which waited for: 12 -> 17; matrix products, arithmetic and copies ran while one was open for 0% -> 1% of each run, Pallas kernels for 4% -> 8%
where the time goes in v4:
time: 140 us; the launch traced here: 139 us
  starting transfers between devices  66.7 us (48%)
  waiting for transfers between devices  53 us (38%)
  Pallas kernels  16.3 us (12%)
  local copies, waits for them, and re-layouts  1.81 us (1%)
  between operations  1.47 us (1%)
    ppermute x16, starting transfers between devices, z_shift(): lax.ppermute(value, 'col', col_pairs(lambda z, y, core: ((z + distance) %...  29.4 us
    ppermute x16, waiting for transfers between devices, z_shift(): lax.ppermute(value, 'col', col_pairs(lambda z, y, core: ((z + distance) %...  21.4 us
    ppermute x12, starting transfers between devices, x_shift(): return lax.ppermute(value, 'row', row_pairs(lambda x, h: (x + distance, h)))  18 us
    ppermute x12, waiting for transfers between devices, x_shift(): return lax.ppermute(value, 'row', row_pairs(lambda x, h: (x + distance, h)))  12.5 us
    all_to_all x1, starting transfers between devices, body(): parts = lax.all_to_all(outer(total, grads, row_count), 'row', 0, 0)  6.64 us
    ppermute x1, waiting for transfers between devices, body(): summed_other = lax.ppermute(summed, 'col', Y_SWAP)  5.92 us
    ppermute x3, starting transfers between devices, h_swap(): return lax.ppermute(value, 'row', row_pairs(lambda x, h: (x, 1 - h)))  5.17 us
    all_to_all x1, starting transfers between devices, body(): lax.all_to_all(spread(parts, Z), 'col', 0, 0, axis_index_groups=Z_GROUPS)  4.79 us
  transfers between devices with their start and end apart: 41, of which 17 were waited for; matrix products, arithmetic and copies ran while one was open for 1% of the time, Pallas kernels for 8%

profile of v4, /device:TPU:2, one launch (start us, length us, event | category | flops | bytes accessed | tf_op | source)
XLA Modules:
  0.0 139.3 jit_solution(9931833474282255954)
XLA Ops:
  0.6 3.3 %collective-permute-start.3 = (f32[128,256]{1,0:T(8,128)}, f32[128,256]{1,0:T(8,128)}, u32[]{:S(2)}, u32[]{:S(2)}) collective-permute-start(f32[128,256]{1,0:T(8,128)} %refs_0_.1), channel_id=1, source_target_pairs={{0,32},{32,0},{64,96},{96,64},{128,160},{160,128},{192,224},{224,1... | collective-permute-start | bytes 393224 | tf_op jit(solution)/shard_map/ppermute | solution.py:56
  3.9 0.5 collective-permute-start
  4.4 2.4 %collective-permute-start.1 = (f32[128,256]{1,0:T(8,128)}, f32[128,256]{1,0:T(8,128)S(1)}, u32[]{:S(2)}, u32[]{:S(2)}) collective-permute-start(f32[128,256]{1,0:T(8,128)} %refs_0_.1), channel_id=1, source_target_pairs={{0,128},{32,160},{64,192},{96,224},{128,0},{160,32},{192,64},{224,... | collective-permute-start | bytes 393224 | tf_op jit(solution)/shard_map/ppermute | solution.py:52
  6.9 1.8 %collective-permute-start.2 = (f32[128,256]{1,0:T(8,128)}, f32[128,256]{1,0:T(8,128)S(1)}, u32[]{:S(2)}, u32[]{:S(2)}) collective-permute-start(f32[128,256]{1,0:T(8,128)} %refs_0_.1), channel_id=1, source_target_pairs={{0,64},{32,96},{64,128},{96,160},{128,192},{160,224},{192,0},{224,... | collective-permute-start | bytes 393224 | tf_op jit(solution)/shard_map/ppermute | solution.py:52
  8.7 0.8 copy.11.place
  10.2 0.3 collective-permute-start.4
  10.5 1.3 collective-permute-start.5
  11.8 2.5 %collective-permute-start.6 = (f32[128,256]{1,0:T(8,128)}, f32[128,256]{1,0:T(8,128)}, u32[]{:S(2)}, u32[]{:S(2)}) collective-permute-start(f32[128,256]{1,0:T(8,128)} %collective-permute-done.3.a), channel_id=1, source_target_pairs={{0,64},{32,96},{64,128},{96,160},{128,192},{160,224},{192,0},{224,... | collective-permute-start | bytes 393224 | tf_op jit(solution)/shard_map/ppermute | solution.py:52
  14.3 0.9 copy-done.10
  15.3 3.4 %collective-permute-done.4.b = f32[128,256]{1,0:T(8,128)} collective-permute-done((f32[128,256]{1,0:T(8,128)}, f32[128,256]{1,0:T(8,128)}, u32[]{:S(2)}, u32[]{:S(2)}) %collective-permute-start.4) | collective-permute-done | bytes 131104 | tf_op jit(solution)/shard_map/ppermute | solution.py:52
  18.6 0.8 collective-permute-done.6.d
  19.4 2.4 %forward_tiles.1 = (f32[16,128,256]{2,1,0:T(8,128)S(1)}, f32[16,128,256]{2,1,0:T(8,128)S(1)}) custom-call(s32[12,2]{1,0:T(8,128)S(1)} %copy.11.place, s32[1]{0:T(128)} %bitcast.10.count, s32[5]{0:T(128)S(1)} %stack.23.where, f32[12,128,128]{2,1,0:T(8,128)S(1)} %bitcast.12, bf16[4,128,256]{2,1,0:T(8,128)(2,1)S(1)} %get-tuple-element.44.near_high, ...), custom_call_target="tpu_custom_call" | custom-call | tf_op jit(solution)/shard_map/forward_tiles/pallas_call | solution.py:134
  21.9 4.1 %collective-permute-done.7.second = f32[16,128,256]{2,1,0:T(8,128)S(1)} collective-permute-done((f32[16,128,256]{2,1,0:T(8,128)S(1)}, f32[16,128,256]{2,1,0:T(8,128)S(1)}, u32[]{:S(2)}, u32[]{:S(2)}) %collective-permute-start.7) | collective-permute-done | bytes 2097184 | tf_op jit(solution)/shard_map/ppermute | solution.py:462
  26.1 0.3 add_cores.1
  26.4 2.0 %collective-permute-start.10 = (f32[256,256]{1,0:T(8,128)S(1)}, f32[256,256]{1,0:T(8,128)S(1)}, u32[]{:S(2)}, u32[]{:S(2)}) collective-permute-start(f32[256,256]{1,0:T(8,128)S(1)} %get-tuple-element.52), channel_id=1, source_target_pairs={{0,4},{1,5},{2,6},{3,7},{4,8},{5,9},{6,10},{7,11},{8,12},{9,13},{1... | collective-permute-start | bytes 786440 | tf_op jit(solution)/shard_map/ppermute | solution.py:39
  28.4 4.0 %collective-permute-start.12 = (f32[256,256]{1,0:T(8,128)S(1)}, f32[256,256]{1,0:T(8,128)S(1)}, u32[]{:S(2)}, u32[]{:S(2)}) collective-permute-start(f32[256,256]{1,0:T(8,128)S(1)} %get-tuple-element.55), channel_id=1, source_target_pairs={{0,28},{1,29},{2,30},{3,31},{4,0},{5,1},{6,2},{7,3},{8,4},{9,5},{1... | collective-permute-start | bytes 786440 | tf_op jit(solution)/shard_map/ppermute | solution.py:39
  32.4 4.1 %collective-permute-start.13 = (f32[128,256]{1,0:T(8,128)S(1)}, f32[128,256]{1,0:T(8,128)S(1)}, u32[]{:S(2)}, u32[]{:S(2)}) collective-permute-start(f32[128,256]{1,0:T(8,128)S(1)} %get-tuple-element.56), channel_id=1, source_target_pairs={{0,24},{1,25},{2,26},{3,27},{4,28},{5,29},{6,30},{7,31},{8,0},{9,1... | collective-permute-start | bytes 393224 | tf_op jit(solution)/shard_map/ppermute | solution.py:39
  36.6 0.7 collective-permute-start.9
  37.3 6.3 %collective-permute-done.11.four_up = f32[128,256]{1,0:T(8,128)S(1)} collective-permute-done((f32[128,256]{1,0:T(8,128)S(1)}, f32[128,256]{1,0:T(8,128)S(1)}, u32[]{:S(2)}, u32[]{:S(2)}) %collective-permute-start.11) | collective-permute-done | bytes 131104 | tf_op jit(solution)/shard_map/ppermute | solution.py:39
  43.6 2.4 %collective-permute-start.8 = (f32[256,256]{1,0:T(8,128)S(1)}, f32[256,256]{1,0:T(8,128)S(1)}, u32[]{:S(2)}, u32[]{:S(2)}) collective-permute-start(f32[256,256]{1,0:T(8,128)S(1)} %get-tuple-element.49), channel_id=1, source_target_pairs={{0,4},{1,5},{2,6},{3,7},{4,8},{5,9},{6,10},{7,11},{8,12},{9,13},{1... | collective-permute-start | bytes 786440 | tf_op jit(solution)/shard_map/ppermute | solution.py:39
  46.1 4.5 %collective-permute-start.14 = (f32[256,256]{1,0:T(8,128)S(1)}, f32[256,256]{1,0:T(8,128)S(1)}, u32[]{:S(2)}, u32[]{:S(2)}) collective-permute-start(f32[256,256]{1,0:T(8,128)S(1)} %get-tuple-element.57), channel_id=1, source_target_pairs={{0,8},{1,9},{2,10},{3,11},{4,12},{5,13},{6,14},{7,15},{8,16},{9,17... | collective-permute-start | bytes 786440 | tf_op jit(solution)/shard_map/ppermute | solution.py:39
  50.6 0.7 collective-permute-start.16
  51.3 3.8 %collective-permute-done.8 = f32[256,256]{1,0:T(8,128)S(1)} collective-permute-done((f32[256,256]{1,0:T(8,128)S(1)}, f32[256,256]{1,0:T(8,128)S(1)}, u32[]{:S(2)}, u32[]{:S(2)}) %collective-permute-start.8) | collective-permute-done | bytes 262176 | tf_op jit(solution)/shard_map/ppermute | solution.py:39
  55.1 9.8 %collective-permute-done.14 = f32[256,256]{1,0:T(8,128)S(1)} collective-permute-done((f32[256,256]{1,0:T(8,128)S(1)}, f32[256,256]{1,0:T(8,128)S(1)}, u32[]{:S(2)}, u32[]{:S(2)}) %collective-permute-start.14) | collective-permute-done | bytes 262176 | tf_op jit(solution)/shard_map/ppermute | solution.py:39
  65.1 0.8 collective-permute-start.17
  65.8 5.9 %collective-permute-done.17.other = f32[256,256]{1,0:T(8,128)S(1)} collective-permute-done((f32[256,256]{1,0:T(8,128)S(1)}, f32[256,256]{1,0:T(8,128)S(1)}, u32[]{:S(2)}, u32[]{:S(2)}) %collective-permute-start.17) | collective-permute-done | bytes 262176 | tf_op jit(solution)/shard_map/ppermute | solution.py:464
  71.7 1.6 %middle.1 = (f32[128,256]{1,0:T(8,128)}, f32[256,256]{1,0:T(8,128)}, f32[256,256]{1,0:T(8,128)S(1)}) custom-call(s32[5]{0:T(128)S(1)} %stack.23.where, f32[256,256]{1,0:T(8,128)S(1)} %add_add_fusion.mine, f32[256,256]{1,0:T(8,128)S(1)} %collective-permute-done.17.other, f32[256,256]{1,0:T(8,128)S(1)} %copy-done.2, f32[1,256]{1,0:T(1,128)S(1)} %bitcast.14, ...), custom_call_target="tpu_custom_call" | custom-call | tf_op jit(solution)/shard_map/middle/pallas_call | solution.py:212
  73.4 2.4 %collective-permute-start.19 = (f32[256,256]{1,0:T(8,128)}, f32[256,256]{1,0:T(8,128)}, u32[]{:S(2)}, u32[]{:S(2)}) collective-permute-start(f32[256,256]{1,0:T(8,128)} %get-tuple-element.62.refs_0_.grad), channel_id=1, source_target_pairs={{0,24},{1,25},{2,26},{3,27},{4,28},{5,29},{6,30},{7,31},{8,0},{9,1... | collective-permute-start | bytes 786440 | tf_op jit(solution)/shard_map/ppermute | solution.py:39
  75.8 0.5 collective-permute-start.21
  76.3 2.0 %collective-permute-start.25 = (f32[256,256]{1,0:T(8,128)}, f32[256,256]{1,0:T(8,128)}, u32[]{:S(2)}, u32[]{:S(2)}) collective-permute-start(f32[256,256]{1,0:T(8,128)} %get-tuple-element.62.refs_0_.grad), channel_id=1, source_target_pairs={{0,4},{1,5},{2,6},{3,7},{4,8},{5,9},{6,10},{7,11},{8,12},{9,13},{1... | collective-permute-start | bytes 786440 | tf_op jit(solution)/shard_map/ppermute | solution.py:39
  78.3 2.0 %outer.1 = f32[8,40,256]{2,1,0:T(8,128)} custom-call(f32[256,256]{1,0:T(8,128)S(1)} %get-tuple-element.73.total, f32[256,256]{1,0:T(8,128)} %get-tuple-element.62.refs_0_.grad), custom_call_target="tpu_custom_call" | custom-call | tf_op jit(solution)/shard_map/outer/pallas_call | solution.py:235
  80.3 6.6 %all-to-all-start = ((f32[8,40,256]{2,1,0:T(8,128)}), f32[8,40,256]{2,1,0:T(8,128)}, u32[]{:S(2)}, u32[]{:S(2)}) async-start(f32[8,40,256]{2,1,0:T(8,128)} %outer.1), calls=%async_computation | async-start | bytes 655360 | tf_op jit(solution)/shard_map/all_to_all | solution.py:471
  87.0 2.2 %collective-permute-start.20 = (f32[256,256]{1,0:T(8,128)}, f32[256,256]{1,0:T(8,128)}, u32[]{:S(2)}, u32[]{:S(2)}) collective-permute-start(f32[256,256]{1,0:T(8,128)} %collective-permute-done.19.two.refs_2_), channel_id=1, source_target_pairs={{0,28},{1,29},{2,30},{3,31},{4,0},{5,1},{6,2},{7,3},{8,4},{9,5},{1... | collective-permute-start | bytes 786440 | tf_op jit(solution)/shard_map/ppermute | solution.py:39
  89.2 0.2 collective-permute-start.24
  89.4 1.0 halves.1
  90.5 3.5 %collective-permute-start.22 = (f32[128,256]{1,0:T(8,128)S(1)}, f32[128,256]{1,0:T(8,128)S(1)}, u32[]{:S(2)}, u32[]{:S(2)}) collective-permute-start(f32[128,256]{1,0:T(8,128)S(1)} %get-tuple-element.63), channel_id=1, source_target_pairs={{0,8},{1,9},{2,10},{3,11},{4,12},{5,13},{6,14},{7,15},{8,16},{9,17... | collective-permute-start | bytes 393224 | tf_op jit(solution)/shard_map/ppermute | solution.py:39
  93.9 0.7 collective-permute-start.23
  94.7 1.7 %spread.1 = f32[8,40,256]{2,1,0:T(8,128)} custom-call(f32[8,40,256]{2,1,0:T(8,128)} %all-to-all-done.parts), custom_call_target="tpu_custom_call" | custom-call | tf_op jit(solution)/shard_map/spread/pallas_call | solution.py:254
  96.4 4.8 %all-to-all-start.1 = ((f32[8,40,256]{2,1,0:T(8,128)}), f32[8,40,256]{2,1,0:T(8,128)}, u32[]{:S(2)}, u32[]{:S(2)}) async-start(f32[8,40,256]{2,1,0:T(8,128)} %spread.1), calls=%async_computation.1 | async-start | bytes 655360 | tf_op jit(solution)/shard_map/all_to_all | solution.py:472
  101.2 1.4 collective-permute-done.22.refs_4_
  102.7 1.6 %join.1 = (f32[512,256]{1,0:T(8,128)S(1)}, f32[512,256]{1,0:T(8,128)S(1)}, f32[512,256]{1,0:T(8,128)S(1)}, f32[512,256]{1,0:T(8,128)S(1)}) custom-call(f32[256,256]{1,0:T(8,128)} %get-tuple-element.62.refs_0_.grad, f32[256,256]{1,0:T(8,128)} %collective-permute-done.18.refs_1_, f32[256,256]{1,0:T(8,128)} %collective-permute-done.19.two.refs_2_, ...), custom_call_target="tpu_custom_call" | custom-call | flops 999999995904 | tf_op jit(solution)/shard_map/join/pallas_call | solution.py:292
  104.4 0.5 collective-permute-start.27
  105.0 0.4 collective-permute-start.29
  105.4 0.9 collective-permute-done.26.refs_4_
  106.3 0.7 collective-permute-done.27.refs_5_
  107.0 0.7 collective-permute-done.28.refs_6_
  107.8 0.7 collective-permute-done.29.refs_7_
  108.5 2.1 %backward_tiles.1 = (f32[128,256]{1,0:T(8,128)S(1)}, f32[128,256]{1,0:T(8,128)S(1)}, f32[128,256]{1,0:T(8,128)S(1)}, f32[128,256]{1,0:T(8,128)S(1)}, f32[128,256...) custom-call(s32[12,2]{1,0:T(8,128)S(1)} %copy-done.6, ...), custom_call_target="tpu_custom_call" | custom-call | tf_op jit(solution)/shard_map/backward_tiles/pallas_call | solution.py:342
  110.6 1.5 %collective-permute-start.35 = (f32[128,256]{1,0:T(8,128)S(1)}, f32[128,256]{1,0:T(8,128)S(1)}, u32[]{:S(2)}, u32[]{:S(2)}) collective-permute-start(f32[128,256]{1,0:T(8,128)S(1)} %get-tuple-element.79), channel_id=1, source_target_pairs={{0,64},{32,96},{64,128},{96,160},{128,192},{160,224},{192,0},{224,... | collective-permute-start | bytes 393224 | tf_op jit(solution)/shard_map/ppermute | solution.py:52
  112.1 3.3 %collective-permute-start.36 = (f32[128,256]{1,0:T(8,128)S(1)}, f32[128,256]{1,0:T(8,128)S(1)}, u32[]{:S(2)}, u32[]{:S(2)}) collective-permute-start(f32[128,256]{1,0:T(8,128)S(1)} %get-tuple-element.80), channel_id=1, source_target_pairs={{0,128},{32,160},{64,192},{96,224},{128,0},{160,32},{192,64},{224,... | collective-permute-start | bytes 393224 | tf_op jit(solution)/shard_map/ppermute | solution.py:52
  115.4 0.8 collective-permute-start.37
  116.3 1.0 total.1
  117.4 1.2 collective-permute-done.30
  118.6 0.8 collective-permute-start.31
  119.4 4.7 %collective-permute-done.31.piece_across = f32[40,256]{1,0:T(8,128)S(1)} collective-permute-done((f32[40,256]{1,0:T(8,128)S(1)}, f32[40,256]{1,0:T(8,128)S(1)}, u32[]{:S(2)}, u32[]{:S(2)}) %collective-permute-start.31) | collective-permute-done | bytes 40992 | tf_op jit(solution)/shard_map/ppermute | solution.py:56
  124.1 1.3 collective-permute-start.32
  125.4 1.4 %collective-permute-start.33 = (f32[208,256]{1,0:T(8,128)S(1)}, f32[208,256]{1,0:T(8,128)S(1)}, u32[]{:S(2)}, u32[]{:S(2)}) collective-permute-start(f32[208,256]{1,0:T(8,128)S(1)} %get-tuple-element.75), channel_id=1, source_target_pairs={{0,128},{32,160},{64,192},{96,224},{128,0},{160,32},{192,64},{224,... | collective-permute-start | bytes 638984 | tf_op jit(solution)/shard_map/ppermute | solution.py:52
  126.8 0.8 collective-permute-start.34
  127.6 1.1 collective-permute-start.38
  128.7 3.7 %collective-permute-done.32.one = f32[208,256]{1,0:T(8,128)S(1)} collective-permute-done((f32[208,256]{1,0:T(8,128)S(1)}, f32[208,256]{1,0:T(8,128)S(1)}, u32[]{:S(2)}, u32[]{:S(2)}) %collective-permute-start.32) | collective-permute-done | bytes 213024 | tf_op jit(solution)/shard_map/ppermute | solution.py:52
  132.4 2.7 %collective-permute-done.33.two = f32[208,256]{1,0:T(8,128)S(1)} collective-permute-done((f32[208,256]{1,0:T(8,128)S(1)}, f32[208,256]{1,0:T(8,128)S(1)}, u32[]{:S(2)}, u32[]{:S(2)}) %collective-permute-start.33) | collective-permute-done | bytes 213024 | tf_op jit(solution)/shard_map/ppermute | solution.py:52
  135.1 1.9 %collective-permute-done.34.three = f32[208,256]{1,0:T(8,128)S(1)} collective-permute-done((f32[208,256]{1,0:T(8,128)S(1)}, f32[208,256]{1,0:T(8,128)S(1)}, u32[]{:S(2)}, u32[]{:S(2)}) %collective-permute-start.34) | collective-permute-done | bytes 213024 | tf_op jit(solution)/shard_map/ppermute | solution.py:52
  137.0 1.3 unpack.1
  138.3 1.0 final.1
  (59 shorter events, 0.9 us)
Async XLA Ops:
  0.6 9.6 %collective-permute-start.3 = (f32[128,256]{1,0:T(8,128)}, f32[128,256]{1,0:T(8,128)}, u32[]{:S(2)}, u32[]{:S(2)}) collective-permute-start(f32[128,256]{1,0:T(8,128)} %refs_0_.1), channel_id=1, source_target_pairs={{0,32},{32,0},{64,96},{96,64},{128,160},{160,128},{192,224},{224,1... | collective-permute-start | bytes 393224 | tf_op jit(solution)/shard_map/ppermute | solution.py:56
  3.9 7.9 %collective-permute-start = (f32[128,256]{1,0:T(8,128)}, f32[128,256]{1,0:T(8,128)S(1)}, u32[]{:S(2)}, u32[]{:S(2)}) collective-permute-start(f32[128,256]{1,0:T(8,128)} %refs_0_.1), channel_id=1, source_target_pairs={{0,192},{32,224},{64,0},{96,32},{128,64},{160,96},{192,128},{224,1... | collective-permute-start | bytes 393224 | tf_op jit(solution)/shard_map/ppermute | solution.py:52
  4.4 9.9 %collective-permute-start.1 = (f32[128,256]{1,0:T(8,128)}, f32[128,256]{1,0:T(8,128)S(1)}, u32[]{:S(2)}, u32[]{:S(2)}) collective-permute-start(f32[128,256]{1,0:T(8,128)} %refs_0_.1), channel_id=1, source_target_pairs={{0,128},{32,160},{64,192},{96,224},{128,0},{160,32},{192,64},{224,... | collective-permute-start | bytes 393224 | tf_op jit(solution)/shard_map/ppermute | solution.py:52
  6.9 7.4 %collective-permute-start.2 = (f32[128,256]{1,0:T(8,128)}, f32[128,256]{1,0:T(8,128)S(1)}, u32[]{:S(2)}, u32[]{:S(2)}) collective-permute-start(f32[128,256]{1,0:T(8,128)} %refs_0_.1), channel_id=1, source_target_pairs={{0,64},{32,96},{64,128},{96,160},{128,192},{160,224},{192,0},{224,... | collective-permute-start | bytes 393224 | tf_op jit(solution)/shard_map/ppermute | solution.py:52
  9.4 10.0 %copy-start.5 = (s32[12,2]{1,0:T(8,128)}, s32[12,2]{1,0:T(8,128)S(1)}, u32[]{:S(2)}) copy-start(s32[12,2]{1,0:T(8,128)S(1)} %copy.11.place) | copy-start | bytes 292
  10.2 61.6 %copy-start.7 = (s32[5]{0:T(128)}, s32[5]{0:T(128)S(1)}, u32[]{:S(2)}) copy-start(s32[5]{0:T(128)S(1)} %stack.23.where) | copy-start | bytes 64
  10.2 8.5 %collective-permute-start.4 = (f32[128,256]{1,0:T(8,128)}, f32[128,256]{1,0:T(8,128)}, u32[]{:S(2)}, u32[]{:S(2)}) collective-permute-start(f32[128,256]{1,0:T(8,128)} %collective-permute-done.3.a), channel_id=1, source_target_pairs={{0,192},{32,224},{64,0},{96,32},{128,64},{160,96},{192,128},{224,1... | collective-permute-start | bytes 393224 | tf_op jit(solution)/shard_map/ppermute | solution.py:52
  10.5 8.2 %collective-permute-start.5 = (f32[128,256]{1,0:T(8,128)}, f32[128,256]{1,0:T(8,128)}, u32[]{:S(2)}, u32[]{:S(2)}) collective-permute-start(f32[128,256]{1,0:T(8,128)} %collective-permute-done.3.a), channel_id=1, source_target_pairs={{0,128},{32,160},{64,192},{96,224},{128,0},{160,32},{192,64},{224,... | collective-permute-start | bytes 393224 | tf_op jit(solution)/shard_map/ppermute | solution.py:52
  11.8 7.7 %collective-permute-start.6 = (f32[128,256]{1,0:T(8,128)}, f32[128,256]{1,0:T(8,128)}, u32[]{:S(2)}, u32[]{:S(2)}) collective-permute-start(f32[128,256]{1,0:T(8,128)} %collective-permute-done.3.a), channel_id=1, source_target_pairs={{0,64},{32,96},{64,128},{96,160},{128,192},{160,224},{192,0},{224,... | collective-permute-start | bytes 393224 | tf_op jit(solution)/shard_map/ppermute | solution.py:52
  14.3 0.9 copy-start.10
  15.2 4.2 %copy-start = (f32[1,1,12,128,128]{4,3,2,1,0:T(8,128)S(1)}, f32[1,1,12,128,128]{4,3,2,1,0:T(8,128)}, u32[]{:S(2)}) copy-start(f32[1,1,12,128,128]{4,3,2,1,0:T(8,128)} %param.10) | copy-start | bytes 2359300
  21.8 4.2 %collective-permute-start.7 = (f32[16,128,256]{2,1,0:T(8,128)S(1)}, f32[16,128,256]{2,1,0:T(8,128)S(1)}, u32[]{:S(2)}, u32[]{:S(2)}) collective-permute-start(f32[16,128,256]{2,1,0:T(8,128)S(1)} %get-tuple-element.47), channel_id=1, source_target_pairs={{0,1},{1,0},{2,3},{3,2},{4,5},{5,4},{6,7},{7,6},{8,9},{9,8},{10,11... | collective-permute-start | bytes 6291464 | tf_op jit(solution)/shard_map/ppermute | solution.py:462
  26.1 24.5 %copy-start.4 = (f32[128,256]{1,0:T(8,128)S(1)}, f32[128,256]{1,0:T(8,128)}, u32[]{:S(2)}) copy-start(f32[128,256]{1,0:T(8,128)} %cot_own.1) | copy-start | bytes 393220
  26.4 45.4 %copy-start.2 = (f32[256,256]{1,0:T(8,128)S(1)}, f32[256,256]{1,0:T(8,128)}, u32[]{:S(2)}) copy-start(f32[256,256]{1,0:T(8,128)} %weight.3) | copy-start | bytes 786436
  26.4 45.3 %copy-start.9 = (f32[256]{0:T(256)S(1)}, f32[256]{0:T(256)}, u32[]{:S(2)}) copy-start(f32[256]{0:T(256)} %param.9) | copy-start | bytes 3076
  26.4 19.6 %collective-permute-start.10 = (f32[256,256]{1,0:T(8,128)S(1)}, f32[256,256]{1,0:T(8,128)S(1)}, u32[]{:S(2)}, u32[]{:S(2)}) collective-permute-start(f32[256,256]{1,0:T(8,128)S(1)} %get-tuple-element.52), channel_id=1, source_target_pairs={{0,4},{1,5},{2,6},{3,7},{4,8},{5,9},{6,10},{7,11},{8,12},{9,13},{1... | collective-permute-start | bytes 786440 | tf_op jit(solution)/shard_map/ppermute | solution.py:39
  28.4 17.6 %collective-permute-start.12 = (f32[256,256]{1,0:T(8,128)S(1)}, f32[256,256]{1,0:T(8,128)S(1)}, u32[]{:S(2)}, u32[]{:S(2)}) collective-permute-start(f32[256,256]{1,0:T(8,128)S(1)} %get-tuple-element.55), channel_id=1, source_target_pairs={{0,28},{1,29},{2,30},{3,31},{4,0},{5,1},{6,2},{7,3},{8,4},{9,5},{1... | collective-permute-start | bytes 786440 | tf_op jit(solution)/shard_map/ppermute | solution.py:39
  32.4 11.2 %collective-permute-start.11 = (f32[128,256]{1,0:T(8,128)S(1)}, f32[128,256]{1,0:T(8,128)S(1)}, u32[]{:S(2)}, u32[]{:S(2)}) collective-permute-start(f32[128,256]{1,0:T(8,128)S(1)} %get-tuple-element.53), channel_id=1, source_target_pairs={{0,8},{1,9},{2,10},{3,11},{4,12},{5,13},{6,14},{7,15},{8,16},{9,17... | collective-permute-start | bytes 393224 | tf_op jit(solution)/shard_map/ppermute | solution.py:39
  32.4 13.6 %collective-permute-start.13 = (f32[128,256]{1,0:T(8,128)S(1)}, f32[128,256]{1,0:T(8,128)S(1)}, u32[]{:S(2)}, u32[]{:S(2)}) collective-permute-start(f32[128,256]{1,0:T(8,128)S(1)} %get-tuple-element.56), channel_id=1, source_target_pairs={{0,24},{1,25},{2,26},{3,27},{4,28},{5,29},{6,30},{7,31},{8,0},{9,1... | collective-permute-start | bytes 393224 | tf_op jit(solution)/shard_map/ppermute | solution.py:39
  36.6 14.7 %collective-permute-start.9 = (f32[256,256]{1,0:T(8,128)S(1)}, f32[256,256]{1,0:T(8,128)S(1)}, u32[]{:S(2)}, u32[]{:S(2)}) collective-permute-start(f32[256,256]{1,0:T(8,128)S(1)} %get-tuple-element.50), channel_id=1, source_target_pairs={{0,28},{1,29},{2,30},{3,31},{4,0},{5,1},{6,2},{7,3},{8,4},{9,5},{1... | collective-permute-start | bytes 786440 | tf_op jit(solution)/shard_map/ppermute | solution.py:39
  43.6 11.5 %collective-permute-start.8 = (f32[256,256]{1,0:T(8,128)S(1)}, f32[256,256]{1,0:T(8,128)S(1)}, u32[]{:S(2)}, u32[]{:S(2)}) collective-permute-start(f32[256,256]{1,0:T(8,128)S(1)} %get-tuple-element.49), channel_id=1, source_target_pairs={{0,4},{1,5},{2,6},{3,7},{4,8},{5,9},{6,10},{7,11},{8,12},{9,13},{1... | collective-permute-start | bytes 786440 | tf_op jit(solution)/shard_map/ppermute | solution.py:39
  46.1 18.8 %collective-permute-start.14 = (f32[256,256]{1,0:T(8,128)S(1)}, f32[256,256]{1,0:T(8,128)S(1)}, u32[]{:S(2)}, u32[]{:S(2)}) collective-permute-start(f32[256,256]{1,0:T(8,128)S(1)} %get-tuple-element.57), channel_id=1, source_target_pairs={{0,8},{1,9},{2,10},{3,11},{4,12},{5,13},{6,14},{7,15},{8,16},{9,17... | collective-permute-start | bytes 786440 | tf_op jit(solution)/shard_map/ppermute | solution.py:39
  50.6 14.3 %collective-permute-start.15 = (f32[256,256]{1,0:T(8,128)S(1)}, f32[256,256]{1,0:T(8,128)S(1)}, u32[]{:S(2)}, u32[]{:S(2)}) collective-permute-start(f32[256,256]{1,0:T(8,128)S(1)} %get-tuple-element.58), channel_id=1, source_target_pairs={{0,24},{1,25},{2,26},{3,27},{4,28},{5,29},{6,30},{7,31},{8,0},{9,1... | collective-permute-start | bytes 786440 | tf_op jit(solution)/shard_map/ppermute | solution.py:39
  50.6 14.4 %collective-permute-start.16 = (f32[128,256]{1,0:T(8,128)S(1)}, f32[128,256]{1,0:T(8,128)S(1)}, u32[]{:S(2)}, u32[]{:S(2)}) collective-permute-start(f32[128,256]{1,0:T(8,128)S(1)} %copy-done.4), channel_id=1, source_target_pairs={{0,2},{1,3},{2,0},{3,1},{4,6},{5,7},{6,4},{7,5},{8,10},{9,11},{10,... | collective-permute-start | bytes 393224 | tf_op jit(solution)/shard_map/ppermute | solution.py:461
  65.1 6.7 %collective-permute-start.17 = (f32[256,256]{1,0:T(8,128)S(1)}, f32[256,256]{1,0:T(8,128)S(1)}, u32[]{:S(2)}, u32[]{:S(2)}) collective-permute-start(f32[256,256]{1,0:T(8,128)S(1)} %add_add_fusion.mine), channel_id=1, source_target_pairs={{0,2},{1,3},{2,0},{3,1},{4,6},{5,7},{6,4},{7,5},{8,10},{9,11},{10,... | collective-permute-start | bytes 786440 | tf_op jit(solution)/shard_map/ppermute | solution.py:464
  73.4 13.6 %collective-permute-start.19 = (f32[256,256]{1,0:T(8,128)}, f32[256,256]{1,0:T(8,128)}, u32[]{:S(2)}, u32[]{:S(2)}) collective-permute-start(f32[256,256]{1,0:T(8,128)} %get-tuple-element.62.refs_0_.grad), channel_id=1, source_target_pairs={{0,24},{1,25},{2,26},{3,27},{4,28},{5,29},{6,30},{7,31},{8,0},{9,1... | collective-permute-start | bytes 786440 | tf_op jit(solution)/shard_map/ppermute | solution.py:39
  75.8 13.4 %collective-permute-start.21 = (f32[256,256]{1,0:T(8,128)}, f32[256,256]{1,0:T(8,128)}, u32[]{:S(2)}, u32[]{:S(2)}) collective-permute-start(f32[256,256]{1,0:T(8,128)} %get-tuple-element.62.refs_0_.grad), channel_id=1, source_target_pairs={{0,8},{1,9},{2,10},{3,11},{4,12},{5,13},{6,14},{7,15},{8,16},{9,17... | collective-permute-start | bytes 786440 | tf_op jit(solution)/shard_map/ppermute | solution.py:39
  76.3 17.7 %collective-permute-start.18 = (f32[256,256]{1,0:T(8,128)}, f32[256,256]{1,0:T(8,128)}, u32[]{:S(2)}, u32[]{:S(2)}) collective-permute-start(f32[256,256]{1,0:T(8,128)} %get-tuple-element.62.refs_0_.grad), channel_id=1, source_target_pairs={{0,28},{1,29},{2,30},{3,31},{4,0},{5,1},{6,2},{7,3},{8,4},{9,5},{1... | collective-permute-start | bytes 786440 | tf_op jit(solution)/shard_map/ppermute | solution.py:39
  76.3 24.9 %collective-permute-start.25 = (f32[256,256]{1,0:T(8,128)}, f32[256,256]{1,0:T(8,128)}, u32[]{:S(2)}, u32[]{:S(2)}) collective-permute-start(f32[256,256]{1,0:T(8,128)} %get-tuple-element.62.refs_0_.grad), channel_id=1, source_target_pairs={{0,4},{1,5},{2,6},{3,7},{4,8},{5,9},{6,10},{7,11},{8,12},{9,13},{1... | collective-permute-start | bytes 786440 | tf_op jit(solution)/shard_map/ppermute | solution.py:39
  80.3 14.4 %all-to-all-start = ((f32[8,40,256]{2,1,0:T(8,128)}), f32[8,40,256]{2,1,0:T(8,128)}, u32[]{:S(2)}, u32[]{:S(2)}) async-start(f32[8,40,256]{2,1,0:T(8,128)} %outer.1), calls=%async_computation | async-start | bytes 655360 | tf_op jit(solution)/shard_map/all_to_all | solution.py:471
  87.0 15.6 %collective-permute-start.20 = (f32[256,256]{1,0:T(8,128)}, f32[256,256]{1,0:T(8,128)}, u32[]{:S(2)}, u32[]{:S(2)}) collective-permute-start(f32[256,256]{1,0:T(8,128)} %collective-permute-done.19.two.refs_2_), channel_id=1, source_target_pairs={{0,28},{1,29},{2,30},{3,31},{4,0},{5,1},{6,2},{7,3},{8,4},{9,5},{1... | collective-permute-start | bytes 786440 | tf_op jit(solution)/shard_map/ppermute | solution.py:39
  89.2 13.4 %collective-permute-start.24 = (f32[256,256]{1,0:T(8,128)}, f32[256,256]{1,0:T(8,128)}, u32[]{:S(2)}, u32[]{:S(2)}) collective-permute-start(f32[256,256]{1,0:T(8,128)} %collective-permute-done.21.six.refs_7_), channel_id=1, source_target_pairs={{0,4},{1,5},{2,6},{3,7},{4,8},{5,9},{6,10},{7,11},{8,12},{9,13},{1... | collective-permute-start | bytes 786440 | tf_op jit(solution)/shard_map/ppermute | solution.py:39
  90.5 12.1 %collective-permute-start.22 = (f32[128,256]{1,0:T(8,128)S(1)}, f32[128,256]{1,0:T(8,128)S(1)}, u32[]{:S(2)}, u32[]{:S(2)}) collective-permute-start(f32[128,256]{1,0:T(8,128)S(1)} %get-tuple-element.63), channel_id=1, source_target_pairs={{0,8},{1,9},{2,10},{3,11},{4,12},{5,13},{6,14},{7,15},{8,16},{9,17... | collective-permute-start | bytes 393224 | tf_op jit(solution)/shard_map/ppermute | solution.py:39
  93.9 8.7 %collective-permute-start.23 = (f32[128,256]{1,0:T(8,128)S(1)}, f32[128,256]{1,0:T(8,128)S(1)}, u32[]{:S(2)}, u32[]{:S(2)}) collective-permute-start(f32[128,256]{1,0:T(8,128)S(1)} %get-tuple-element.64), channel_id=1, source_target_pairs={{0,24},{1,25},{2,26},{3,27},{4,28},{5,29},{6,30},{7,31},{8,0},{9,1... | collective-permute-start | bytes 393224 | tf_op jit(solution)/shard_map/ppermute | solution.py:39
  96.4 19.8 %all-to-all-start.1 = ((f32[8,40,256]{2,1,0:T(8,128)}), f32[8,40,256]{2,1,0:T(8,128)}, u32[]{:S(2)}, u32[]{:S(2)}) async-start(f32[8,40,256]{2,1,0:T(8,128)} %spread.1), calls=%async_computation.1 | async-start | bytes 655360 | tf_op jit(solution)/shard_map/all_to_all | solution.py:472
  102.6 5.9 %copy-start.1 = (f32[1,1,12,128,128]{4,3,2,1,0:T(8,128)S(1)}, f32[1,1,12,128,128]{4,3,2,1,0:T(8,128)}, u32[]{:S(2)}) copy-start(f32[1,1,12,128,128]{4,3,2,1,0:T(8,128)} %param.10) | copy-start | bytes 2359300
  102.6 5.9 %copy-start.6 = (s32[12,2]{1,0:T(8,128)S(1)}, s32[12,2]{1,0:T(8,128)}, u32[]{:S(2)}) copy-start(s32[12,2]{1,0:T(8,128)} %copy-done.5) | copy-start | bytes 292
  102.6 5.9 %copy-start.8 = (s32[5]{0:T(128)S(1)}, s32[5]{0:T(128)}, u32[]{:S(2)}) copy-start(s32[5]{0:T(128)} %copy-done.7) | copy-start | bytes 64
  104.3 2.0 %collective-permute-start.26 = (f32[512,256]{1,0:T(8,128)S(1)}, f32[512,256]{1,0:T(8,128)S(1)}, u32[]{:S(2)}, u32[]{:S(2)}) collective-permute-start(f32[512,256]{1,0:T(8,128)S(1)} %get-tuple-element.65.refs_0_), channel_id=1, source_target_pairs={{0,1},{1,0},{2,3},{3,2},{4,5},{5,4},{6,7},{7,6},{8,9},{9,8},{10,11... | collective-permute-start | bytes 1572872 | tf_op jit(solution)/shard_map/ppermute | solution.py:477
  104.4 2.6 %collective-permute-start.27 = (f32[512,256]{1,0:T(8,128)S(1)}, f32[512,256]{1,0:T(8,128)S(1)}, u32[]{:S(2)}, u32[]{:S(2)}) collective-permute-start(f32[512,256]{1,0:T(8,128)S(1)} %get-tuple-element.66.refs_1_), channel_id=1, source_target_pairs={{0,1},{1,0},{2,3},{3,2},{4,5},{5,4},{6,7},{7,6},{8,9},{9,8},{10,11... | collective-permute-start | bytes 1572872 | tf_op jit(solution)/shard_map/ppermute | solution.py:477
  104.9 2.9 %collective-permute-start.28 = (f32[512,256]{1,0:T(8,128)S(1)}, f32[512,256]{1,0:T(8,128)S(1)}, u32[]{:S(2)}, u32[]{:S(2)}) collective-permute-start(f32[512,256]{1,0:T(8,128)S(1)} %get-tuple-element.67.refs_2_), channel_id=1, source_target_pairs={{0,1},{1,0},{2,3},{3,2},{4,5},{5,4},{6,7},{7,6},{8,9},{9,8},{10,11... | collective-permute-start | bytes 1572872 | tf_op jit(solution)/shard_map/ppermute | solution.py:477
  105.0 3.5 %collective-permute-start.29 = (f32[512,256]{1,0:T(8,128)S(1)}, f32[512,256]{1,0:T(8,128)S(1)}, u32[]{:S(2)}, u32[]{:S(2)}) collective-permute-start(f32[512,256]{1,0:T(8,128)S(1)} %get-tuple-element.68.refs_3_), channel_id=1, source_target_pairs={{0,1},{1,0},{2,3},{3,2},{4,5},{5,4},{6,7},{7,6},{8,9},{9,8},{10,11... | collective-permute-start | bytes 1572872 | tf_op jit(solution)/shard_map/ppermute | solution.py:477
  110.6 16.2 %collective-permute-start.35 = (f32[128,256]{1,0:T(8,128)S(1)}, f32[128,256]{1,0:T(8,128)S(1)}, u32[]{:S(2)}, u32[]{:S(2)}) collective-permute-start(f32[128,256]{1,0:T(8,128)S(1)} %get-tuple-element.79), channel_id=1, source_target_pairs={{0,64},{32,96},{64,128},{96,160},{128,192},{160,224},{192,0},{224,... | collective-permute-start | bytes 393224 | tf_op jit(solution)/shard_map/ppermute | solution.py:52
  112.1 15.5 %collective-permute-start.36 = (f32[128,256]{1,0:T(8,128)S(1)}, f32[128,256]{1,0:T(8,128)S(1)}, u32[]{:S(2)}, u32[]{:S(2)}) collective-permute-start(f32[128,256]{1,0:T(8,128)S(1)} %get-tuple-element.80), channel_id=1, source_target_pairs={{0,128},{32,160},{64,192},{96,224},{128,0},{160,32},{192,64},{224,... | collective-permute-start | bytes 393224 | tf_op jit(solution)/shard_map/ppermute | solution.py:52
  115.4 12.1 %collective-permute-start.37 = (f32[128,256]{1,0:T(8,128)S(1)}, f32[128,256]{1,0:T(8,128)S(1)}, u32[]{:S(2)}, u32[]{:S(2)}) collective-permute-start(f32[128,256]{1,0:T(8,128)S(1)} %get-tuple-element.81), channel_id=1, source_target_pairs={{0,192},{32,224},{64,0},{96,32},{128,64},{160,96},{192,128},{224,1... | collective-permute-start | bytes 393224 | tf_op jit(solution)/shard_map/ppermute | solution.py:52
  117.3 1.3 collective-permute-start.30
  118.6 5.5 %collective-permute-start.31 = (f32[40,256]{1,0:T(8,128)S(1)}, f32[40,256]{1,0:T(8,128)S(1)}, u32[]{:S(2)}, u32[]{:S(2)}) collective-permute-start(f32[40,256]{1,0:T(8,128)S(1)} %add.19.piece), channel_id=1, source_target_pairs={{0,32},{32,0},{64,96},{96,64},{128,160},{160,128},{192,224},{224,1... | collective-permute-start | bytes 122888 | tf_op jit(solution)/shard_map/ppermute | solution.py:56
  124.1 8.3 %collective-permute-start.32 = (f32[208,256]{1,0:T(8,128)S(1)}, f32[208,256]{1,0:T(8,128)S(1)}, u32[]{:S(2)}, u32[]{:S(2)}) collective-permute-start(f32[208,256]{1,0:T(8,128)S(1)} %get-tuple-element.74), channel_id=1, source_target_pairs={{0,64},{32,96},{64,128},{96,160},{128,192},{160,224},{192,0},{224,... | collective-permute-start | bytes 638984 | tf_op jit(solution)/shard_map/ppermute | solution.py:52
  125.4 9.7 %collective-permute-start.33 = (f32[208,256]{1,0:T(8,128)S(1)}, f32[208,256]{1,0:T(8,128)S(1)}, u32[]{:S(2)}, u32[]{:S(2)}) collective-permute-start(f32[208,256]{1,0:T(8,128)S(1)} %get-tuple-element.75), channel_id=1, source_target_pairs={{0,128},{32,160},{64,192},{96,224},{128,0},{160,32},{192,64},{224,... | collective-permute-start | bytes 638984 | tf_op jit(solution)/shard_map/ppermute | solution.py:52
  126.8 10.2 %collective-permute-start.34 = (f32[208,256]{1,0:T(8,128)S(1)}, f32[208,256]{1,0:T(8,128)S(1)}, u32[]{:S(2)}, u32[]{:S(2)}) collective-permute-start(f32[208,256]{1,0:T(8,128)S(1)} %get-tuple-element.76), channel_id=1, source_target_pairs={{0,192},{32,224},{64,0},{96,32},{128,64},{160,96},{192,128},{224,1... | collective-permute-start | bytes 638984 | tf_op jit(solution)/shard_map/ppermute | solution.py:52
  127.6 10.7 %collective-permute-start.38 = (f32[128,256]{1,0:T(8,128)S(1)}, f32[128,256]{1,0:T(8,128)S(1)}, u32[]{:S(2)}, u32[]{:S(2)}) collective-permute-start(f32[128,256]{1,0:T(8,128)S(1)} %gather_sums.1), channel_id=1, source_target_pairs={{0,32},{32,0},{64,96},{96,64},{128,160},{160,128},{192,224},{224,1... | collective-permute-start | bytes 393224 | tf_op jit(solution)/shard_map/ppermute | solution.py:56
  137.0 1.3 copy-start.3

commit v5 on v4

--- a/solution.py
+++ b/solution.py
@@ -36,7 +36,10 @@
 
 
 def z_shift(value, distance):
-    return lax.ppermute(value, "col", col_pairs(lambda z, y, core: ((z + distance) % Z, y, core)))
+    def move(z, y, core):
+        return (z + (1 - 2 * core) * distance) % Z, y, core
+
+    return lax.ppermute(value, "col", col_pairs(move))
 
 
 def row_pairs(move):
@@ -83,7 +86,8 @@
 
 def locate(tile, where):
     mine = lax.rem(tile, 2) == where[2]
-    distance = lax.rem(lax.div(tile, 2 * YL) - where[0] + Z, Z)
+    away = lax.div(tile, 2 * YL) - where[0]
+    distance = lax.rem(jnp.where(lax.rem(tile, 2) == 0, away, -away) + Z, Z)
     return mine, distance, lax.rem(lax.div(tile, 2), YL)
 
 
@@ -142,76 +146,80 @@
     )(place, count, where, values, *near, *far)
 
 
-def add_cores_kernel(first, second, own, one, two, three, four_up, four_down, five, six, seven):
-    def total(tile):
-        return first[tile] + second[tile]
-
-    for distance, out in ((3, three), (5, five), (0, own), (1, one), (2, two), (6, six), (7, seven)):
-        for y in range(YL):
-            out[y * TILE : (y + 1) * TILE, :] = total(distance * YL + y)
-    four_up[...] = total(4 * YL)
-    four_down[...] = total(4 * YL + 1)
+def add_cores_kernel(first, second, *outs):
+    for tile, out in enumerate(outs):
+        out[...] = first[tile] + second[tile]
 
 
 def add_cores(first, second):
-    width = first.shape[-1]
-    whole, half = shaped(PAIR, width), shaped(TILE, width)
+    tiles = first.shape[0]
     return pl.pallas_call(
         add_cores_kernel,
-        out_shape=(whole,) * 4 + (half,) * 2 + (whole,) * 3,
+        out_shape=(shaped(*first.shape[1:]),) * tiles,
         in_specs=[VMEM] * 2,
-        out_specs=(VMEM,) * 9,
+        out_specs=(VMEM,) * tiles,
         compiler_params=params(10),
         name="add_cores",
     )(first, second)
 
 
-def relay_kernel(two, three, four_up, six, five, four_down, up, down):
-    up[:TILE, :] = two[:TILE, :] + three[:TILE, :] + four_up[...]
-    up[TILE:, :] = two[TILE:, :] + three[TILE:, :]
-    down[:TILE, :] = six[:TILE, :] + five[:TILE, :]
-    down[TILE:, :] = six[TILE:, :] + five[TILE:, :] + four_down[...]
-
-
-def relay(*operands):
-    return pl.pallas_call(
-        relay_kernel,
-        out_shape=(jax.ShapeDtypeStruct(operands[0].shape, jnp.float32),) * 2,
-        in_specs=[VMEM] * 6,
-        out_specs=(VMEM,) * 2,
-        compiler_params=params(5),
-        name="relay",
-    )(*operands)
-
-
-def scatter_z(own, one, two, three, four_up, four_down, five, six, seven):
-    from_three, from_five = z_shift(three, 1), z_shift(five, -1)
-    from_up, from_down = z_shift(four_up, 2), z_shift(four_down, -2)
-    from_one, from_seven = z_shift(one, 1), z_shift(seven, -1)
-    up, down = relay(two, from_three, from_up, six, from_five, from_down)
-    from_two, from_six = z_shift(up, 2), z_shift(down, -2)
-    return ((own + from_one) + from_seven) + (from_two + from_six)
-
-
-def middle_kernel(where, mine, other, weight, bias, cot_own, cot_other, output, grad, total, cots):
+def ring_z(blocks):
+    up, down = blocks[4], blocks[5]
+    for step in (3, 2, 1):
+        up = blocks[step] + z_shift(up, 1)
+    for step in (6, 7):
+        down = blocks[step] + z_shift(down, -1)
+    return blocks[0], z_shift(up, 1), z_shift(down, -1)
+
+
+def last_sum_kernel(*refs):
+    out = refs[-1]
+    for y in range(YL):
+        part = refs[3 * y][...] + refs[3 * y + 1][...] + refs[3 * y + 2][...]
+        out[y * TILE : (y + 1) * TILE, :] = part
+
+
+def last_sum(*parts):
+    return pl.pallas_call(
+        last_sum_kernel,
+        out_shape=shaped(PAIR, parts[0].shape[1]),
+        in_specs=[VMEM] * len(parts),
+        out_specs=VMEM,
+        compiler_params=params(4),
+        name="last_sum",
+    )(*parts)
+
+
+def middle_kernel(where, mine, other, weight, bias, cot_own, cot_other, output, grad, extra, cots):
     y = where[1]
     cots[y] = cot_own[...]
     cots[1 - y] = cot_other[...]
     cot = cots[...].reshape(grad.shape)
-    summed = mine[...] + other[...]
-    total[...] = summed
-    pre = dot3(split(summed), split(weight[...]), ((1,), (0,))) + bias[...]
+    summed = split(mine[...] + other[...])
+    pre = dot3(summed, split(weight[...]), ((1,), (0,))) + bias[...]
     sigma = jax.nn.sigmoid(pre)
-    grad[...] = cot * (sigma * (1.0 + pre * (1.0 - sigma)))
+    value = cot * (sigma * (1.0 + pre * (1.0 - sigma)))
+    grad[...] = value
     cots[...] = (pre * sigma).reshape(cots.shape)
     output[...] = cots[y]
+    sums = jnp.broadcast_to(jnp.sum(value, axis=0, keepdims=True), (8, value.shape[1]))
+    product = dot3(summed, split(value), ((0,), (0,)))
+    pieces = extra.shape[0]
+    rows = product.shape[0] // pieces
+    for j in range(pieces):
+        extra[j, :rows, :] = product[j * rows : (j + 1) * rows, :]
+        extra[j, rows:, :] = sums
 
 
 def middle(where, mine, other, weight, bias, cot_own, cot_other):
-    width = weight.shape[1]
+    depth, width = weight.shape
     return pl.pallas_call(
         middle_kernel,
-        out_shape=(shaped(TILE, width), shaped(PAIR, width), shaped(PAIR, weight.shape[0])),
+        out_shape=(
+            shaped(TILE, width),
+            shaped(PAIR, width),
+            shaped(X * YH, depth // (X * YH) + 8, width),
+        ),
         in_specs=[SMEM] + [VMEM] * 6,
         out_specs=(VMEM,) * 3,
         scratch_shapes=[pltpu.VMEM((YL, TILE, width), jnp.float32)],
@@ -220,28 +228,6 @@
     )(where, mine, other, weight, bias, cot_own, cot_other)
 
 
-def outer_kernel(total, grad, extra):
-    value = grad[...]
-    sums = jnp.broadcast_to(jnp.sum(value, axis=0, keepdims=True), (8, value.shape[1]))
-    product = dot3(split(total[...]), split(value), ((0,), (0,)))
-    pieces = extra.shape[0]
-    rows = product.shape[0] // pieces
-    for j in range(pieces):
-        extra[j, :rows, :] = product[j * rows : (j + 1) * rows, :]
-        extra[j, rows:, :] = sums
-
-
-def outer(total, grad, pieces):
-    return pl.pallas_call(
-        outer_kernel,
-        out_shape=shaped(pieces, total.shape[1] // pieces + 8, grad.shape[1]),
-        in_specs=[VMEM] * 2,
-        out_specs=VMEM,
-        compiler_params=params(4),
-        name="outer",
-    )(total, grad)
-
-
 def spread_kernel(parts, out):
     piece = parts[0]
     for j in range(1, parts.shape[0]):
@@ -256,7 +242,7 @@
         out_shape=shaped(copies, *parts.shape[1:]),
         in_specs=[VMEM],
         out_specs=VMEM,
-        compiler_params=params(3),
+        compiler_params=params(4),
         name="spread",
     )(parts)
 
@@ -459,16 +445,17 @@
     far = (partner, x_shift(partner, -1), x_shift(partner, 2), x_shift(partner, 1))
     keep, send = forward(place, count, where, values, near, far)
     cot_other = lax.ppermute(cotangent, "col", Y_SWAP)
-    summed = scatter_z(*add_cores(keep, lax.ppermute(send, "col", CORE_SWAP)))
+    tiles = add_cores(keep, lax.ppermute(send, "col", CORE_SWAP))
+    summed = last_sum(*ring_z(tiles[0::YL]), *ring_z(tiles[1::YL]))
     summed, cot_other = lax.optimization_barrier((summed, cot_other))
     summed_other = lax.ppermute(summed, "col", Y_SWAP)
-    output, grads, total = middle(
+    output, grads, extra = middle(
         where, summed, summed_other, weight, bias.reshape(1, width), cotangent, cot_other
     )
 
     two, six = z_shift(grads, -2), z_shift(grads, 2)
     one, seven = z_shift(grads, -1), z_shift(grads, 1)
-    parts = lax.all_to_all(outer(total, grads, row_count), "row", 0, 0)
+    parts = lax.all_to_all(extra, "row", 0, 0)
     parts = lax.all_to_all(spread(parts, Z), "col", 0, 0, axis_index_groups=Z_GROUPS)
     three, five = z_shift(two, -1), z_shift(six, 1)
     low, high = halves(two, six)

time: 140 us -> 137 us (0.979)
  waiting for transfers between devices: 53 us -> 44.4 us
  starting transfers between devices: 66.7 us -> 74.1 us
  Pallas kernels: 16.3 us -> 14.5 us
    ppermute x17 -> x23, waiting for transfers between devices: 25.5 us -> 16.6 us  [the longest x22 12.4 us: z_shift(): return lax.ppermute(value, 'col', col_pairs(move))]
    ppermute x17 -> x23, starting transfers between devices: 29.5 us -> 35.3 us  [the longest x22 35.2 us: z_shift(): return lax.ppermute(value, 'col', col_pairs(move))]
    pallas_call x3 -> x2, Pallas kernels: 2.42 us -> 0.34 us  [the longest x1 0.3 us: add_cores(): pl.pallas_call(add_cores_kernel, out_shape=(shaped(*first.shape[1:]),) *...]
  transfers between devices with their start and end apart: 41 -> 47, of which waited for: 17 -> 21; matrix products, arithmetic and copies ran while one was open for 1% -> 1% of each run, Pallas kernels for 8% -> 7%
where the time goes in v5:
time: 137 us
  starting transfers between devices  74.1 us (54%)
  waiting for transfers between devices  44.4 us (32%)
  Pallas kernels  14.5 us (11%)
  local copies, waits for them, and re-layouts  1.81 us (1%)
  between operations  1.58 us (1%)
    ppermute x22, starting transfers between devices, z_shift(): return lax.ppermute(value, 'col', col_pairs(move))  35.2 us
    ppermute x12, starting transfers between devices, x_shift(): return lax.ppermute(value, 'row', row_pairs(lambda x, h: (x + distance, h)))  19.3 us
    ppermute x12, waiting for transfers between devices, x_shift(): return lax.ppermute(value, 'row', row_pairs(lambda x, h: (x + distance, h)))  13.1 us
    ppermute x22, waiting for transfers between devices, z_shift(): return lax.ppermute(value, 'col', col_pairs(move))  12.4 us
    all_to_all x1, starting transfers between devices, body(): parts = lax.all_to_all(extra, 'row', 0, 0)  6.66 us
    all_to_all x1, starting transfers between devices, body(): lax.all_to_all(spread(parts, Z), 'col', 0, 0, axis_index_groups=Z_GROUPS)  5.82 us
    ppermute x1, waiting for transfers between devices, body(): summed_other = lax.ppermute(summed, 'col', Y_SWAP)  5.69 us
    ppermute x3, waiting for transfers between devices, h_swap(): return lax.ppermute(value, 'row', row_pairs(lambda x, h: (x, 1 - h)))  4.7 us
  transfers between devices with their start and end apart: 47, of which 21 were waited for; matrix products, arithmetic and copies ran while one was open for 1% of the time, Pallas kernels for 7%

profile of v5, /device:TPU:2, one launch (start us, length us, event | category | flops | bytes accessed | tf_op | source)
XLA Modules:
  0.0 136.7 jit_solution(1002731197676589966)
XLA Ops:
  0.6 3.3 %collective-permute-start.3 = (f32[128,256]{1,0:T(8,128)}, f32[128,256]{1,0:T(8,128)}, u32[]{:S(2)}, u32[]{:S(2)}) collective-permute-start(f32[128,256]{1,0:T(8,128)} %refs_0_.1), channel_id=1, source_target_pairs={{0,32},{32,0},{64,96},{96,64},{128,160},{160,128},{192,224},{224,1... | collective-permute-start | bytes 393224 | tf_op jit(solution)/shard_map/ppermute | solution.py:59
  3.9 0.5 collective-permute-start
  4.4 2.4 %collective-permute-start.1 = (f32[128,256]{1,0:T(8,128)}, f32[128,256]{1,0:T(8,128)S(1)}, u32[]{:S(2)}, u32[]{:S(2)}) collective-permute-start(f32[128,256]{1,0:T(8,128)} %refs_0_.1), channel_id=1, source_target_pairs={{0,128},{32,160},{64,192},{96,224},{128,0},{160,32},{192,64},{224,... | collective-permute-start | bytes 393224 | tf_op jit(solution)/shard_map/ppermute | solution.py:55
  6.9 1.8 %collective-permute-start.2 = (f32[128,256]{1,0:T(8,128)}, f32[128,256]{1,0:T(8,128)S(1)}, u32[]{:S(2)}, u32[]{:S(2)}) collective-permute-start(f32[128,256]{1,0:T(8,128)} %refs_0_.1), channel_id=1, source_target_pairs={{0,64},{32,96},{64,128},{96,160},{128,192},{160,224},{192,0},{224,... | collective-permute-start | bytes 393224 | tf_op jit(solution)/shard_map/ppermute | solution.py:55
  8.7 0.8 copy.11.place
  10.5 1.3 collective-permute-start.5
  11.8 2.5 %collective-permute-start.6 = (f32[128,256]{1,0:T(8,128)}, f32[128,256]{1,0:T(8,128)}, u32[]{:S(2)}, u32[]{:S(2)}) collective-permute-start(f32[128,256]{1,0:T(8,128)} %collective-permute-done.3.a), channel_id=1, source_target_pairs={{0,64},{32,96},{64,128},{96,160},{128,192},{160,224},{192,0},{224,... | collective-permute-start | bytes 393224 | tf_op jit(solution)/shard_map/ppermute | solution.py:55
  14.3 0.9 copy-done.10
  15.3 3.4 %collective-permute-done.4.b = f32[128,256]{1,0:T(8,128)} collective-permute-done((f32[128,256]{1,0:T(8,128)}, f32[128,256]{1,0:T(8,128)}, u32[]{:S(2)}, u32[]{:S(2)}) %collective-permute-start.4) | collective-permute-done | bytes 131104 | tf_op jit(solution)/shard_map/ppermute | solution.py:55
  18.6 0.8 collective-permute-done.6.d
  19.4 2.4 %forward_tiles.1 = (f32[16,128,256]{2,1,0:T(8,128)S(1)}, f32[16,128,256]{2,1,0:T(8,128)S(1)}) custom-call(s32[12,2]{1,0:T(8,128)S(1)} %copy.11.place, s32[1]{0:T(128)} %bitcast.10.count, s32[5]{0:T(128)S(1)} %stack.23.where, f32[12,128,128]{2,1,0:T(8,128)S(1)} %bitcast.12, bf16[4,128,256]{2,1,0:T(8,128)(2,1)S(1)} %get-tuple-element.49.near_high, ...), custom_call_target="tpu_custom_call" | custom-call | tf_op jit(solution)/shard_map/forward_tiles/pallas_call | solution.py:138
  21.9 4.1 %collective-permute-done.7.second = f32[16,128,256]{2,1,0:T(8,128)S(1)} collective-permute-done((f32[16,128,256]{2,1,0:T(8,128)S(1)}, f32[16,128,256]{2,1,0:T(8,128)S(1)}, u32[]{:S(2)}, u32[]{:S(2)}) %collective-permute-start.7) | collective-permute-done | bytes 2097184 | tf_op jit(solution)/shard_map/ppermute | solution.py:448
  26.4 2.0 %collective-permute-start.8 = (f32[128,256]{1,0:T(8,128)S(1)}, f32[128,256]{1,0:T(8,128)S(1)}, u32[]{:S(2)}, u32[]{:S(2)}) collective-permute-start(f32[128,256]{1,0:T(8,128)S(1)} %get-tuple-element.57), channel_id=1, source_target_pairs={{0,4},{1,29},{2,6},{3,31},{4,8},{5,1},{6,10},{7,3},{8,12},{9,5},{1... | collective-permute-start | bytes 393224 | tf_op jit(solution)/shard_map/ppermute | solution.py:42
  28.4 1.9 %collective-permute-start.15 = (f32[128,256]{1,0:T(8,128)S(1)}, f32[128,256]{1,0:T(8,128)S(1)}, u32[]{:S(2)}, u32[]{:S(2)}) collective-permute-start(f32[128,256]{1,0:T(8,128)S(1)} %get-tuple-element.65), channel_id=1, source_target_pairs={{0,4},{1,29},{2,6},{3,31},{4,8},{5,1},{6,10},{7,3},{8,12},{9,5},{1... | collective-permute-start | bytes 393224 | tf_op jit(solution)/shard_map/ppermute | solution.py:42
  30.3 2.2 %collective-permute-start.12 = (f32[128,256]{1,0:T(8,128)S(1)}, f32[128,256]{1,0:T(8,128)S(1)}, u32[]{:S(2)}, u32[]{:S(2)}) collective-permute-start(f32[128,256]{1,0:T(8,128)S(1)} %get-tuple-element.60), channel_id=1, source_target_pairs={{0,28},{1,5},{2,30},{3,7},{4,0},{5,9},{6,2},{7,11},{8,4},{9,13},{1... | collective-permute-start | bytes 393224 | tf_op jit(solution)/shard_map/ppermute | solution.py:42
  32.5 1.9 %collective-permute-start.19 = (f32[128,256]{1,0:T(8,128)S(1)}, f32[128,256]{1,0:T(8,128)S(1)}, u32[]{:S(2)}, u32[]{:S(2)}) collective-permute-start(f32[128,256]{1,0:T(8,128)S(1)} %get-tuple-element.68), channel_id=1, source_target_pairs={{0,28},{1,5},{2,30},{3,7},{4,0},{5,9},{6,2},{7,11},{8,4},{9,13},{1... | collective-permute-start | bytes 393224 | tf_op jit(solution)/shard_map/ppermute | solution.py:42
  34.4 0.8 collective-permute-done.8
  35.4 1.3 collective-permute-done.15
  36.8 4.5 %collective-permute-start.13 = (f32[128,256]{1,0:T(8,128)S(1)}, f32[128,256]{1,0:T(8,128)S(1)}, u32[]{:S(2)}, u32[]{:S(2)}) collective-permute-start(f32[128,256]{1,0:T(8,128)S(1)} %add.36), channel_id=1, source_target_pairs={{0,28},{1,5},{2,30},{3,7},{4,0},{5,9},{6,2},{7,11},{8,4},{9,13},{1... | collective-permute-start | bytes 393224 | tf_op jit(solution)/shard_map/ppermute | solution.py:42
  41.4 2.1 %collective-permute-start.20 = (f32[128,256]{1,0:T(8,128)S(1)}, f32[128,256]{1,0:T(8,128)S(1)}, u32[]{:S(2)}, u32[]{:S(2)}) collective-permute-start(f32[128,256]{1,0:T(8,128)S(1)} %add.41), channel_id=1, source_target_pairs={{0,28},{1,5},{2,30},{3,7},{4,0},{5,9},{6,2},{7,11},{8,4},{9,13},{1... | collective-permute-start | bytes 393224 | tf_op jit(solution)/shard_map/ppermute | solution.py:42
  44.0 0.5 collective-permute-start.17
  44.5 3.3 %collective-permute-start.14 = (f32[128,256]{1,0:T(8,128)S(1)}, f32[128,256]{1,0:T(8,128)S(1)}, u32[]{:S(2)}, u32[]{:S(2)}) collective-permute-start(f32[128,256]{1,0:T(8,128)S(1)} %add.37), channel_id=1, source_target_pairs={{0,28},{1,5},{2,30},{3,7},{4,0},{5,9},{6,2},{7,11},{8,4},{9,13},{1... | collective-permute-start | bytes 393224 | tf_op jit(solution)/shard_map/ppermute | solution.py:42
  47.8 3.3 %collective-permute-start.21 = (f32[128,256]{1,0:T(8,128)S(1)}, f32[128,256]{1,0:T(8,128)S(1)}, u32[]{:S(2)}, u32[]{:S(2)}) collective-permute-start(f32[128,256]{1,0:T(8,128)S(1)} %add.42), channel_id=1, source_target_pairs={{0,28},{1,5},{2,30},{3,7},{4,0},{5,9},{6,2},{7,11},{8,4},{9,13},{1... | collective-permute-start | bytes 393224 | tf_op jit(solution)/shard_map/ppermute | solution.py:42
  51.3 0.7 collective-permute-done.17
  52.1 0.8 collective-permute-start.22
  52.9 2.2 %collective-permute-done.21.refs_5_ = f32[128,256]{1,0:T(8,128)S(1)} collective-permute-done((f32[128,256]{1,0:T(8,128)S(1)}, f32[128,256]{1,0:T(8,128)S(1)}, u32[]{:S(2)}, u32[]{:S(2)}) %collective-permute-start.21) | collective-permute-done | bytes 131104 | tf_op jit(solution)/shard_map/ppermute | solution.py:42
  55.0 2.4 %collective-permute-done.11.refs_1_ = f32[128,256]{1,0:T(8,128)S(1)} collective-permute-done((f32[128,256]{1,0:T(8,128)S(1)}, f32[128,256]{1,0:T(8,128)S(1)}, u32[]{:S(2)}, u32[]{:S(2)}) %collective-permute-start.11) | collective-permute-done | bytes 131104 | tf_op jit(solution)/shard_map/ppermute | solution.py:42
  57.4 1.4 %collective-permute-done.18.refs_4_ = f32[128,256]{1,0:T(8,128)S(1)} collective-permute-done((f32[128,256]{1,0:T(8,128)S(1)}, f32[128,256]{1,0:T(8,128)S(1)}, u32[]{:S(2)}, u32[]{:S(2)}) %collective-permute-start.18) | collective-permute-done | bytes 131104 | tf_op jit(solution)/shard_map/ppermute | solution.py:42
  58.9 0.8 collective-permute-start.23
  59.6 5.7 %collective-permute-done.23.other = f32[256,256]{1,0:T(8,128)S(1)} collective-permute-done((f32[256,256]{1,0:T(8,128)S(1)}, f32[256,256]{1,0:T(8,128)S(1)}, u32[]{:S(2)}, u32[]{:S(2)}) %collective-permute-start.23) | collective-permute-done | bytes 262176 | tf_op jit(solution)/shard_map/ppermute | solution.py:451
  65.3 2.0 %middle.1 = (f32[128,256]{1,0:T(8,128)}, f32[256,256]{1,0:T(8,128)}, f32[8,40,256]{2,1,0:T(8,128)}) custom-call(s32[5]{0:T(128)S(1)} %stack.23.where, f32[256,256]{1,0:T(8,128)S(1)} %last_sum.1.mine, f32[256,256]{1,0:T(8,128)S(1)} %collective-permute-done.23.other, f32[256,256]{1,0:T(8,128)S(1)} %copy-done.2, f32[1,256]{1,0:T(1,128)S(1)} %bitcast.14, ...), custom_call_target="tpu_custom_call" | custom-call | tf_op jit(solution)/shard_map/middle/pallas_call | solution.py:216
  67.3 2.6 %collective-permute-start.25 = (f32[256,256]{1,0:T(8,128)}, f32[256,256]{1,0:T(8,128)}, u32[]{:S(2)}, u32[]{:S(2)}) collective-permute-start(f32[256,256]{1,0:T(8,128)} %get-tuple-element.72.refs_0_), channel_id=1, source_target_pairs={{0,24},{1,9},{2,26},{3,11},{4,28},{5,13},{6,30},{7,15},{8,0},{9,17... | collective-permute-start | bytes 786440 | tf_op jit(solution)/shard_map/ppermute | solution.py:42
  69.9 2.0 %collective-permute-start.27 = (f32[256,256]{1,0:T(8,128)}, f32[256,256]{1,0:T(8,128)}, u32[]{:S(2)}, u32[]{:S(2)}) collective-permute-start(f32[256,256]{1,0:T(8,128)} %get-tuple-element.72.refs_0_), channel_id=1, source_target_pairs={{0,8},{1,25},{2,10},{3,27},{4,12},{5,29},{6,14},{7,31},{8,16},{9,1... | collective-permute-start | bytes 786440 | tf_op jit(solution)/shard_map/ppermute | solution.py:42
  71.9 1.4 %collective-permute-start.24 = (f32[256,256]{1,0:T(8,128)}, f32[256,256]{1,0:T(8,128)}, u32[]{:S(2)}, u32[]{:S(2)}) collective-permute-start(f32[256,256]{1,0:T(8,128)} %get-tuple-element.72.refs_0_), channel_id=1, source_target_pairs={{0,28},{1,5},{2,30},{3,7},{4,0},{5,9},{6,2},{7,11},{8,4},{9,13},{1... | collective-permute-start | bytes 786440 | tf_op jit(solution)/shard_map/ppermute | solution.py:42
  73.3 0.6 collective-permute-start.31
  73.9 6.7 %all-to-all-start = ((f32[8,40,256]{2,1,0:T(8,128)}), f32[8,40,256]{2,1,0:T(8,128)}, u32[]{:S(2)}, u32[]{:S(2)}) async-start(f32[8,40,256]{2,1,0:T(8,128)} %get-tuple-element.83), calls=%async_computation | async-start | bytes 655360 | tf_op jit(solution)/shard_map/all_to_all | solution.py:458
  80.6 3.2 %collective-permute-done.25.two.refs_2_ = f32[256,256]{1,0:T(8,128)} collective-permute-done((f32[256,256]{1,0:T(8,128)}, f32[256,256]{1,0:T(8,128)}, u32[]{:S(2)}, u32[]{:S(2)}) %collective-permute-start.25) | collective-permute-done | bytes 262176 | tf_op jit(solution)/shard_map/ppermute | solution.py:42
  83.8 2.0 %collective-permute-start.30 = (f32[256,256]{1,0:T(8,128)}, f32[256,256]{1,0:T(8,128)}, u32[]{:S(2)}, u32[]{:S(2)}) collective-permute-start(f32[256,256]{1,0:T(8,128)} %collective-permute-done.27.six.refs_7_), channel_id=1, source_target_pairs={{0,4},{1,29},{2,6},{3,31},{4,8},{5,1},{6,10},{7,3},{8,12},{9,5},{1... | collective-permute-start | bytes 786440 | tf_op jit(solution)/shard_map/ppermute | solution.py:42
  85.8 1.0 halves.1
  86.9 2.9 %collective-permute-start.28 = (f32[128,256]{1,0:T(8,128)S(1)}, f32[128,256]{1,0:T(8,128)S(1)}, u32[]{:S(2)}, u32[]{:S(2)}) collective-permute-start(f32[128,256]{1,0:T(8,128)S(1)} %get-tuple-element.73), channel_id=1, source_target_pairs={{0,8},{1,25},{2,10},{3,27},{4,12},{5,29},{6,14},{7,31},{8,16},{9,1... | collective-permute-start | bytes 393224 | tf_op jit(solution)/shard_map/ppermute | solution.py:42
  89.8 1.6 %collective-permute-start.29 = (f32[128,256]{1,0:T(8,128)S(1)}, f32[128,256]{1,0:T(8,128)S(1)}, u32[]{:S(2)}, u32[]{:S(2)}) collective-permute-start(f32[128,256]{1,0:T(8,128)S(1)} %get-tuple-element.74), channel_id=1, source_target_pairs={{0,24},{1,9},{2,26},{3,11},{4,28},{5,13},{6,30},{7,15},{8,0},{9,17... | collective-permute-start | bytes 393224 | tf_op jit(solution)/shard_map/ppermute | solution.py:42
  91.3 1.7 %spread.1 = f32[8,40,256]{2,1,0:T(8,128)} custom-call(f32[8,40,256]{2,1,0:T(8,128)} %all-to-all-done.parts), custom_call_target="tpu_custom_call" | custom-call | tf_op jit(solution)/shard_map/spread/pallas_call | solution.py:240
  93.1 5.8 %all-to-all-start.1 = ((f32[8,40,256]{2,1,0:T(8,128)}), f32[8,40,256]{2,1,0:T(8,128)}, u32[]{:S(2)}, u32[]{:S(2)}) async-start(f32[8,40,256]{2,1,0:T(8,128)} %spread.1), calls=%async_computation.1 | async-start | bytes 655360 | tf_op jit(solution)/shard_map/all_to_all | solution.py:459
  99.0 1.6 %join.1 = (f32[512,256]{1,0:T(8,128)S(1)}, f32[512,256]{1,0:T(8,128)S(1)}, f32[512,256]{1,0:T(8,128)S(1)}, f32[512,256]{1,0:T(8,128)S(1)}) custom-call(f32[256,256]{1,0:T(8,128)} %get-tuple-element.72.refs_0_, f32[256,256]{1,0:T(8,128)} %collective-permute-done.24.refs_1_, f32[256,256]{1,0:T(8,128)} %collective-permute-done.25.two.refs_2_, ...), custom_call_target="tpu_custom_call" | custom-call | flops 999999995904 | tf_op jit(solution)/shard_map/join/pallas_call | solution.py:278
  100.7 0.5 collective-permute-start.33
  101.7 0.9 collective-permute-done.32.refs_4_
  102.6 0.7 collective-permute-done.33.refs_5_
  103.4 0.7 collective-permute-done.34.refs_6_
  104.1 0.7 collective-permute-done.35.refs_7_
  104.9 2.0 %backward_tiles.1 = (f32[128,256]{1,0:T(8,128)S(1)}, f32[128,256]{1,0:T(8,128)S(1)}, f32[128,256]{1,0:T(8,128)S(1)}, f32[128,256]{1,0:T(8,128)S(1)}, f32[128,256...) custom-call(s32[12,2]{1,0:T(8,128)S(1)} %copy-done.6, ...), custom_call_target="tpu_custom_call" | custom-call | tf_op jit(solution)/shard_map/backward_tiles/pallas_call | solution.py:328
  106.9 1.5 %collective-permute-start.41 = (f32[128,256]{1,0:T(8,128)S(1)}, f32[128,256]{1,0:T(8,128)S(1)}, u32[]{:S(2)}, u32[]{:S(2)}) collective-permute-start(f32[128,256]{1,0:T(8,128)S(1)} %get-tuple-element.89), channel_id=1, source_target_pairs={{0,64},{32,96},{64,128},{96,160},{128,192},{160,224},{192,0},{224,... | collective-permute-start | bytes 393224 | tf_op jit(solution)/shard_map/ppermute | solution.py:55
  108.4 4.7 %collective-permute-start.42 = (f32[128,256]{1,0:T(8,128)S(1)}, f32[128,256]{1,0:T(8,128)S(1)}, u32[]{:S(2)}, u32[]{:S(2)}) collective-permute-start(f32[128,256]{1,0:T(8,128)S(1)} %get-tuple-element.90), channel_id=1, source_target_pairs={{0,128},{32,160},{64,192},{96,224},{128,0},{160,32},{192,64},{224,... | collective-permute-start | bytes 393224 | tf_op jit(solution)/shard_map/ppermute | solution.py:55
  113.1 1.0 total.1
  114.2 1.2 collective-permute-done.36
  115.4 0.8 collective-permute-start.37
  116.2 4.7 %collective-permute-done.37.piece_across = f32[40,256]{1,0:T(8,128)S(1)} collective-permute-done((f32[40,256]{1,0:T(8,128)S(1)}, f32[40,256]{1,0:T(8,128)S(1)}, u32[]{:S(2)}, u32[]{:S(2)}) %collective-permute-start.37) | collective-permute-done | bytes 40992 | tf_op jit(solution)/shard_map/ppermute | solution.py:59
  120.9 2.1 %collective-permute-start.38 = (f32[208,256]{1,0:T(8,128)S(1)}, f32[208,256]{1,0:T(8,128)S(1)}, u32[]{:S(2)}, u32[]{:S(2)}) collective-permute-start(f32[208,256]{1,0:T(8,128)S(1)} %get-tuple-element.84), channel_id=1, source_target_pairs={{0,64},{32,96},{64,128},{96,160},{128,192},{160,224},{192,0},{224,... | collective-permute-start | bytes 638984 | tf_op jit(solution)/shard_map/ppermute | solution.py:55
  123.0 1.2 collective-permute-start.39
  124.3 1.0 collective-permute-start.40
  125.5 5.8 %collective-permute-done.38.one = f32[208,256]{1,0:T(8,128)S(1)} collective-permute-done((f32[208,256]{1,0:T(8,128)S(1)}, f32[208,256]{1,0:T(8,128)S(1)}, u32[]{:S(2)}, u32[]{:S(2)}) %collective-permute-start.38) | collective-permute-done | bytes 213024 | tf_op jit(solution)/shard_map/ppermute | solution.py:55
  131.3 1.4 %collective-permute-done.39.two = f32[208,256]{1,0:T(8,128)S(1)} collective-permute-done((f32[208,256]{1,0:T(8,128)S(1)}, f32[208,256]{1,0:T(8,128)S(1)}, u32[]{:S(2)}, u32[]{:S(2)}) %collective-permute-start.39) | collective-permute-done | bytes 213024 | tf_op jit(solution)/shard_map/ppermute | solution.py:55
  132.7 1.7 %collective-permute-done.40.three = f32[208,256]{1,0:T(8,128)S(1)} collective-permute-done((f32[208,256]{1,0:T(8,128)S(1)}, f32[208,256]{1,0:T(8,128)S(1)}, u32[]{:S(2)}, u32[]{:S(2)}) %collective-permute-start.40) | collective-permute-done | bytes 213024 | tf_op jit(solution)/shard_map/ppermute | solution.py:55
  134.4 1.3 unpack.1
  135.7 0.9 final.1
  (79 shorter events, 3.0 us)
Async XLA Ops:
  0.6 9.6 %collective-permute-start.3 = (f32[128,256]{1,0:T(8,128)}, f32[128,256]{1,0:T(8,128)}, u32[]{:S(2)}, u32[]{:S(2)}) collective-permute-start(f32[128,256]{1,0:T(8,128)} %refs_0_.1), channel_id=1, source_target_pairs={{0,32},{32,0},{64,96},{96,64},{128,160},{160,128},{192,224},{224,1... | collective-permute-start | bytes 393224 | tf_op jit(solution)/shard_map/ppermute | solution.py:59
  3.9 7.9 %collective-permute-start = (f32[128,256]{1,0:T(8,128)}, f32[128,256]{1,0:T(8,128)S(1)}, u32[]{:S(2)}, u32[]{:S(2)}) collective-permute-start(f32[128,256]{1,0:T(8,128)} %refs_0_.1), channel_id=1, source_target_pairs={{0,192},{32,224},{64,0},{96,32},{128,64},{160,96},{192,128},{224,1... | collective-permute-start | bytes 393224 | tf_op jit(solution)/shard_map/ppermute | solution.py:55
  4.4 9.9 %collective-permute-start.1 = (f32[128,256]{1,0:T(8,128)}, f32[128,256]{1,0:T(8,128)S(1)}, u32[]{:S(2)}, u32[]{:S(2)}) collective-permute-start(f32[128,256]{1,0:T(8,128)} %refs_0_.1), channel_id=1, source_target_pairs={{0,128},{32,160},{64,192},{96,224},{128,0},{160,32},{192,64},{224,... | collective-permute-start | bytes 393224 | tf_op jit(solution)/shard_map/ppermute | solution.py:55
  6.9 7.4 %collective-permute-start.2 = (f32[128,256]{1,0:T(8,128)}, f32[128,256]{1,0:T(8,128)S(1)}, u32[]{:S(2)}, u32[]{:S(2)}) collective-permute-start(f32[128,256]{1,0:T(8,128)} %refs_0_.1), channel_id=1, source_target_pairs={{0,64},{32,96},{64,128},{96,160},{128,192},{160,224},{192,0},{224,... | collective-permute-start | bytes 393224 | tf_op jit(solution)/shard_map/ppermute | solution.py:55
  9.4 10.0 %copy-start.5 = (s32[12,2]{1,0:T(8,128)}, s32[12,2]{1,0:T(8,128)S(1)}, u32[]{:S(2)}) copy-start(s32[12,2]{1,0:T(8,128)S(1)} %copy.11.place) | copy-start | bytes 292
  10.2 55.2 %copy-start.7 = (s32[5]{0:T(128)}, s32[5]{0:T(128)S(1)}, u32[]{:S(2)}) copy-start(s32[5]{0:T(128)S(1)} %stack.23.where) | copy-start | bytes 64
  10.2 8.5 %collective-permute-start.4 = (f32[128,256]{1,0:T(8,128)}, f32[128,256]{1,0:T(8,128)}, u32[]{:S(2)}, u32[]{:S(2)}) collective-permute-start(f32[128,256]{1,0:T(8,128)} %collective-permute-done.3.a), channel_id=1, source_target_pairs={{0,192},{32,224},{64,0},{96,32},{128,64},{160,96},{192,128},{224,1... | collective-permute-start | bytes 393224 | tf_op jit(solution)/shard_map/ppermute | solution.py:55
  10.5 8.2 %collective-permute-start.5 = (f32[128,256]{1,0:T(8,128)}, f32[128,256]{1,0:T(8,128)}, u32[]{:S(2)}, u32[]{:S(2)}) collective-permute-start(f32[128,256]{1,0:T(8,128)} %collective-permute-done.3.a), channel_id=1, source_target_pairs={{0,128},{32,160},{64,192},{96,224},{128,0},{160,32},{192,64},{224,... | collective-permute-start | bytes 393224 | tf_op jit(solution)/shard_map/ppermute | solution.py:55
  11.8 7.7 %collective-permute-start.6 = (f32[128,256]{1,0:T(8,128)}, f32[128,256]{1,0:T(8,128)}, u32[]{:S(2)}, u32[]{:S(2)}) collective-permute-start(f32[128,256]{1,0:T(8,128)} %collective-permute-done.3.a), channel_id=1, source_target_pairs={{0,64},{32,96},{64,128},{96,160},{128,192},{160,224},{192,0},{224,... | collective-permute-start | bytes 393224 | tf_op jit(solution)/shard_map/ppermute | solution.py:55
  14.3 0.9 copy-start.10
  15.2 4.2 %copy-start = (f32[1,1,12,128,128]{4,3,2,1,0:T(8,128)S(1)}, f32[1,1,12,128,128]{4,3,2,1,0:T(8,128)}, u32[]{:S(2)}) copy-start(f32[1,1,12,128,128]{4,3,2,1,0:T(8,128)} %param.10) | copy-start | bytes 2359300
  21.8 4.2 %collective-permute-start.7 = (f32[16,128,256]{2,1,0:T(8,128)S(1)}, f32[16,128,256]{2,1,0:T(8,128)S(1)}, u32[]{:S(2)}, u32[]{:S(2)}) collective-permute-start(f32[16,128,256]{2,1,0:T(8,128)S(1)} %get-tuple-element.52), channel_id=1, source_target_pairs={{0,1},{1,0},{2,3},{3,2},{4,5},{5,4},{6,7},{7,6},{8,9},{9,8},{10,11... | collective-permute-start | bytes 6291464 | tf_op jit(solution)/shard_map/ppermute | solution.py:448
  26.4 25.7 %copy-start.4 = (f32[128,256]{1,0:T(8,128)S(1)}, f32[128,256]{1,0:T(8,128)}, u32[]{:S(2)}) copy-start(f32[128,256]{1,0:T(8,128)} %cot_own.1) | copy-start | bytes 393220
  26.4 8.9 %collective-permute-start.8 = (f32[128,256]{1,0:T(8,128)S(1)}, f32[128,256]{1,0:T(8,128)S(1)}, u32[]{:S(2)}, u32[]{:S(2)}) collective-permute-start(f32[128,256]{1,0:T(8,128)S(1)} %get-tuple-element.57), channel_id=1, source_target_pairs={{0,4},{1,29},{2,6},{3,31},{4,8},{5,1},{6,10},{7,3},{8,12},{9,5},{1... | collective-permute-start | bytes 393224 | tf_op jit(solution)/shard_map/ppermute | solution.py:42
  28.4 8.3 %collective-permute-start.15 = (f32[128,256]{1,0:T(8,128)S(1)}, f32[128,256]{1,0:T(8,128)S(1)}, u32[]{:S(2)}, u32[]{:S(2)}) collective-permute-start(f32[128,256]{1,0:T(8,128)S(1)} %get-tuple-element.65), channel_id=1, source_target_pairs={{0,4},{1,29},{2,6},{3,31},{4,8},{5,1},{6,10},{7,3},{8,12},{9,5},{1... | collective-permute-start | bytes 393224 | tf_op jit(solution)/shard_map/ppermute | solution.py:42
  30.3 6.5 %collective-permute-start.12 = (f32[128,256]{1,0:T(8,128)S(1)}, f32[128,256]{1,0:T(8,128)S(1)}, u32[]{:S(2)}, u32[]{:S(2)}) collective-permute-start(f32[128,256]{1,0:T(8,128)S(1)} %get-tuple-element.60), channel_id=1, source_target_pairs={{0,28},{1,5},{2,30},{3,7},{4,0},{5,9},{6,2},{7,11},{8,4},{9,13},{1... | collective-permute-start | bytes 393224 | tf_op jit(solution)/shard_map/ppermute | solution.py:42
  32.5 8.9 %collective-permute-start.19 = (f32[128,256]{1,0:T(8,128)S(1)}, f32[128,256]{1,0:T(8,128)S(1)}, u32[]{:S(2)}, u32[]{:S(2)}) collective-permute-start(f32[128,256]{1,0:T(8,128)S(1)} %get-tuple-element.68), channel_id=1, source_target_pairs={{0,28},{1,5},{2,30},{3,7},{4,0},{5,9},{6,2},{7,11},{8,4},{9,13},{1... | collective-permute-start | bytes 393224 | tf_op jit(solution)/shard_map/ppermute | solution.py:42
  35.3 8.2 %collective-permute-start.9 = (f32[128,256]{1,0:T(8,128)S(1)}, f32[128,256]{1,0:T(8,128)S(1)}, u32[]{:S(2)}, u32[]{:S(2)}) collective-permute-start(f32[128,256]{1,0:T(8,128)S(1)} %add.33), channel_id=1, source_target_pairs={{0,4},{1,29},{2,6},{3,31},{4,8},{5,1},{6,10},{7,3},{8,12},{9,5},{1... | collective-permute-start | bytes 393224 | tf_op jit(solution)/shard_map/ppermute | solution.py:42
  36.7 7.3 %collective-permute-start.16 = (f32[128,256]{1,0:T(8,128)S(1)}, f32[128,256]{1,0:T(8,128)S(1)}, u32[]{:S(2)}, u32[]{:S(2)}) collective-permute-start(f32[128,256]{1,0:T(8,128)S(1)} %add.38), channel_id=1, source_target_pairs={{0,4},{1,29},{2,6},{3,31},{4,8},{5,1},{6,10},{7,3},{8,12},{9,5},{1... | collective-permute-start | bytes 393224 | tf_op jit(solution)/shard_map/ppermute | solution.py:42
  36.8 28.5 %copy-start.2 = (f32[256,256]{1,0:T(8,128)S(1)}, f32[256,256]{1,0:T(8,128)}, u32[]{:S(2)}) copy-start(f32[256,256]{1,0:T(8,128)} %weight.3) | copy-start | bytes 786436
  36.8 28.5 %copy-start.9 = (f32[256]{0:T(256)S(1)}, f32[256]{0:T(256)}, u32[]{:S(2)}) copy-start(f32[256]{0:T(256)} %param.9) | copy-start | bytes 3076
  36.8 7.6 %collective-permute-start.13 = (f32[128,256]{1,0:T(8,128)S(1)}, f32[128,256]{1,0:T(8,128)S(1)}, u32[]{:S(2)}, u32[]{:S(2)}) collective-permute-start(f32[128,256]{1,0:T(8,128)S(1)} %add.36), channel_id=1, source_target_pairs={{0,28},{1,5},{2,30},{3,7},{4,0},{5,9},{6,2},{7,11},{8,4},{9,13},{1... | collective-permute-start | bytes 393224 | tf_op jit(solution)/shard_map/ppermute | solution.py:42
  41.4 6.4 %collective-permute-start.20 = (f32[128,256]{1,0:T(8,128)S(1)}, f32[128,256]{1,0:T(8,128)S(1)}, u32[]{:S(2)}, u32[]{:S(2)}) collective-permute-start(f32[128,256]{1,0:T(8,128)S(1)} %add.41), channel_id=1, source_target_pairs={{0,28},{1,5},{2,30},{3,7},{4,0},{5,9},{6,2},{7,11},{8,4},{9,13},{1... | collective-permute-start | bytes 393224 | tf_op jit(solution)/shard_map/ppermute | solution.py:42
  43.5 7.7 %collective-permute-start.10 = (f32[128,256]{1,0:T(8,128)S(1)}, f32[128,256]{1,0:T(8,128)S(1)}, u32[]{:S(2)}, u32[]{:S(2)}) collective-permute-start(f32[128,256]{1,0:T(8,128)S(1)} %add.34), channel_id=1, source_target_pairs={{0,4},{1,29},{2,6},{3,31},{4,8},{5,1},{6,10},{7,3},{8,12},{9,5},{1... | collective-permute-start | bytes 393224 | tf_op jit(solution)/shard_map/ppermute | solution.py:42
  44.0 8.0 %collective-permute-start.17 = (f32[128,256]{1,0:T(8,128)S(1)}, f32[128,256]{1,0:T(8,128)S(1)}, u32[]{:S(2)}, u32[]{:S(2)}) collective-permute-start(f32[128,256]{1,0:T(8,128)S(1)} %add.39), channel_id=1, source_target_pairs={{0,4},{1,29},{2,6},{3,31},{4,8},{5,1},{6,10},{7,3},{8,12},{9,5},{1... | collective-permute-start | bytes 393224 | tf_op jit(solution)/shard_map/ppermute | solution.py:42
  44.5 8.4 %collective-permute-start.14 = (f32[128,256]{1,0:T(8,128)S(1)}, f32[128,256]{1,0:T(8,128)S(1)}, u32[]{:S(2)}, u32[]{:S(2)}) collective-permute-start(f32[128,256]{1,0:T(8,128)S(1)} %add.37), channel_id=1, source_target_pairs={{0,28},{1,5},{2,30},{3,7},{4,0},{5,9},{6,2},{7,11},{8,4},{9,13},{1... | collective-permute-start | bytes 393224 | tf_op jit(solution)/shard_map/ppermute | solution.py:42
  47.8 7.2 %collective-permute-start.21 = (f32[128,256]{1,0:T(8,128)S(1)}, f32[128,256]{1,0:T(8,128)S(1)}, u32[]{:S(2)}, u32[]{:S(2)}) collective-permute-start(f32[128,256]{1,0:T(8,128)S(1)} %add.42), channel_id=1, source_target_pairs={{0,28},{1,5},{2,30},{3,7},{4,0},{5,9},{6,2},{7,11},{8,4},{9,13},{1... | collective-permute-start | bytes 393224 | tf_op jit(solution)/shard_map/ppermute | solution.py:42
  51.2 6.3 %collective-permute-start.11 = (f32[128,256]{1,0:T(8,128)S(1)}, f32[128,256]{1,0:T(8,128)S(1)}, u32[]{:S(2)}, u32[]{:S(2)}) collective-permute-start(f32[128,256]{1,0:T(8,128)S(1)} %add.35), channel_id=1, source_target_pairs={{0,4},{1,29},{2,6},{3,31},{4,8},{5,1},{6,10},{7,3},{8,12},{9,5},{1... | collective-permute-start | bytes 393224 | tf_op jit(solution)/shard_map/ppermute | solution.py:42
  52.0 6.8 %collective-permute-start.18 = (f32[128,256]{1,0:T(8,128)S(1)}, f32[128,256]{1,0:T(8,128)S(1)}, u32[]{:S(2)}, u32[]{:S(2)}) collective-permute-start(f32[128,256]{1,0:T(8,128)S(1)} %add.40), channel_id=1, source_target_pairs={{0,4},{1,29},{2,6},{3,31},{4,8},{5,1},{6,10},{7,3},{8,12},{9,5},{1... | collective-permute-start | bytes 393224 | tf_op jit(solution)/shard_map/ppermute | solution.py:42
  52.1 6.8 %collective-permute-start.22 = (f32[128,256]{1,0:T(8,128)S(1)}, f32[128,256]{1,0:T(8,128)S(1)}, u32[]{:S(2)}, u32[]{:S(2)}) collective-permute-start(f32[128,256]{1,0:T(8,128)S(1)} %copy-done.4), channel_id=1, source_target_pairs={{0,2},{1,3},{2,0},{3,1},{4,6},{5,7},{6,4},{7,5},{8,10},{9,11},{10,... | collective-permute-start | bytes 393224 | tf_op jit(solution)/shard_map/ppermute | solution.py:447
  58.9 6.5 %collective-permute-start.23 = (f32[256,256]{1,0:T(8,128)S(1)}, f32[256,256]{1,0:T(8,128)S(1)}, u32[]{:S(2)}, u32[]{:S(2)}) collective-permute-start(f32[256,256]{1,0:T(8,128)S(1)} %last_sum.1.mine), channel_id=1, source_target_pairs={{0,2},{1,3},{2,0},{3,1},{4,6},{5,7},{6,4},{7,5},{8,10},{9,11},{10,... | collective-permute-start | bytes 786440 | tf_op jit(solution)/shard_map/ppermute | solution.py:451
  67.3 16.5 %collective-permute-start.25 = (f32[256,256]{1,0:T(8,128)}, f32[256,256]{1,0:T(8,128)}, u32[]{:S(2)}, u32[]{:S(2)}) collective-permute-start(f32[256,256]{1,0:T(8,128)} %get-tuple-element.72.refs_0_), channel_id=1, source_target_pairs={{0,24},{1,9},{2,26},{3,11},{4,28},{5,13},{6,30},{7,15},{8,0},{9,17... | collective-permute-start | bytes 786440 | tf_op jit(solution)/shard_map/ppermute | solution.py:42
  69.9 13.9 %collective-permute-start.27 = (f32[256,256]{1,0:T(8,128)}, f32[256,256]{1,0:T(8,128)}, u32[]{:S(2)}, u32[]{:S(2)}) collective-permute-start(f32[256,256]{1,0:T(8,128)} %get-tuple-element.72.refs_0_), channel_id=1, source_target_pairs={{0,8},{1,25},{2,10},{3,27},{4,12},{5,29},{6,14},{7,31},{8,16},{9,1... | collective-permute-start | bytes 786440 | tf_op jit(solution)/shard_map/ppermute | solution.py:42
  71.9 17.9 %collective-permute-start.24 = (f32[256,256]{1,0:T(8,128)}, f32[256,256]{1,0:T(8,128)}, u32[]{:S(2)}, u32[]{:S(2)}) collective-permute-start(f32[256,256]{1,0:T(8,128)} %get-tuple-element.72.refs_0_), channel_id=1, source_target_pairs={{0,28},{1,5},{2,30},{3,7},{4,0},{5,9},{6,2},{7,11},{8,4},{9,13},{1... | collective-permute-start | bytes 786440 | tf_op jit(solution)/shard_map/ppermute | solution.py:42
  73.3 25.5 %collective-permute-start.31 = (f32[256,256]{1,0:T(8,128)}, f32[256,256]{1,0:T(8,128)}, u32[]{:S(2)}, u32[]{:S(2)}) collective-permute-start(f32[256,256]{1,0:T(8,128)} %get-tuple-element.72.refs_0_), channel_id=1, source_target_pairs={{0,4},{1,29},{2,6},{3,31},{4,8},{5,1},{6,10},{7,3},{8,12},{9,5},{1... | collective-permute-start | bytes 786440 | tf_op jit(solution)/shard_map/ppermute | solution.py:42
  73.9 17.4 %all-to-all-start = ((f32[8,40,256]{2,1,0:T(8,128)}), f32[8,40,256]{2,1,0:T(8,128)}, u32[]{:S(2)}, u32[]{:S(2)}) async-start(f32[8,40,256]{2,1,0:T(8,128)} %get-tuple-element.83), calls=%async_computation | async-start | bytes 655360 | tf_op jit(solution)/shard_map/all_to_all | solution.py:458
  83.8 15.1 %collective-permute-start.26 = (f32[256,256]{1,0:T(8,128)}, f32[256,256]{1,0:T(8,128)}, u32[]{:S(2)}, u32[]{:S(2)}) collective-permute-start(f32[256,256]{1,0:T(8,128)} %collective-permute-done.25.two.refs_2_), channel_id=1, source_target_pairs={{0,28},{1,5},{2,30},{3,7},{4,0},{5,9},{6,2},{7,11},{8,4},{9,13},{1... | collective-permute-start | bytes 786440 | tf_op jit(solution)/shard_map/ppermute | solution.py:42
  83.8 15.1 %collective-permute-start.30 = (f32[256,256]{1,0:T(8,128)}, f32[256,256]{1,0:T(8,128)}, u32[]{:S(2)}, u32[]{:S(2)}) collective-permute-start(f32[256,256]{1,0:T(8,128)} %collective-permute-done.27.six.refs_7_), channel_id=1, source_target_pairs={{0,4},{1,29},{2,6},{3,31},{4,8},{5,1},{6,10},{7,3},{8,12},{9,5},{1... | collective-permute-start | bytes 786440 | tf_op jit(solution)/shard_map/ppermute | solution.py:42
  86.9 12.0 %collective-permute-start.28 = (f32[128,256]{1,0:T(8,128)S(1)}, f32[128,256]{1,0:T(8,128)S(1)}, u32[]{:S(2)}, u32[]{:S(2)}) collective-permute-start(f32[128,256]{1,0:T(8,128)S(1)} %get-tuple-element.73), channel_id=1, source_target_pairs={{0,8},{1,25},{2,10},{3,27},{4,12},{5,29},{6,14},{7,31},{8,16},{9,1... | collective-permute-start | bytes 393224 | tf_op jit(solution)/shard_map/ppermute | solution.py:42
  89.8 9.1 %collective-permute-start.29 = (f32[128,256]{1,0:T(8,128)S(1)}, f32[128,256]{1,0:T(8,128)S(1)}, u32[]{:S(2)}, u32[]{:S(2)}) collective-permute-start(f32[128,256]{1,0:T(8,128)S(1)} %get-tuple-element.74), channel_id=1, source_target_pairs={{0,24},{1,9},{2,26},{3,11},{4,28},{5,13},{6,30},{7,15},{8,0},{9,17... | collective-permute-start | bytes 393224 | tf_op jit(solution)/shard_map/ppermute | solution.py:42
  93.1 20.0 %all-to-all-start.1 = ((f32[8,40,256]{2,1,0:T(8,128)}), f32[8,40,256]{2,1,0:T(8,128)}, u32[]{:S(2)}, u32[]{:S(2)}) async-start(f32[8,40,256]{2,1,0:T(8,128)} %spread.1), calls=%async_computation.1 | async-start | bytes 655360 | tf_op jit(solution)/shard_map/all_to_all | solution.py:459
  98.9 5.9 %copy-start.1 = (f32[1,1,12,128,128]{4,3,2,1,0:T(8,128)S(1)}, f32[1,1,12,128,128]{4,3,2,1,0:T(8,128)}, u32[]{:S(2)}) copy-start(f32[1,1,12,128,128]{4,3,2,1,0:T(8,128)} %param.10) | copy-start | bytes 2359300
  98.9 5.9 %copy-start.6 = (s32[12,2]{1,0:T(8,128)S(1)}, s32[12,2]{1,0:T(8,128)}, u32[]{:S(2)}) copy-start(s32[12,2]{1,0:T(8,128)} %copy-done.5) | copy-start | bytes 292
  99.0 5.9 %copy-start.8 = (s32[5]{0:T(128)S(1)}, s32[5]{0:T(128)}, u32[]{:S(2)}) copy-start(s32[5]{0:T(128)} %copy-done.7) | copy-start | bytes 64
  100.6 2.0 %collective-permute-start.32 = (f32[512,256]{1,0:T(8,128)S(1)}, f32[512,256]{1,0:T(8,128)S(1)}, u32[]{:S(2)}, u32[]{:S(2)}) collective-permute-start(f32[512,256]{1,0:T(8,128)S(1)} %get-tuple-element.75.refs_0_), channel_id=1, source_target_pairs={{0,1},{1,0},{2,3},{3,2},{4,5},{5,4},{6,7},{7,6},{8,9},{9,8},{10,11... | collective-permute-start | bytes 1572872 | tf_op jit(solution)/shard_map/ppermute | solution.py:464
  100.7 2.6 %collective-permute-start.33 = (f32[512,256]{1,0:T(8,128)S(1)}, f32[512,256]{1,0:T(8,128)S(1)}, u32[]{:S(2)}, u32[]{:S(2)}) collective-permute-start(f32[512,256]{1,0:T(8,128)S(1)} %get-tuple-element.76.refs_1_), channel_id=1, source_target_pairs={{0,1},{1,0},{2,3},{3,2},{4,5},{5,4},{6,7},{7,6},{8,9},{9,8},{10,11... | collective-permute-start | bytes 1572872 | tf_op jit(solution)/shard_map/ppermute | solution.py:464
  101.2 2.9 %collective-permute-start.34 = (f32[512,256]{1,0:T(8,128)S(1)}, f32[512,256]{1,0:T(8,128)S(1)}, u32[]{:S(2)}, u32[]{:S(2)}) collective-permute-start(f32[512,256]{1,0:T(8,128)S(1)} %get-tuple-element.77.refs_2_), channel_id=1, source_target_pairs={{0,1},{1,0},{2,3},{3,2},{4,5},{5,4},{6,7},{7,6},{8,9},{9,8},{10,11... | collective-permute-start | bytes 1572872 | tf_op jit(solution)/shard_map/ppermute | solution.py:464
  101.3 3.5 %collective-permute-start.35 = (f32[512,256]{1,0:T(8,128)S(1)}, f32[512,256]{1,0:T(8,128)S(1)}, u32[]{:S(2)}, u32[]{:S(2)}) collective-permute-start(f32[512,256]{1,0:T(8,128)S(1)} %get-tuple-element.78.refs_3_), channel_id=1, source_target_pairs={{0,1},{1,0},{2,3},{3,2},{4,5},{5,4},{6,7},{7,6},{8,9},{9,8},{10,11... | collective-permute-start | bytes 1572872 | tf_op jit(solution)/shard_map/ppermute | solution.py:464
  106.9 17.3 %collective-permute-start.41 = (f32[128,256]{1,0:T(8,128)S(1)}, f32[128,256]{1,0:T(8,128)S(1)}, u32[]{:S(2)}, u32[]{:S(2)}) collective-permute-start(f32[128,256]{1,0:T(8,128)S(1)} %get-tuple-element.89), channel_id=1, source_target_pairs={{0,64},{32,96},{64,128},{96,160},{128,192},{160,224},{192,0},{224,... | collective-permute-start | bytes 393224 | tf_op jit(solution)/shard_map/ppermute | solution.py:55
  108.4 16.8 %collective-permute-start.42 = (f32[128,256]{1,0:T(8,128)S(1)}, f32[128,256]{1,0:T(8,128)S(1)}, u32[]{:S(2)}, u32[]{:S(2)}) collective-permute-start(f32[128,256]{1,0:T(8,128)S(1)} %get-tuple-element.90), channel_id=1, source_target_pairs={{0,128},{32,160},{64,192},{96,224},{128,0},{160,32},{192,64},{224,... | collective-permute-start | bytes 393224 | tf_op jit(solution)/shard_map/ppermute | solution.py:55
  113.1 12.1 %collective-permute-start.43 = (f32[128,256]{1,0:T(8,128)S(1)}, f32[128,256]{1,0:T(8,128)S(1)}, u32[]{:S(2)}, u32[]{:S(2)}) collective-permute-start(f32[128,256]{1,0:T(8,128)S(1)} %get-tuple-element.91), channel_id=1, source_target_pairs={{0,192},{32,224},{64,0},{96,32},{128,64},{160,96},{192,128},{224,1... | collective-permute-start | bytes 393224 | tf_op jit(solution)/shard_map/ppermute | solution.py:55
  114.1 1.3 collective-permute-start.36
  115.4 5.5 %collective-permute-start.37 = (f32[40,256]{1,0:T(8,128)S(1)}, f32[40,256]{1,0:T(8,128)S(1)}, u32[]{:S(2)}, u32[]{:S(2)}) collective-permute-start(f32[40,256]{1,0:T(8,128)S(1)} %add.43.piece), channel_id=1, source_target_pairs={{0,32},{32,0},{64,96},{96,64},{128,160},{160,128},{192,224},{224,1... | collective-permute-start | bytes 122888 | tf_op jit(solution)/shard_map/ppermute | solution.py:59
  120.9 10.4 %collective-permute-start.38 = (f32[208,256]{1,0:T(8,128)S(1)}, f32[208,256]{1,0:T(8,128)S(1)}, u32[]{:S(2)}, u32[]{:S(2)}) collective-permute-start(f32[208,256]{1,0:T(8,128)S(1)} %get-tuple-element.84), channel_id=1, source_target_pairs={{0,64},{32,96},{64,128},{96,160},{128,192},{160,224},{192,0},{224,... | collective-permute-start | bytes 638984 | tf_op jit(solution)/shard_map/ppermute | solution.py:55
  123.0 9.7 %collective-permute-start.39 = (f32[208,256]{1,0:T(8,128)S(1)}, f32[208,256]{1,0:T(8,128)S(1)}, u32[]{:S(2)}, u32[]{:S(2)}) collective-permute-start(f32[208,256]{1,0:T(8,128)S(1)} %get-tuple-element.85), channel_id=1, source_target_pairs={{0,128},{32,160},{64,192},{96,224},{128,0},{160,32},{192,64},{224,... | collective-permute-start | bytes 638984 | tf_op jit(solution)/shard_map/ppermute | solution.py:55
  124.3 10.2 %collective-permute-start.40 = (f32[208,256]{1,0:T(8,128)S(1)}, f32[208,256]{1,0:T(8,128)S(1)}, u32[]{:S(2)}, u32[]{:S(2)}) collective-permute-start(f32[208,256]{1,0:T(8,128)S(1)} %get-tuple-element.86), channel_id=1, source_target_pairs={{0,192},{32,224},{64,0},{96,32},{128,64},{160,96},{192,128},{224,1... | collective-permute-start | bytes 638984 | tf_op jit(solution)/shard_map/ppermute | solution.py:55
  125.3 10.5 %collective-permute-start.44 = (f32[128,256]{1,0:T(8,128)S(1)}, f32[128,256]{1,0:T(8,128)S(1)}, u32[]{:S(2)}, u32[]{:S(2)}) collective-permute-start(f32[128,256]{1,0:T(8,128)S(1)} %gather_sums.1), channel_id=1, source_target_pairs={{0,32},{32,0},{64,96},{96,64},{128,160},{160,128},{192,224},{224,1... | collective-permute-start | bytes 393224 | tf_op jit(solution)/shard_map/ppermute | solution.py:59
  134.4 1.3 copy-start.3

commit v6 on v5

--- a/solution.py
+++ b/solution.py
@@ -12,6 +12,7 @@
 X, YH = 4, 2
 TILE = 128
 PAIR = YL * TILE
+FAR, NEAR = (3, 4, 5, 6), (7, 0, 1, 2)
 JOIN_COST = 10**12
 HALVES_COST = 10**12
 ROWS_COST = 10**12
@@ -37,7 +38,7 @@
 
 def z_shift(value, distance):
     def move(z, y, core):
-        return (z + (1 - 2 * core) * distance) % Z, y, core
+        return (z + (2 * core - 1) * distance) % Z, y, core
 
     return lax.ppermute(value, "col", col_pairs(move))
 
@@ -87,7 +88,7 @@
 def locate(tile, where):
     mine = lax.rem(tile, 2) == where[2]
     away = lax.div(tile, 2 * YL) - where[0]
-    distance = lax.rem(jnp.where(lax.rem(tile, 2) == 0, away, -away) + Z, Z)
+    distance = lax.rem(jnp.where(lax.rem(tile, 2) == 0, -away, away) + Z, Z)
     return mine, distance, lax.rem(lax.div(tile, 2), YL)
 
 
@@ -115,9 +116,12 @@
     return across * X + lax.rem(lax.div(tile, YH) - where[3] + X, X)
 
 
-def forward_kernel(place, count, where, values, near_high, near_low, a, b, c, d, keep, send, high, low):
-    keep[...] = jnp.zeros_like(keep)
-    send[...] = jnp.zeros_like(send)
+def forward_kernel(
+    place, count, where, values, near_high, near_low, a, b, c, d,
+    keep_far, send_far, keep_near, send_near, high, low,
+):
+    for out in (keep_far, send_far, keep_near, send_near):
+        out[...] = jnp.zeros_like(out)
     for j, part in enumerate((a, b, c, d)):
         high[j], low[j] = near_high[j], near_low[j]
         high[X + j], low[X + j] = split(part[...])
@@ -126,20 +130,24 @@
         mine, distance, y = locate(place[k, 0], where)
         live = k < count[0]
         product = dot3(split(values[k]), (high[col], low[col]), ((1,), (0,)))
-        index = distance * YL + y
-        keep[index] += jnp.where(live & mine, product, 0.0)
-        send[index] += jnp.where(live & ~mine, product, 0.0)
+        is_far = (distance >= FAR[0]) & (distance <= FAR[-1])
+        far = jnp.where(is_far, distance - FAR[0], 0) * YL + y
+        near = jnp.where(is_far, 0, lax.rem(distance + Z - NEAR[0], Z)) * YL + y
+        keep_far[far] += jnp.where(live & mine & is_far, product, 0.0)
+        send_far[far] += jnp.where(live & ~mine & is_far, product, 0.0)
+        keep_near[near] += jnp.where(live & mine & ~is_far, product, 0.0)
+        send_near[near] += jnp.where(live & ~mine & ~is_far, product, 0.0)
 
 
 def forward(place, count, where, values, near, far):
-    tiles = Z * YL
     width = far[0].shape[-1]
     parts = pltpu.VMEM((X * YH, TILE, width), jnp.bfloat16)
     return pl.pallas_call(
         forward_kernel,
-        out_shape=(shaped(tiles, TILE, width),) * 2,
+        out_shape=(shaped(len(FAR) * YL, TILE, width),) * 2
+        + (shaped(len(NEAR) * YL, TILE, width),) * 2,
         in_specs=[SMEM, SMEM, SMEM] + [VMEM] * 7,
-        out_specs=(VMEM,) * 2,
+        out_specs=(VMEM,) * 4,
         scratch_shapes=[parts, parts],
         compiler_params=params(12),
         name="forward_tiles",
@@ -443,18 +451,23 @@
         x_shift(node_features, 1),
     )
     far = (partner, x_shift(partner, -1), x_shift(partner, 2), x_shift(partner, 1))
-    keep, send = forward(place, count, where, values, near, far)
+    keep_far, send_far, keep_near, send_near = forward(place, count, where, values, near, far)
+    other_far = lax.ppermute(send_far, "col", CORE_SWAP)
+    other_far, send_near = lax.optimization_barrier((other_far, send_near))
+    tiles = add_cores(keep_far, other_far)
+    tiles += add_cores(keep_near, lax.ppermute(send_near, "col", CORE_SWAP))
+    tiles = dict(zip([(d, y) for d in FAR + NEAR for y in range(YL)], tiles))
     cot_other = lax.ppermute(cotangent, "col", Y_SWAP)
-    tiles = add_cores(keep, lax.ppermute(send, "col", CORE_SWAP))
-    summed = last_sum(*ring_z(tiles[0::YL]), *ring_z(tiles[1::YL]))
+    low, high = (ring_z([tiles[d, y] for d in range(Z)]) for y in range(YL))
+    summed = last_sum(*low, *high)
     summed, cot_other = lax.optimization_barrier((summed, cot_other))
     summed_other = lax.ppermute(summed, "col", Y_SWAP)
     output, grads, extra = middle(
         where, summed, summed_other, weight, bias.reshape(1, width), cotangent, cot_other
     )
 
-    two, six = z_shift(grads, -2), z_shift(grads, 2)
-    one, seven = z_shift(grads, -1), z_shift(grads, 1)
+    six, two = z_shift(grads, 2), z_shift(grads, -2)
+    seven, one = z_shift(grads, 1), z_shift(grads, -1)
     parts = lax.all_to_all(extra, "row", 0, 0)
     parts = lax.all_to_all(spread(parts, Z), "col", 0, 0, axis_index_groups=Z_GROUPS)
     three, five = z_shift(two, -1), z_shift(six, 1)

time: 137 us -> 137 us (level)
  starting transfers between devices: 74.1 us -> 70.7 us
  waiting for transfers between devices: 44.4 us -> 46.7 us
    ppermute x12, starting transfers between devices: 19.3 us -> 16.4 us  [x_shift(): return lax.ppermute(value, 'row', row_pairs(lambda x, h: (x + distance, h)))]
    ppermute x22, starting transfers between devices: 35.2 us -> 37.9 us  [z_shift(): return lax.ppermute(value, 'col', col_pairs(move))]
    ppermute x1, waiting for transfers between devices: 0.01 us -> 2.31 us  [body(): cot_other = lax.ppermute(cotangent, 'col', Y_SWAP)]
    all_to_all x1, starting transfers between devices: 5.82 us -> 4.27 us  [body(): lax.all_to_all(spread(parts, Z), 'col', 0, 0, axis_index_groups=Z_GROUPS)]
    all_to_all x1, starting transfers between devices: 6.66 us -> 5.15 us  [body(): parts = lax.all_to_all(extra, 'row', 0, 0)]
    ppermute x1 -> x2, waiting for transfers between devices: 4.15 us -> 2.65 us  [the longest x1 2.65 us: body(): other_far = lax.ppermute(send_far, 'col', CORE_SWAP)]
  transfers between devices with their start and end apart: 47 -> 48, of which waited for: 21 -> 25; matrix products, arithmetic and copies ran while one was open for 1% -> 0% of each run, Pallas kernels for 7% -> 7%
where the time goes in v6:
time: 137 us; the launch traced here: 136 us
  starting transfers between devices  70.7 us (52%)
  waiting for transfers between devices  46.7 us (34%)
  Pallas kernels  14.9 us (11%)
  local copies, waits for them, and re-layouts  1.8 us (1%)
  between operations  1.54 us (1%)
    ppermute x22, starting transfers between devices, z_shift(): return lax.ppermute(value, 'col', col_pairs(move))  37.9 us
    ppermute x12, starting transfers between devices, x_shift(): return lax.ppermute(value, 'row', row_pairs(lambda x, h: (x + distance, h)))  16.4 us
    ppermute x12, waiting for transfers between devices, x_shift(): return lax.ppermute(value, 'row', row_pairs(lambda x, h: (x + distance, h)))  13.4 us
    ppermute x22, waiting for transfers between devices, z_shift(): return lax.ppermute(value, 'col', col_pairs(move))  12.8 us
    ppermute x1, waiting for transfers between devices, body(): summed_other = lax.ppermute(summed, 'col', Y_SWAP)  5.69 us
    ppermute x3, waiting for transfers between devices, h_swap(): return lax.ppermute(value, 'row', row_pairs(lambda x, h: (x, 1 - h)))  5.5 us
    all_to_all x1, starting transfers between devices, body(): parts = lax.all_to_all(extra, 'row', 0, 0)  5.15 us
    all_to_all x1, starting transfers between devices, body(): lax.all_to_all(spread(parts, Z), 'col', 0, 0, axis_index_groups=Z_GROUPS)  4.27 us
  transfers between devices with their start and end apart: 48, of which 25 were waited for; matrix products, arithmetic and copies ran while one was open for 0% of the time, Pallas kernels for 7%

profile of v6, /device:TPU:2, one launch (start us, length us, event | category | flops | bytes accessed | tf_op | source)
XLA Modules:
  0.0 135.8 jit_solution(11434307898300326786)
XLA Ops:
  0.6 3.3 %collective-permute-start.3 = (f32[128,256]{1,0:T(8,128)}, f32[128,256]{1,0:T(8,128)}, u32[]{:S(2)}, u32[]{:S(2)}) collective-permute-start(f32[128,256]{1,0:T(8,128)} %refs_0_.1), channel_id=1, source_target_pairs={{0,32},{32,0},{64,96},{96,64},{128,160},{160,128},{192,224},{224,1... | collective-permute-start | bytes 393224 | tf_op jit(solution)/shard_map/ppermute | solution.py:60
  3.9 1.5 %collective-permute-start.2 = (f32[128,256]{1,0:T(8,128)}, f32[128,256]{1,0:T(8,128)S(1)}, u32[]{:S(2)}, u32[]{:S(2)}) collective-permute-start(f32[128,256]{1,0:T(8,128)} %refs_0_.1), channel_id=1, source_target_pairs={{0,64},{32,96},{64,128},{96,160},{128,192},{160,224},{192,0},{224,... | collective-permute-start | bytes 393224 | tf_op jit(solution)/shard_map/ppermute | solution.py:56
  5.4 1.1 collective-permute-start.1
  6.5 2.2 %collective-permute-start = (f32[128,256]{1,0:T(8,128)}, f32[128,256]{1,0:T(8,128)S(1)}, u32[]{:S(2)}, u32[]{:S(2)}) collective-permute-start(f32[128,256]{1,0:T(8,128)} %refs_0_.1), channel_id=1, source_target_pairs={{0,192},{32,224},{64,0},{96,32},{128,64},{160,96},{192,128},{224,1... | collective-permute-start | bytes 393224 | tf_op jit(solution)/shard_map/ppermute | solution.py:56
  9.3 0.7 copy-done.11
  10.3 3.5 %collective-permute-start.5 = (f32[128,256]{1,0:T(8,128)}, f32[128,256]{1,0:T(8,128)}, u32[]{:S(2)}, u32[]{:S(2)}) collective-permute-start(f32[128,256]{1,0:T(8,128)} %collective-permute-done.3.a), channel_id=1, source_target_pairs={{0,128},{32,160},{64,192},{96,224},{128,0},{160,32},{192,64},{224,... | collective-permute-start | bytes 393224 | tf_op jit(solution)/shard_map/ppermute | solution.py:56
  13.8 0.6 collective-permute-done.refs_1_
  14.4 0.9 copy-done.10
  15.4 0.8 collective-permute-done.6.d
  16.2 2.5 %collective-permute-done.5.c = f32[128,256]{1,0:T(8,128)} collective-permute-done((f32[128,256]{1,0:T(8,128)}, f32[128,256]{1,0:T(8,128)}, u32[]{:S(2)}, u32[]{:S(2)}) %collective-permute-start.5) | collective-permute-done | bytes 131104 | tf_op jit(solution)/shard_map/ppermute | solution.py:56
  18.8 1.0 collective-permute-done.4.b
  19.8 2.7 %forward_tiles.1 = (f32[8,128,256]{2,1,0:T(8,128)S(1)}, f32[8,128,256]{2,1,0:T(8,128)S(1)}, f32[8,128,256]{2,1,0:T(8,128)S(1)}, f32[8,128,256]{2,1,0:T(8,128)S(1)}) custom-call(s32[12,2]{1,0:T(8,128)S(1)} %copy.11.place, s32[1]{0:T(128)} %bitcast.10.count, s32[5]{0:T(128)S(1)} %stack.23.where, f32[12,128,128]{2,1,0:T(8,128)S(1)} %bitcast.12, ...), custom_call_target="tpu_custom_call" | custom-call | tf_op jit(solution)/shard_map/forward_tiles/pallas_call | solution.py:145
  22.6 2.6 %collective-permute-done.7.second = f32[8,128,256]{2,1,0:T(8,128)S(1)} collective-permute-done((f32[8,128,256]{2,1,0:T(8,128)S(1)}, f32[8,128,256]{2,1,0:T(8,128)S(1)}, u32[]{:S(2)}, u32[]{:S(2)}) %collective-permute-start.7) | collective-permute-done | bytes 1048608 | tf_op jit(solution)/shard_map/ppermute | solution.py:455
  25.5 5.9 %collective-permute-start.9 = (f32[128,256]{1,0:T(8,128)S(1)}, f32[128,256]{1,0:T(8,128)S(1)}, u32[]{:S(2)}, u32[]{:S(2)}) collective-permute-start(f32[128,256]{1,0:T(8,128)S(1)} %get-tuple-element.65), channel_id=1, source_target_pairs={{0,28},{1,5},{2,30},{3,7},{4,0},{5,9},{6,2},{7,11},{8,4},{9,13},{1... | collective-permute-start | bytes 393224 | tf_op jit(solution)/shard_map/ppermute | solution.py:43
  31.5 1.0 collective-permute-start.16
  32.5 1.0 collective-permute-start.13
  33.5 1.7 %collective-permute-done.9 = f32[128,256]{1,0:T(8,128)S(1)} collective-permute-done((f32[128,256]{1,0:T(8,128)S(1)}, f32[128,256]{1,0:T(8,128)S(1)}, u32[]{:S(2)}, u32[]{:S(2)}) %collective-permute-start.9) | collective-permute-done | bytes 131104 | tf_op jit(solution)/shard_map/ppermute | solution.py:43
  35.3 3.8 %collective-permute-start.10 = (f32[128,256]{1,0:T(8,128)S(1)}, f32[128,256]{1,0:T(8,128)S(1)}, u32[]{:S(2)}, u32[]{:S(2)}) collective-permute-start(f32[128,256]{1,0:T(8,128)S(1)} %add.33), channel_id=1, source_target_pairs={{0,28},{1,5},{2,30},{3,7},{4,0},{5,9},{6,2},{7,11},{8,4},{9,13},{1... | collective-permute-start | bytes 393224 | tf_op jit(solution)/shard_map/ppermute | solution.py:43
  39.1 2.5 %collective-permute-start.17 = (f32[128,256]{1,0:T(8,128)S(1)}, f32[128,256]{1,0:T(8,128)S(1)}, u32[]{:S(2)}, u32[]{:S(2)}) collective-permute-start(f32[128,256]{1,0:T(8,128)S(1)} %add.38), channel_id=1, source_target_pairs={{0,28},{1,5},{2,30},{3,7},{4,0},{5,9},{6,2},{7,11},{8,4},{9,13},{1... | collective-permute-start | bytes 393224 | tf_op jit(solution)/shard_map/ppermute | solution.py:43
  41.8 0.5 collective-permute-done.20
  42.8 3.2 %collective-permute-start.11 = (f32[128,256]{1,0:T(8,128)S(1)}, f32[128,256]{1,0:T(8,128)S(1)}, u32[]{:S(2)}, u32[]{:S(2)}) collective-permute-start(f32[128,256]{1,0:T(8,128)S(1)} %add.34), channel_id=1, source_target_pairs={{0,28},{1,5},{2,30},{3,7},{4,0},{5,9},{6,2},{7,11},{8,4},{9,13},{1... | collective-permute-start | bytes 393224 | tf_op jit(solution)/shard_map/ppermute | solution.py:43
  46.0 2.2 %collective-permute-start.18 = (f32[128,256]{1,0:T(8,128)S(1)}, f32[128,256]{1,0:T(8,128)S(1)}, u32[]{:S(2)}, u32[]{:S(2)}) collective-permute-start(f32[128,256]{1,0:T(8,128)S(1)} %add.39), channel_id=1, source_target_pairs={{0,28},{1,5},{2,30},{3,7},{4,0},{5,9},{6,2},{7,11},{8,4},{9,13},{1... | collective-permute-start | bytes 393224 | tf_op jit(solution)/shard_map/ppermute | solution.py:43
  48.2 1.2 collective-permute-done.14
  49.5 1.3 collective-permute-done.21
  51.0 3.3 %collective-permute-start.12 = (f32[128,256]{1,0:T(8,128)S(1)}, f32[128,256]{1,0:T(8,128)S(1)}, u32[]{:S(2)}, u32[]{:S(2)}) collective-permute-start(f32[128,256]{1,0:T(8,128)S(1)} %add.35), channel_id=1, source_target_pairs={{0,28},{1,5},{2,30},{3,7},{4,0},{5,9},{6,2},{7,11},{8,4},{9,13},{1... | collective-permute-start | bytes 393224 | tf_op jit(solution)/shard_map/ppermute | solution.py:43
  54.3 1.1 collective-permute-start.19
  55.4 0.7 collective-permute-start.23
  56.2 1.4 %collective-permute-done.22.refs_5_ = f32[128,256]{1,0:T(8,128)S(1)} collective-permute-done((f32[128,256]{1,0:T(8,128)S(1)}, f32[128,256]{1,0:T(8,128)S(1)}, u32[]{:S(2)}, u32[]{:S(2)}) %collective-permute-start.22) | collective-permute-done | bytes 131104 | tf_op jit(solution)/shard_map/ppermute | solution.py:43
  57.6 1.7 %collective-permute-done.19.refs_4_ = f32[128,256]{1,0:T(8,128)S(1)} collective-permute-done((f32[128,256]{1,0:T(8,128)S(1)}, f32[128,256]{1,0:T(8,128)S(1)}, u32[]{:S(2)}, u32[]{:S(2)}) %collective-permute-start.19) | collective-permute-done | bytes 131104 | tf_op jit(solution)/shard_map/ppermute | solution.py:43
  59.4 2.3 %collective-permute-done.23.cot_other = f32[128,256]{1,0:T(8,128)S(1)} collective-permute-done((f32[128,256]{1,0:T(8,128)S(1)}, f32[128,256]{1,0:T(8,128)S(1)}, u32[]{:S(2)}, u32[]{:S(2)}) %collective-permute-start.23) | collective-permute-done | bytes 131104 | tf_op jit(solution)/shard_map/ppermute | solution.py:460
  61.7 0.7 collective-permute-start.24
  62.4 5.7 %collective-permute-done.24.other = f32[256,256]{1,0:T(8,128)S(1)} collective-permute-done((f32[256,256]{1,0:T(8,128)S(1)}, f32[256,256]{1,0:T(8,128)S(1)}, u32[]{:S(2)}, u32[]{:S(2)}) %collective-permute-start.24) | collective-permute-done | bytes 262176 | tf_op jit(solution)/shard_map/ppermute | solution.py:464
  68.1 2.0 %middle.1 = (f32[128,256]{1,0:T(8,128)}, f32[256,256]{1,0:T(8,128)}, f32[8,40,256]{2,1,0:T(8,128)}) custom-call(s32[5]{0:T(128)S(1)} %stack.23.where, f32[256,256]{1,0:T(8,128)S(1)} %last_sum.1.mine, f32[256,256]{1,0:T(8,128)S(1)} %collective-permute-done.24.other, f32[256,256]{1,0:T(8,128)S(1)} %copy-done.2, f32[1,256]{1,0:T(1,128)S(1)} %bitcast.14, ...), custom_call_target="tpu_custom_call" | custom-call | tf_op jit(solution)/shard_map/middle/pallas_call | solution.py:224
  70.1 2.9 %collective-permute-start.26 = (f32[256,256]{1,0:T(8,128)}, f32[256,256]{1,0:T(8,128)}, u32[]{:S(2)}, u32[]{:S(2)}) collective-permute-start(f32[256,256]{1,0:T(8,128)} %get-tuple-element.80.refs_0_), channel_id=1, source_target_pairs={{0,8},{1,25},{2,10},{3,27},{4,12},{5,29},{6,14},{7,31},{8,16},{9,1... | collective-permute-start | bytes 786440 | tf_op jit(solution)/shard_map/ppermute | solution.py:43
  73.0 2.0 %collective-permute-start.32 = (f32[256,256]{1,0:T(8,128)}, f32[256,256]{1,0:T(8,128)}, u32[]{:S(2)}, u32[]{:S(2)}) collective-permute-start(f32[256,256]{1,0:T(8,128)} %get-tuple-element.80.refs_0_), channel_id=1, source_target_pairs={{0,28},{1,5},{2,30},{3,7},{4,0},{5,9},{6,2},{7,11},{8,4},{9,13},{1... | collective-permute-start | bytes 786440 | tf_op jit(solution)/shard_map/ppermute | solution.py:43
  75.0 5.2 %all-to-all-start = ((f32[8,40,256]{2,1,0:T(8,128)}), f32[8,40,256]{2,1,0:T(8,128)}, u32[]{:S(2)}, u32[]{:S(2)}) async-start(f32[8,40,256]{2,1,0:T(8,128)} %get-tuple-element.91), calls=%async_computation | async-start | bytes 655360 | tf_op jit(solution)/shard_map/all_to_all | solution.py:471
  80.2 2.3 %collective-permute-done.28.six.refs_7_ = f32[256,256]{1,0:T(8,128)} collective-permute-done((f32[256,256]{1,0:T(8,128)}, f32[256,256]{1,0:T(8,128)}, u32[]{:S(2)}, u32[]{:S(2)}) %collective-permute-start.28) | collective-permute-done | bytes 262176 | tf_op jit(solution)/shard_map/ppermute | solution.py:43
  82.5 3.3 %collective-permute-start.31 = (f32[256,256]{1,0:T(8,128)}, f32[256,256]{1,0:T(8,128)}, u32[]{:S(2)}, u32[]{:S(2)}) collective-permute-start(f32[256,256]{1,0:T(8,128)} %collective-permute-done.28.six.refs_7_), channel_id=1, source_target_pairs={{0,28},{1,5},{2,30},{3,7},{4,0},{5,9},{6,2},{7,11},{8,4},{9,13},{1... | collective-permute-start | bytes 786440 | tf_op jit(solution)/shard_map/ppermute | solution.py:43
  86.2 1.0 halves.1
  87.3 3.1 %collective-permute-start.29 = (f32[128,256]{1,0:T(8,128)S(1)}, f32[128,256]{1,0:T(8,128)S(1)}, u32[]{:S(2)}, u32[]{:S(2)}) collective-permute-start(f32[128,256]{1,0:T(8,128)S(1)} %get-tuple-element.81), channel_id=1, source_target_pairs={{0,24},{1,9},{2,26},{3,11},{4,28},{5,13},{6,30},{7,15},{8,0},{9,17... | collective-permute-start | bytes 393224 | tf_op jit(solution)/shard_map/ppermute | solution.py:43
  90.4 1.5 %collective-permute-start.30 = (f32[128,256]{1,0:T(8,128)S(1)}, f32[128,256]{1,0:T(8,128)S(1)}, u32[]{:S(2)}, u32[]{:S(2)}) collective-permute-start(f32[128,256]{1,0:T(8,128)S(1)} %get-tuple-element.82), channel_id=1, source_target_pairs={{0,8},{1,25},{2,10},{3,27},{4,12},{5,29},{6,14},{7,31},{8,16},{9,1... | collective-permute-start | bytes 393224 | tf_op jit(solution)/shard_map/ppermute | solution.py:43
  91.9 1.7 %spread.1 = f32[8,40,256]{2,1,0:T(8,128)} custom-call(f32[8,40,256]{2,1,0:T(8,128)} %all-to-all-done.parts), custom_call_target="tpu_custom_call" | custom-call | tf_op jit(solution)/shard_map/spread/pallas_call | solution.py:248
  93.6 4.3 %all-to-all-start.1 = ((f32[8,40,256]{2,1,0:T(8,128)}), f32[8,40,256]{2,1,0:T(8,128)}, u32[]{:S(2)}, u32[]{:S(2)}) async-start(f32[8,40,256]{2,1,0:T(8,128)} %spread.1), calls=%async_computation.1 | async-start | bytes 655360 | tf_op jit(solution)/shard_map/all_to_all | solution.py:472
  97.9 2.4 %collective-permute-done.30.refs_5_ = f32[128,256]{1,0:T(8,128)S(1)} collective-permute-done((f32[128,256]{1,0:T(8,128)S(1)}, f32[128,256]{1,0:T(8,128)S(1)}, u32[]{:S(2)}, u32[]{:S(2)}) %collective-permute-start.30) | collective-permute-done | bytes 131104 | tf_op jit(solution)/shard_map/ppermute | solution.py:43
  100.3 1.6 %join.1 = (f32[512,256]{1,0:T(8,128)S(1)}, f32[512,256]{1,0:T(8,128)S(1)}, f32[512,256]{1,0:T(8,128)S(1)}, f32[512,256]{1,0:T(8,128)S(1)}) custom-call(f32[256,256]{1,0:T(8,128)} %get-tuple-element.80.refs_0_, f32[256,256]{1,0:T(8,128)} %collective-permute-done.25.refs_1_, f32[256,256]{1,0:T(8,128)} %collective-permute-done.26.two.refs_2_, ...), custom_call_target="tpu_custom_call" | custom-call | flops 999999995904 | tf_op jit(solution)/shard_map/join/pallas_call | solution.py:286
  102.1 0.5 collective-permute-start.34
  103.1 0.9 collective-permute-done.33.refs_4_
  104.0 0.7 collective-permute-done.34.refs_5_
  104.7 0.7 collective-permute-done.35.refs_6_
  105.5 0.7 collective-permute-done.36.refs_7_
  106.2 2.0 %backward_tiles.1 = (f32[128,256]{1,0:T(8,128)S(1)}, f32[128,256]{1,0:T(8,128)S(1)}, f32[128,256]{1,0:T(8,128)S(1)}, f32[128,256]{1,0:T(8,128)S(1)}, f32[128,256...) custom-call(s32[12,2]{1,0:T(8,128)S(1)} %copy-done.6, ...), custom_call_target="tpu_custom_call" | custom-call | tf_op jit(solution)/shard_map/backward_tiles/pallas_call | solution.py:336
  108.3 1.2 collective-permute-start.42
  109.5 2.1 %collective-permute-start.43 = (f32[128,256]{1,0:T(8,128)S(1)}, f32[128,256]{1,0:T(8,128)S(1)}, u32[]{:S(2)}, u32[]{:S(2)}) collective-permute-start(f32[128,256]{1,0:T(8,128)S(1)} %get-tuple-element.98), channel_id=1, source_target_pairs={{0,128},{32,160},{64,192},{96,224},{128,0},{160,32},{192,64},{224,... | collective-permute-start | bytes 393224 | tf_op jit(solution)/shard_map/ppermute | solution.py:56
  111.6 1.6 %collective-permute-start.44 = (f32[128,256]{1,0:T(8,128)S(1)}, f32[128,256]{1,0:T(8,128)S(1)}, u32[]{:S(2)}, u32[]{:S(2)}) collective-permute-start(f32[128,256]{1,0:T(8,128)S(1)} %get-tuple-element.99), channel_id=1, source_target_pairs={{0,192},{32,224},{64,0},{96,32},{128,64},{160,96},{192,128},{224,1... | collective-permute-start | bytes 393224 | tf_op jit(solution)/shard_map/ppermute | solution.py:56
  113.3 1.0 total.1
  114.4 1.2 collective-permute-done.37
  115.6 5.5 %collective-permute-done.38.piece_across = f32[40,256]{1,0:T(8,128)S(1)} collective-permute-done((f32[40,256]{1,0:T(8,128)S(1)}, f32[40,256]{1,0:T(8,128)S(1)}, u32[]{:S(2)}, u32[]{:S(2)}) %collective-permute-start.38) | collective-permute-done | bytes 40992 | tf_op jit(solution)/shard_map/ppermute | solution.py:60
  121.6 2.6 %collective-permute-start.40 = (f32[208,256]{1,0:T(8,128)S(1)}, f32[208,256]{1,0:T(8,128)S(1)}, u32[]{:S(2)}, u32[]{:S(2)}) collective-permute-start(f32[208,256]{1,0:T(8,128)S(1)} %get-tuple-element.93), channel_id=1, source_target_pairs={{0,128},{32,160},{64,192},{96,224},{128,0},{160,32},{192,64},{224,... | collective-permute-start | bytes 638984 | tf_op jit(solution)/shard_map/ppermute | solution.py:56
  124.3 0.9 collective-permute-start.45
  125.2 4.2 %collective-permute-done.39.one = f32[208,256]{1,0:T(8,128)S(1)} collective-permute-done((f32[208,256]{1,0:T(8,128)S(1)}, f32[208,256]{1,0:T(8,128)S(1)}, u32[]{:S(2)}, u32[]{:S(2)}) %collective-permute-start.39) | collective-permute-done | bytes 213024 | tf_op jit(solution)/shard_map/ppermute | solution.py:56
  129.4 1.9 %collective-permute-done.40.two = f32[208,256]{1,0:T(8,128)S(1)} collective-permute-done((f32[208,256]{1,0:T(8,128)S(1)}, f32[208,256]{1,0:T(8,128)S(1)}, u32[]{:S(2)}, u32[]{:S(2)}) %collective-permute-start.40) | collective-permute-done | bytes 213024 | tf_op jit(solution)/shard_map/ppermute | solution.py:56
  131.3 2.3 %collective-permute-done.41.three = f32[208,256]{1,0:T(8,128)S(1)} collective-permute-done((f32[208,256]{1,0:T(8,128)S(1)}, f32[208,256]{1,0:T(8,128)S(1)}, u32[]{:S(2)}, u32[]{:S(2)}) %collective-permute-start.41) | collective-permute-done | bytes 213024 | tf_op jit(solution)/shard_map/ppermute | solution.py:56
  133.6 1.3 unpack.1
  134.9 1.0 final.1
  (84 shorter events, 3.8 us)
Async XLA Ops:
  0.6 9.6 %collective-permute-start.3 = (f32[128,256]{1,0:T(8,128)}, f32[128,256]{1,0:T(8,128)}, u32[]{:S(2)}, u32[]{:S(2)}) collective-permute-start(f32[128,256]{1,0:T(8,128)} %refs_0_.1), channel_id=1, source_target_pairs={{0,32},{32,0},{64,96},{96,64},{128,160},{160,128},{192,224},{224,1... | collective-permute-start | bytes 393224 | tf_op jit(solution)/shard_map/ppermute | solution.py:60
  3.9 9.8 %collective-permute-start.2 = (f32[128,256]{1,0:T(8,128)}, f32[128,256]{1,0:T(8,128)S(1)}, u32[]{:S(2)}, u32[]{:S(2)}) collective-permute-start(f32[128,256]{1,0:T(8,128)} %refs_0_.1), channel_id=1, source_target_pairs={{0,64},{32,96},{64,128},{96,160},{128,192},{160,224},{192,0},{224,... | collective-permute-start | bytes 393224 | tf_op jit(solution)/shard_map/ppermute | solution.py:56
  5.4 8.4 %collective-permute-start.1 = (f32[128,256]{1,0:T(8,128)}, f32[128,256]{1,0:T(8,128)S(1)}, u32[]{:S(2)}, u32[]{:S(2)}) collective-permute-start(f32[128,256]{1,0:T(8,128)} %refs_0_.1), channel_id=1, source_target_pairs={{0,128},{32,160},{64,192},{96,224},{128,0},{160,32},{192,64},{224,... | collective-permute-start | bytes 393224 | tf_op jit(solution)/shard_map/ppermute | solution.py:56
  6.5 7.9 %collective-permute-start = (f32[128,256]{1,0:T(8,128)}, f32[128,256]{1,0:T(8,128)S(1)}, u32[]{:S(2)}, u32[]{:S(2)}) collective-permute-start(f32[128,256]{1,0:T(8,128)} %refs_0_.1), channel_id=1, source_target_pairs={{0,192},{32,224},{64,0},{96,32},{128,64},{160,96},{192,128},{224,1... | collective-permute-start | bytes 393224 | tf_op jit(solution)/shard_map/ppermute | solution.py:56
  9.3 0.7 copy-start.11
  10.1 9.7 %copy-start.5 = (s32[12,2]{1,0:T(8,128)}, s32[12,2]{1,0:T(8,128)S(1)}, u32[]{:S(2)}) copy-start(s32[12,2]{1,0:T(8,128)S(1)} %copy.11.place) | copy-start | bytes 292
  10.2 57.9 %copy-start.7 = (s32[5]{0:T(128)}, s32[5]{0:T(128)S(1)}, u32[]{:S(2)}) copy-start(s32[5]{0:T(128)S(1)} %stack.23.where) | copy-start | bytes 64
  10.2 6.0 %collective-permute-start.6 = (f32[128,256]{1,0:T(8,128)}, f32[128,256]{1,0:T(8,128)}, u32[]{:S(2)}, u32[]{:S(2)}) collective-permute-start(f32[128,256]{1,0:T(8,128)} %collective-permute-done.3.a), channel_id=1, source_target_pairs={{0,64},{32,96},{64,128},{96,160},{128,192},{160,224},{192,0},{224,... | collective-permute-start | bytes 393224 | tf_op jit(solution)/shard_map/ppermute | solution.py:56
  10.3 8.5 %collective-permute-start.5 = (f32[128,256]{1,0:T(8,128)}, f32[128,256]{1,0:T(8,128)}, u32[]{:S(2)}, u32[]{:S(2)}) collective-permute-start(f32[128,256]{1,0:T(8,128)} %collective-permute-done.3.a), channel_id=1, source_target_pairs={{0,128},{32,160},{64,192},{96,224},{128,0},{160,32},{192,64},{224,... | collective-permute-start | bytes 393224 | tf_op jit(solution)/shard_map/ppermute | solution.py:56
  13.8 6.0 %collective-permute-start.4 = (f32[128,256]{1,0:T(8,128)}, f32[128,256]{1,0:T(8,128)}, u32[]{:S(2)}, u32[]{:S(2)}) collective-permute-start(f32[128,256]{1,0:T(8,128)} %collective-permute-done.3.a), channel_id=1, source_target_pairs={{0,192},{32,224},{64,0},{96,32},{128,64},{160,96},{192,128},{224,1... | collective-permute-start | bytes 393224 | tf_op jit(solution)/shard_map/ppermute | solution.py:56
  14.4 0.9 copy-start.10
  15.3 4.5 %copy-start = (f32[1,1,12,128,128]{4,3,2,1,0:T(8,128)S(1)}, f32[1,1,12,128,128]{4,3,2,1,0:T(8,128)}, u32[]{:S(2)}) copy-start(f32[1,1,12,128,128]{4,3,2,1,0:T(8,128)} %param.10) | copy-start | bytes 2359300
  22.5 2.7 %collective-permute-start.7 = (f32[8,128,256]{2,1,0:T(8,128)S(1)}, f32[8,128,256]{2,1,0:T(8,128)S(1)}, u32[]{:S(2)}, u32[]{:S(2)}) collective-permute-start(f32[8,128,256]{2,1,0:T(8,128)S(1)} %get-tuple-element.56), channel_id=1, source_target_pairs={{0,1},{1,0},{2,3},{3,2},{4,5},{5,4},{6,7},{7,6},{8,9},{9,8},{10,11... | collective-permute-start | bytes 3145736 | tf_op jit(solution)/shard_map/ppermute | solution.py:455
  25.3 17.4 %collective-permute-start.8 = (f32[8,128,256]{2,1,0:T(8,128)S(1)}, f32[8,128,256]{2,1,0:T(8,128)S(1)}, u32[]{:S(2)}, u32[]{:S(2)}) collective-permute-start(f32[8,128,256]{2,1,0:T(8,128)S(1)} %get-tuple-element.58), channel_id=1, source_target_pairs={{0,1},{1,0},{2,3},{3,2},{4,5},{5,4},{6,7},{7,6},{8,9},{9,8},{10,11... | collective-permute-start | bytes 3145736 | tf_op jit(solution)/shard_map/ppermute | solution.py:458
  25.5 9.7 %collective-permute-start.9 = (f32[128,256]{1,0:T(8,128)S(1)}, f32[128,256]{1,0:T(8,128)S(1)}, u32[]{:S(2)}, u32[]{:S(2)}) collective-permute-start(f32[128,256]{1,0:T(8,128)S(1)} %get-tuple-element.65), channel_id=1, source_target_pairs={{0,28},{1,5},{2,30},{3,7},{4,0},{5,9},{6,2},{7,11},{8,4},{9,13},{1... | collective-permute-start | bytes 393224 | tf_op jit(solution)/shard_map/ppermute | solution.py:43
  31.5 7.6 %collective-permute-start.16 = (f32[128,256]{1,0:T(8,128)S(1)}, f32[128,256]{1,0:T(8,128)S(1)}, u32[]{:S(2)}, u32[]{:S(2)}) collective-permute-start(f32[128,256]{1,0:T(8,128)S(1)} %get-tuple-element.73), channel_id=1, source_target_pairs={{0,28},{1,5},{2,30},{3,7},{4,0},{5,9},{6,2},{7,11},{8,4},{9,13},{1... | collective-permute-start | bytes 393224 | tf_op jit(solution)/shard_map/ppermute | solution.py:43
  32.5 9.1 %collective-permute-start.13 = (f32[128,256]{1,0:T(8,128)S(1)}, f32[128,256]{1,0:T(8,128)S(1)}, u32[]{:S(2)}, u32[]{:S(2)}) collective-permute-start(f32[128,256]{1,0:T(8,128)S(1)} %get-tuple-element.68), channel_id=1, source_target_pairs={{0,4},{1,29},{2,6},{3,31},{4,8},{5,1},{6,10},{7,3},{8,12},{9,5},{1... | collective-permute-start | bytes 393224 | tf_op jit(solution)/shard_map/ppermute | solution.py:43
  33.5 8.9 %collective-permute-start.20 = (f32[128,256]{1,0:T(8,128)S(1)}, f32[128,256]{1,0:T(8,128)S(1)}, u32[]{:S(2)}, u32[]{:S(2)}) collective-permute-start(f32[128,256]{1,0:T(8,128)S(1)} %get-tuple-element.76), channel_id=1, source_target_pairs={{0,4},{1,29},{2,6},{3,31},{4,8},{5,1},{6,10},{7,3},{8,12},{9,5},{1... | collective-permute-start | bytes 393224 | tf_op jit(solution)/shard_map/ppermute | solution.py:43
  35.3 7.5 %collective-permute-start.10 = (f32[128,256]{1,0:T(8,128)S(1)}, f32[128,256]{1,0:T(8,128)S(1)}, u32[]{:S(2)}, u32[]{:S(2)}) collective-permute-start(f32[128,256]{1,0:T(8,128)S(1)} %add.33), channel_id=1, source_target_pairs={{0,28},{1,5},{2,30},{3,7},{4,0},{5,9},{6,2},{7,11},{8,4},{9,13},{1... | collective-permute-start | bytes 393224 | tf_op jit(solution)/shard_map/ppermute | solution.py:43
  39.1 6.9 %collective-permute-start.17 = (f32[128,256]{1,0:T(8,128)S(1)}, f32[128,256]{1,0:T(8,128)S(1)}, u32[]{:S(2)}, u32[]{:S(2)}) collective-permute-start(f32[128,256]{1,0:T(8,128)S(1)} %add.38), channel_id=1, source_target_pairs={{0,28},{1,5},{2,30},{3,7},{4,0},{5,9},{6,2},{7,11},{8,4},{9,13},{1... | collective-permute-start | bytes 393224 | tf_op jit(solution)/shard_map/ppermute | solution.py:43
  41.6 7.8 %collective-permute-start.14 = (f32[128,256]{1,0:T(8,128)S(1)}, f32[128,256]{1,0:T(8,128)S(1)}, u32[]{:S(2)}, u32[]{:S(2)}) collective-permute-start(f32[128,256]{1,0:T(8,128)S(1)} %add.36), channel_id=1, source_target_pairs={{0,4},{1,29},{2,6},{3,31},{4,8},{5,1},{6,10},{7,3},{8,12},{9,5},{1... | collective-permute-start | bytes 393224 | tf_op jit(solution)/shard_map/ppermute | solution.py:43
  42.4 8.4 %collective-permute-start.21 = (f32[128,256]{1,0:T(8,128)S(1)}, f32[128,256]{1,0:T(8,128)S(1)}, u32[]{:S(2)}, u32[]{:S(2)}) collective-permute-start(f32[128,256]{1,0:T(8,128)S(1)} %add.41), channel_id=1, source_target_pairs={{0,4},{1,29},{2,6},{3,31},{4,8},{5,1},{6,10},{7,3},{8,12},{9,5},{1... | collective-permute-start | bytes 393224 | tf_op jit(solution)/shard_map/ppermute | solution.py:43
  42.8 8.1 %collective-permute-start.11 = (f32[128,256]{1,0:T(8,128)S(1)}, f32[128,256]{1,0:T(8,128)S(1)}, u32[]{:S(2)}, u32[]{:S(2)}) collective-permute-start(f32[128,256]{1,0:T(8,128)S(1)} %add.34), channel_id=1, source_target_pairs={{0,28},{1,5},{2,30},{3,7},{4,0},{5,9},{6,2},{7,11},{8,4},{9,13},{1... | collective-permute-start | bytes 393224 | tf_op jit(solution)/shard_map/ppermute | solution.py:43
  46.0 8.2 %collective-permute-start.18 = (f32[128,256]{1,0:T(8,128)S(1)}, f32[128,256]{1,0:T(8,128)S(1)}, u32[]{:S(2)}, u32[]{:S(2)}) collective-permute-start(f32[128,256]{1,0:T(8,128)S(1)} %add.39), channel_id=1, source_target_pairs={{0,28},{1,5},{2,30},{3,7},{4,0},{5,9},{6,2},{7,11},{8,4},{9,13},{1... | collective-permute-start | bytes 393224 | tf_op jit(solution)/shard_map/ppermute | solution.py:43
  49.4 6.8 %collective-permute-start.15 = (f32[128,256]{1,0:T(8,128)S(1)}, f32[128,256]{1,0:T(8,128)S(1)}, u32[]{:S(2)}, u32[]{:S(2)}) collective-permute-start(f32[128,256]{1,0:T(8,128)S(1)} %add.37), channel_id=1, source_target_pairs={{0,4},{1,29},{2,6},{3,31},{4,8},{5,1},{6,10},{7,3},{8,12},{9,5},{1... | collective-permute-start | bytes 393224 | tf_op jit(solution)/shard_map/ppermute | solution.py:43
  50.8 6.8 %collective-permute-start.22 = (f32[128,256]{1,0:T(8,128)S(1)}, f32[128,256]{1,0:T(8,128)S(1)}, u32[]{:S(2)}, u32[]{:S(2)}) collective-permute-start(f32[128,256]{1,0:T(8,128)S(1)} %add.42), channel_id=1, source_target_pairs={{0,4},{1,29},{2,6},{3,31},{4,8},{5,1},{6,10},{7,3},{8,12},{9,5},{1... | collective-permute-start | bytes 393224 | tf_op jit(solution)/shard_map/ppermute | solution.py:43
  51.0 6.7 %collective-permute-start.12 = (f32[128,256]{1,0:T(8,128)S(1)}, f32[128,256]{1,0:T(8,128)S(1)}, u32[]{:S(2)}, u32[]{:S(2)}) collective-permute-start(f32[128,256]{1,0:T(8,128)S(1)} %add.35), channel_id=1, source_target_pairs={{0,28},{1,5},{2,30},{3,7},{4,0},{5,9},{6,2},{7,11},{8,4},{9,13},{1... | collective-permute-start | bytes 393224 | tf_op jit(solution)/shard_map/ppermute | solution.py:43
  54.3 1.1 copy-start.4
  54.3 5.0 %collective-permute-start.19 = (f32[128,256]{1,0:T(8,128)S(1)}, f32[128,256]{1,0:T(8,128)S(1)}, u32[]{:S(2)}, u32[]{:S(2)}) collective-permute-start(f32[128,256]{1,0:T(8,128)S(1)} %add.40), channel_id=1, source_target_pairs={{0,28},{1,5},{2,30},{3,7},{4,0},{5,9},{6,2},{7,11},{8,4},{9,13},{1... | collective-permute-start | bytes 393224 | tf_op jit(solution)/shard_map/ppermute | solution.py:43
  55.4 6.3 %collective-permute-start.23 = (f32[128,256]{1,0:T(8,128)S(1)}, f32[128,256]{1,0:T(8,128)S(1)}, u32[]{:S(2)}, u32[]{:S(2)}) collective-permute-start(f32[128,256]{1,0:T(8,128)S(1)} %copy-done.4), channel_id=1, source_target_pairs={{0,2},{1,3},{2,0},{3,1},{4,6},{5,7},{6,4},{7,5},{8,10},{9,11},{10,... | collective-permute-start | bytes 393224 | tf_op jit(solution)/shard_map/ppermute | solution.py:460
  59.3 8.8 %copy-start.2 = (f32[256,256]{1,0:T(8,128)S(1)}, f32[256,256]{1,0:T(8,128)}, u32[]{:S(2)}) copy-start(f32[256,256]{1,0:T(8,128)} %weight.3) | copy-start | bytes 786436
  59.4 8.7 %copy-start.9 = (f32[256]{0:T(256)S(1)}, f32[256]{0:T(256)}, u32[]{:S(2)}) copy-start(f32[256]{0:T(256)} %param.9) | copy-start | bytes 3076
  61.7 6.4 %collective-permute-start.24 = (f32[256,256]{1,0:T(8,128)S(1)}, f32[256,256]{1,0:T(8,128)S(1)}, u32[]{:S(2)}, u32[]{:S(2)}) collective-permute-start(f32[256,256]{1,0:T(8,128)S(1)} %last_sum.1.mine), channel_id=1, source_target_pairs={{0,2},{1,3},{2,0},{3,1},{4,6},{5,7},{6,4},{7,5},{8,10},{9,11},{10,... | collective-permute-start | bytes 786440 | tf_op jit(solution)/shard_map/ppermute | solution.py:464
  70.1 12.4 %collective-permute-start.28 = (f32[256,256]{1,0:T(8,128)}, f32[256,256]{1,0:T(8,128)}, u32[]{:S(2)}, u32[]{:S(2)}) collective-permute-start(f32[256,256]{1,0:T(8,128)} %get-tuple-element.80.refs_0_), channel_id=1, source_target_pairs={{0,24},{1,9},{2,26},{3,11},{4,28},{5,13},{6,30},{7,15},{8,0},{9,17... | collective-permute-start | bytes 786440 | tf_op jit(solution)/shard_map/ppermute | solution.py:43
  70.1 15.7 %collective-permute-start.26 = (f32[256,256]{1,0:T(8,128)}, f32[256,256]{1,0:T(8,128)}, u32[]{:S(2)}, u32[]{:S(2)}) collective-permute-start(f32[256,256]{1,0:T(8,128)} %get-tuple-element.80.refs_0_), channel_id=1, source_target_pairs={{0,8},{1,25},{2,10},{3,27},{4,12},{5,29},{6,14},{7,31},{8,16},{9,1... | collective-permute-start | bytes 786440 | tf_op jit(solution)/shard_map/ppermute | solution.py:43
  73.0 17.4 %collective-permute-start.32 = (f32[256,256]{1,0:T(8,128)}, f32[256,256]{1,0:T(8,128)}, u32[]{:S(2)}, u32[]{:S(2)}) collective-permute-start(f32[256,256]{1,0:T(8,128)} %get-tuple-element.80.refs_0_), channel_id=1, source_target_pairs={{0,28},{1,5},{2,30},{3,7},{4,0},{5,9},{6,2},{7,11},{8,4},{9,13},{1... | collective-permute-start | bytes 786440 | tf_op jit(solution)/shard_map/ppermute | solution.py:43
  75.0 22.9 %collective-permute-start.25 = (f32[256,256]{1,0:T(8,128)}, f32[256,256]{1,0:T(8,128)}, u32[]{:S(2)}, u32[]{:S(2)}) collective-permute-start(f32[256,256]{1,0:T(8,128)} %get-tuple-element.80.refs_0_), channel_id=1, source_target_pairs={{0,4},{1,29},{2,6},{3,31},{4,8},{5,1},{6,10},{7,3},{8,12},{9,5},{1... | collective-permute-start | bytes 786440 | tf_op jit(solution)/shard_map/ppermute | solution.py:43
  75.0 16.8 %all-to-all-start = ((f32[8,40,256]{2,1,0:T(8,128)}), f32[8,40,256]{2,1,0:T(8,128)}, u32[]{:S(2)}, u32[]{:S(2)}) async-start(f32[8,40,256]{2,1,0:T(8,128)} %get-tuple-element.91), calls=%async_computation | async-start | bytes 655360 | tf_op jit(solution)/shard_map/all_to_all | solution.py:471
  82.5 17.8 %collective-permute-start.31 = (f32[256,256]{1,0:T(8,128)}, f32[256,256]{1,0:T(8,128)}, u32[]{:S(2)}, u32[]{:S(2)}) collective-permute-start(f32[256,256]{1,0:T(8,128)} %collective-permute-done.28.six.refs_7_), channel_id=1, source_target_pairs={{0,28},{1,5},{2,30},{3,7},{4,0},{5,9},{6,2},{7,11},{8,4},{9,13},{1... | collective-permute-start | bytes 786440 | tf_op jit(solution)/shard_map/ppermute | solution.py:43
  85.8 14.6 %collective-permute-start.27 = (f32[256,256]{1,0:T(8,128)}, f32[256,256]{1,0:T(8,128)}, u32[]{:S(2)}, u32[]{:S(2)}) collective-permute-start(f32[256,256]{1,0:T(8,128)} %collective-permute-done.26.two.refs_2_), channel_id=1, source_target_pairs={{0,4},{1,29},{2,6},{3,31},{4,8},{5,1},{6,10},{7,3},{8,12},{9,5},{1... | collective-permute-start | bytes 786440 | tf_op jit(solution)/shard_map/ppermute | solution.py:43
  87.3 10.6 %collective-permute-start.29 = (f32[128,256]{1,0:T(8,128)S(1)}, f32[128,256]{1,0:T(8,128)S(1)}, u32[]{:S(2)}, u32[]{:S(2)}) collective-permute-start(f32[128,256]{1,0:T(8,128)S(1)} %get-tuple-element.81), channel_id=1, source_target_pairs={{0,24},{1,9},{2,26},{3,11},{4,28},{5,13},{6,30},{7,15},{8,0},{9,17... | collective-permute-start | bytes 393224 | tf_op jit(solution)/shard_map/ppermute | solution.py:43
  90.4 9.9 %collective-permute-start.30 = (f32[128,256]{1,0:T(8,128)S(1)}, f32[128,256]{1,0:T(8,128)S(1)}, u32[]{:S(2)}, u32[]{:S(2)}) collective-permute-start(f32[128,256]{1,0:T(8,128)S(1)} %get-tuple-element.82), channel_id=1, source_target_pairs={{0,8},{1,25},{2,10},{3,27},{4,12},{5,29},{6,14},{7,31},{8,16},{9,1... | collective-permute-start | bytes 393224 | tf_op jit(solution)/shard_map/ppermute | solution.py:43
  93.6 19.7 %all-to-all-start.1 = ((f32[8,40,256]{2,1,0:T(8,128)}), f32[8,40,256]{2,1,0:T(8,128)}, u32[]{:S(2)}, u32[]{:S(2)}) async-start(f32[8,40,256]{2,1,0:T(8,128)} %spread.1), calls=%async_computation.1 | async-start | bytes 655360 | tf_op jit(solution)/shard_map/all_to_all | solution.py:472
  100.3 5.9 %copy-start.1 = (f32[1,1,12,128,128]{4,3,2,1,0:T(8,128)S(1)}, f32[1,1,12,128,128]{4,3,2,1,0:T(8,128)}, u32[]{:S(2)}) copy-start(f32[1,1,12,128,128]{4,3,2,1,0:T(8,128)} %param.10) | copy-start | bytes 2359300
  102.0 4.3 %copy-start.6 = (s32[12,2]{1,0:T(8,128)S(1)}, s32[12,2]{1,0:T(8,128)}, u32[]{:S(2)}) copy-start(s32[12,2]{1,0:T(8,128)} %copy-done.5) | copy-start | bytes 292
  102.0 2.0 %collective-permute-start.33 = (f32[512,256]{1,0:T(8,128)S(1)}, f32[512,256]{1,0:T(8,128)S(1)}, u32[]{:S(2)}, u32[]{:S(2)}) collective-permute-start(f32[512,256]{1,0:T(8,128)S(1)} %get-tuple-element.83.refs_0_), channel_id=1, source_target_pairs={{0,1},{1,0},{2,3},{3,2},{4,5},{5,4},{6,7},{7,6},{8,9},{9,8},{10,11... | collective-permute-start | bytes 1572872 | tf_op jit(solution)/shard_map/ppermute | solution.py:477
  102.1 2.6 %collective-permute-start.34 = (f32[512,256]{1,0:T(8,128)S(1)}, f32[512,256]{1,0:T(8,128)S(1)}, u32[]{:S(2)}, u32[]{:S(2)}) collective-permute-start(f32[512,256]{1,0:T(8,128)S(1)} %get-tuple-element.84.refs_1_), channel_id=1, source_target_pairs={{0,1},{1,0},{2,3},{3,2},{4,5},{5,4},{6,7},{7,6},{8,9},{9,8},{10,11... | collective-permute-start | bytes 1572872 | tf_op jit(solution)/shard_map/ppermute | solution.py:477
  102.6 2.9 %collective-permute-start.35 = (f32[512,256]{1,0:T(8,128)S(1)}, f32[512,256]{1,0:T(8,128)S(1)}, u32[]{:S(2)}, u32[]{:S(2)}) collective-permute-start(f32[512,256]{1,0:T(8,128)S(1)} %get-tuple-element.85.refs_2_), channel_id=1, source_target_pairs={{0,1},{1,0},{2,3},{3,2},{4,5},{5,4},{6,7},{7,6},{8,9},{9,8},{10,11... | collective-permute-start | bytes 1572872 | tf_op jit(solution)/shard_map/ppermute | solution.py:477
  102.7 3.6 %copy-start.8 = (s32[5]{0:T(128)S(1)}, s32[5]{0:T(128)}, u32[]{:S(2)}) copy-start(s32[5]{0:T(128)} %copy-done.7) | copy-start | bytes 64
  102.7 3.5 %collective-permute-start.36 = (f32[512,256]{1,0:T(8,128)S(1)}, f32[512,256]{1,0:T(8,128)S(1)}, u32[]{:S(2)}, u32[]{:S(2)}) collective-permute-start(f32[512,256]{1,0:T(8,128)S(1)} %get-tuple-element.86.refs_3_), channel_id=1, source_target_pairs={{0,1},{1,0},{2,3},{3,2},{4,5},{5,4},{6,7},{7,6},{8,9},{9,8},{10,11... | collective-permute-start | bytes 1572872 | tf_op jit(solution)/shard_map/ppermute | solution.py:477
  108.3 15.9 %collective-permute-start.42 = (f32[128,256]{1,0:T(8,128)S(1)}, f32[128,256]{1,0:T(8,128)S(1)}, u32[]{:S(2)}, u32[]{:S(2)}) collective-permute-start(f32[128,256]{1,0:T(8,128)S(1)} %get-tuple-element.97), channel_id=1, source_target_pairs={{0,64},{32,96},{64,128},{96,160},{128,192},{160,224},{192,0},{224,... | collective-permute-start | bytes 393224 | tf_op jit(solution)/shard_map/ppermute | solution.py:56
  109.5 14.7 %collective-permute-start.43 = (f32[128,256]{1,0:T(8,128)S(1)}, f32[128,256]{1,0:T(8,128)S(1)}, u32[]{:S(2)}, u32[]{:S(2)}) collective-permute-start(f32[128,256]{1,0:T(8,128)S(1)} %get-tuple-element.98), channel_id=1, source_target_pairs={{0,128},{32,160},{64,192},{96,224},{128,0},{160,32},{192,64},{224,... | collective-permute-start | bytes 393224 | tf_op jit(solution)/shard_map/ppermute | solution.py:56
  111.6 12.6 %collective-permute-start.44 = (f32[128,256]{1,0:T(8,128)S(1)}, f32[128,256]{1,0:T(8,128)S(1)}, u32[]{:S(2)}, u32[]{:S(2)}) collective-permute-start(f32[128,256]{1,0:T(8,128)S(1)} %get-tuple-element.99), channel_id=1, source_target_pairs={{0,192},{32,224},{64,0},{96,32},{128,64},{160,96},{192,128},{224,1... | collective-permute-start | bytes 393224 | tf_op jit(solution)/shard_map/ppermute | solution.py:56
  114.2 1.3 collective-permute-start.37
  115.6 5.5 %collective-permute-start.38 = (f32[40,256]{1,0:T(8,128)S(1)}, f32[40,256]{1,0:T(8,128)S(1)}, u32[]{:S(2)}, u32[]{:S(2)}) collective-permute-start(f32[40,256]{1,0:T(8,128)S(1)} %add.43.piece), channel_id=1, source_target_pairs={{0,32},{32,0},{64,96},{96,64},{128,160},{160,128},{192,224},{224,1... | collective-permute-start | bytes 122888 | tf_op jit(solution)/shard_map/ppermute | solution.py:60
  121.1 8.3 %collective-permute-start.39 = (f32[208,256]{1,0:T(8,128)S(1)}, f32[208,256]{1,0:T(8,128)S(1)}, u32[]{:S(2)}, u32[]{:S(2)}) collective-permute-start(f32[208,256]{1,0:T(8,128)S(1)} %get-tuple-element.92), channel_id=1, source_target_pairs={{0,64},{32,96},{64,128},{96,160},{128,192},{160,224},{192,0},{224,... | collective-permute-start | bytes 638984 | tf_op jit(solution)/shard_map/ppermute | solution.py:56
  121.6 9.7 %collective-permute-start.40 = (f32[208,256]{1,0:T(8,128)S(1)}, f32[208,256]{1,0:T(8,128)S(1)}, u32[]{:S(2)}, u32[]{:S(2)}) collective-permute-start(f32[208,256]{1,0:T(8,128)S(1)} %get-tuple-element.93), channel_id=1, source_target_pairs={{0,128},{32,160},{64,192},{96,224},{128,0},{160,32},{192,64},{224,... | collective-permute-start | bytes 638984 | tf_op jit(solution)/shard_map/ppermute | solution.py:56
  124.2 9.3 %collective-permute-start.41 = (f32[208,256]{1,0:T(8,128)S(1)}, f32[208,256]{1,0:T(8,128)S(1)}, u32[]{:S(2)}, u32[]{:S(2)}) collective-permute-start(f32[208,256]{1,0:T(8,128)S(1)} %get-tuple-element.94), channel_id=1, source_target_pairs={{0,192},{32,224},{64,0},{96,32},{128,64},{160,96},{192,128},{224,1... | collective-permute-start | bytes 638984 | tf_op jit(solution)/shard_map/ppermute | solution.py:56
  124.3 10.6 %collective-permute-start.45 = (f32[128,256]{1,0:T(8,128)S(1)}, f32[128,256]{1,0:T(8,128)S(1)}, u32[]{:S(2)}, u32[]{:S(2)}) collective-permute-start(f32[128,256]{1,0:T(8,128)S(1)} %gather_sums.1), channel_id=1, source_target_pairs={{0,32},{32,0},{64,96},{96,64},{128,160},{160,128},{192,224},{224,1... | collective-permute-start | bytes 393224 | tf_op jit(solution)/shard_map/ppermute | solution.py:60
  133.5 1.3 copy-start.3

commit v7 on v6

--- a/solution.py
+++ b/solution.py
@@ -380,8 +380,26 @@
     )(*parts)
 
 
-def unpack_kernel(where, home, one, two, three, piece, piece_across, back, weight_grad, bias_grad):
+def near_sum_kernel(home, one, two, three, back):
     back[...] = (home[...] + one[:TILE, :]) + (two[:TILE, :] + three[:TILE, :])
+
+
+def near_sum(home, one, two, three):
+    return pl.pallas_call(
+        near_sum_kernel,
+        out_shape=shaped(*home.shape),
+        in_specs=[VMEM] * 4,
+        out_specs=VMEM,
+        compiler_params=params(5),
+        cost_estimate=pl.CostEstimate(flops=UNPACK_COST, bytes_accessed=0, transcendentals=0),
+        name="near_sum",
+    )(home, one, two, three)
+
+
+def final_kernel(
+    where, back, partner, weight, one, two, three, piece, piece_across, result, weight_grad, bias_grad
+):
+    result[...] = dot3(split(back[...] + partner[...]), split(weight[...]), ((1,), (1,)))
     rows = weight_grad.shape[0] // (X * YH)
     step = rows + 8
     for distance, source in enumerate((None, three, two, one)):
@@ -397,31 +415,19 @@
     bias_grad[...] = piece[rows : rows + 1, :]
 
 
-def unpack(where, home, one, two, three, piece, piece_across, shape):
-    return pl.pallas_call(
-        unpack_kernel,
-        out_shape=(shaped(*home.shape), shaped(*shape), shaped(1, shape[1])),
-        in_specs=[SMEM] + [VMEM] * 6,
+def final(where, back, partner, weight, near, piece, piece_across):
+    return pl.pallas_call(
+        final_kernel,
+        out_shape=(
+            shaped(TILE, weight.shape[0]),
+            shaped(*weight.shape),
+            shaped(1, weight.shape[1]),
+        ),
+        in_specs=[SMEM] + [VMEM] * 8,
         out_specs=(VMEM,) * 3,
-        compiler_params=params(5),
-        cost_estimate=pl.CostEstimate(flops=UNPACK_COST, bytes_accessed=0, transcendentals=0),
-        name="unpack",
-    )(where, home, one, two, three, piece, piece_across)
-
-
-def final_kernel(back, partner, weight, result):
-    result[...] = dot3(split(back[...] + partner[...]), split(weight[...]), ((1,), (1,)))
-
-
-def final(back, partner, weight):
-    return pl.pallas_call(
-        final_kernel,
-        out_shape=shaped(TILE, weight.shape[0]),
-        in_specs=[VMEM] * 3,
-        out_specs=VMEM,
-        compiler_params=params(3),
+        compiler_params=params(6),
         name="final",
-    )(back, partner, weight)
+    )(where, back, partner, weight, *near, piece, piece_across)
 
 
 def body(node_features, weight, bias, tile_values, tile_coords, tile_count, cotangent):
@@ -482,8 +488,10 @@
     near = pack(*near, piece, piece_across)
     sums = gather_sums(cross, x_shift(one, 1), x_shift(two, 2), x_shift(three, -1))
     near = [x_shift(part, distance) for part, distance in zip(near, (1, 2, -1))]
-    back, weight_grad, bias_grad = unpack(where, home, *near, piece, piece_across, weight.shape)
-    input_grad = final(back, h_swap(sums), weight)
+    back = near_sum(home, *near)
+    input_grad, weight_grad, bias_grad = final(
+        where, back, h_swap(sums), weight, near, piece, piece_across
+    )
     return (output, input_grad, weight_grad, bias_grad.reshape(width))
 
 

time: 137 us -> 137 us (level)
  transfers between devices with their start and end apart: 48 -> 48, of which waited for: 25 -> 25; matrix products, arithmetic and copies ran while one was open for 0% -> 0% of each run, Pallas kernels for 7% -> 6%
where the time goes in v7:
time: 137 us; the launch traced here: 136 us
  starting transfers between devices  70.7 us (52%)
  waiting for transfers between devices  46.7 us (34%)
  Pallas kernels  14.2 us (10%)
  local copies, waits for them, and re-layouts  2.7 us (2%)
  between operations  1.55 us (1%)
    ppermute x22, starting transfers between devices, z_shift(): return lax.ppermute(value, 'col', col_pairs(move))  37.9 us
    ppermute x12, starting transfers between devices, x_shift(): return lax.ppermute(value, 'row', row_pairs(lambda x, h: (x + distance, h)))  16.4 us
    ppermute x12, waiting for transfers between devices, x_shift(): return lax.ppermute(value, 'row', row_pairs(lambda x, h: (x + distance, h)))  13.4 us
    ppermute x22, waiting for transfers between devices, z_shift(): return lax.ppermute(value, 'col', col_pairs(move))  12.8 us
    ppermute x1, waiting for transfers between devices, body(): summed_other = lax.ppermute(summed, 'col', Y_SWAP)  5.69 us
    ppermute x3, waiting for transfers between devices, h_swap(): return lax.ppermute(value, 'row', row_pairs(lambda x, h: (x, 1 - h)))  5.5 us
    all_to_all x1, starting transfers between devices, body(): parts = lax.all_to_all(extra, 'row', 0, 0)  5.15 us
    all_to_all x1, starting transfers between devices, body(): lax.all_to_all(spread(parts, Z), 'col', 0, 0, axis_index_groups=Z_GROUPS)  4.27 us
  transfers between devices with their start and end apart: 48, of which 25 were waited for; matrix products, arithmetic and copies ran while one was open for 0% of the time, Pallas kernels for 6%

profile of v7, /device:TPU:2, one launch (start us, length us, event | category | flops | bytes accessed | tf_op | source)
XLA Modules:
  0.0 136.0 jit_solution(1871168612111707761)
XLA Ops:
  0.6 3.3 %collective-permute-start.3 = (f32[128,256]{1,0:T(8,128)}, f32[128,256]{1,0:T(8,128)}, u32[]{:S(2)}, u32[]{:S(2)}) collective-permute-start(f32[128,256]{1,0:T(8,128)} %refs_0_.1), channel_id=1, source_target_pairs={{0,32},{32,0},{64,96},{96,64},{128,160},{160,128},{192,224},{224,1... | collective-permute-start | bytes 393224 | tf_op jit(solution)/shard_map/ppermute | solution.py:60
  3.9 1.5 %collective-permute-start.2 = (f32[128,256]{1,0:T(8,128)}, f32[128,256]{1,0:T(8,128)S(1)}, u32[]{:S(2)}, u32[]{:S(2)}) collective-permute-start(f32[128,256]{1,0:T(8,128)} %refs_0_.1), channel_id=1, source_target_pairs={{0,64},{32,96},{64,128},{96,160},{128,192},{160,224},{192,0},{224,... | collective-permute-start | bytes 393224 | tf_op jit(solution)/shard_map/ppermute | solution.py:56
  5.4 1.1 collective-permute-start.1
  6.5 2.2 %collective-permute-start = (f32[128,256]{1,0:T(8,128)}, f32[128,256]{1,0:T(8,128)S(1)}, u32[]{:S(2)}, u32[]{:S(2)}) collective-permute-start(f32[128,256]{1,0:T(8,128)} %refs_0_.1), channel_id=1, source_target_pairs={{0,192},{32,224},{64,0},{96,32},{128,64},{160,96},{192,128},{224,1... | collective-permute-start | bytes 393224 | tf_op jit(solution)/shard_map/ppermute | solution.py:56
  9.3 0.7 copy-done.11
  10.3 3.5 %collective-permute-start.5 = (f32[128,256]{1,0:T(8,128)}, f32[128,256]{1,0:T(8,128)}, u32[]{:S(2)}, u32[]{:S(2)}) collective-permute-start(f32[128,256]{1,0:T(8,128)} %collective-permute-done.3.a), channel_id=1, source_target_pairs={{0,128},{32,160},{64,192},{96,224},{128,0},{160,32},{192,64},{224,... | collective-permute-start | bytes 393224 | tf_op jit(solution)/shard_map/ppermute | solution.py:56
  13.8 0.6 collective-permute-done.refs_1_
  14.4 0.9 copy-done.10
  15.4 0.8 collective-permute-done.6.d
  16.2 2.5 %collective-permute-done.5.c = f32[128,256]{1,0:T(8,128)} collective-permute-done((f32[128,256]{1,0:T(8,128)}, f32[128,256]{1,0:T(8,128)}, u32[]{:S(2)}, u32[]{:S(2)}) %collective-permute-start.5) | collective-permute-done | bytes 131104 | tf_op jit(solution)/shard_map/ppermute | solution.py:56
  18.8 1.0 collective-permute-done.4.b
  19.8 2.7 %forward_tiles.1 = (f32[8,128,256]{2,1,0:T(8,128)S(1)}, f32[8,128,256]{2,1,0:T(8,128)S(1)}, f32[8,128,256]{2,1,0:T(8,128)S(1)}, f32[8,128,256]{2,1,0:T(8,128)S(1)}) custom-call(s32[12,2]{1,0:T(8,128)S(1)} %copy.11.place, s32[1]{0:T(128)} %bitcast.10.count, s32[5]{0:T(128)S(1)} %stack.23.where, f32[12,128,128]{2,1,0:T(8,128)S(1)} %bitcast.12, ...), custom_call_target="tpu_custom_call" | custom-call | tf_op jit(solution)/shard_map/forward_tiles/pallas_call | solution.py:145
  22.6 2.6 %collective-permute-done.7.second = f32[8,128,256]{2,1,0:T(8,128)S(1)} collective-permute-done((f32[8,128,256]{2,1,0:T(8,128)S(1)}, f32[8,128,256]{2,1,0:T(8,128)S(1)}, u32[]{:S(2)}, u32[]{:S(2)}) %collective-permute-start.7) | collective-permute-done | bytes 1048608 | tf_op jit(solution)/shard_map/ppermute | solution.py:461
  25.5 5.9 %collective-permute-start.9 = (f32[128,256]{1,0:T(8,128)S(1)}, f32[128,256]{1,0:T(8,128)S(1)}, u32[]{:S(2)}, u32[]{:S(2)}) collective-permute-start(f32[128,256]{1,0:T(8,128)S(1)} %get-tuple-element.65), channel_id=1, source_target_pairs={{0,28},{1,5},{2,30},{3,7},{4,0},{5,9},{6,2},{7,11},{8,4},{9,13},{1... | collective-permute-start | bytes 393224 | tf_op jit(solution)/shard_map/ppermute | solution.py:43
  31.5 1.0 collective-permute-start.16
  32.5 1.0 collective-permute-start.13
  33.5 1.7 %collective-permute-done.9 = f32[128,256]{1,0:T(8,128)S(1)} collective-permute-done((f32[128,256]{1,0:T(8,128)S(1)}, f32[128,256]{1,0:T(8,128)S(1)}, u32[]{:S(2)}, u32[]{:S(2)}) %collective-permute-start.9) | collective-permute-done | bytes 131104 | tf_op jit(solution)/shard_map/ppermute | solution.py:43
  35.3 3.8 %collective-permute-start.10 = (f32[128,256]{1,0:T(8,128)S(1)}, f32[128,256]{1,0:T(8,128)S(1)}, u32[]{:S(2)}, u32[]{:S(2)}) collective-permute-start(f32[128,256]{1,0:T(8,128)S(1)} %add.33), channel_id=1, source_target_pairs={{0,28},{1,5},{2,30},{3,7},{4,0},{5,9},{6,2},{7,11},{8,4},{9,13},{1... | collective-permute-start | bytes 393224 | tf_op jit(solution)/shard_map/ppermute | solution.py:43
  39.1 2.5 %collective-permute-start.17 = (f32[128,256]{1,0:T(8,128)S(1)}, f32[128,256]{1,0:T(8,128)S(1)}, u32[]{:S(2)}, u32[]{:S(2)}) collective-permute-start(f32[128,256]{1,0:T(8,128)S(1)} %add.38), channel_id=1, source_target_pairs={{0,28},{1,5},{2,30},{3,7},{4,0},{5,9},{6,2},{7,11},{8,4},{9,13},{1... | collective-permute-start | bytes 393224 | tf_op jit(solution)/shard_map/ppermute | solution.py:43
  41.8 0.5 collective-permute-done.20
  42.8 3.2 %collective-permute-start.11 = (f32[128,256]{1,0:T(8,128)S(1)}, f32[128,256]{1,0:T(8,128)S(1)}, u32[]{:S(2)}, u32[]{:S(2)}) collective-permute-start(f32[128,256]{1,0:T(8,128)S(1)} %add.34), channel_id=1, source_target_pairs={{0,28},{1,5},{2,30},{3,7},{4,0},{5,9},{6,2},{7,11},{8,4},{9,13},{1... | collective-permute-start | bytes 393224 | tf_op jit(solution)/shard_map/ppermute | solution.py:43
  46.0 2.2 %collective-permute-start.18 = (f32[128,256]{1,0:T(8,128)S(1)}, f32[128,256]{1,0:T(8,128)S(1)}, u32[]{:S(2)}, u32[]{:S(2)}) collective-permute-start(f32[128,256]{1,0:T(8,128)S(1)} %add.39), channel_id=1, source_target_pairs={{0,28},{1,5},{2,30},{3,7},{4,0},{5,9},{6,2},{7,11},{8,4},{9,13},{1... | collective-permute-start | bytes 393224 | tf_op jit(solution)/shard_map/ppermute | solution.py:43
  48.2 1.2 collective-permute-done.14
  49.5 1.3 collective-permute-done.21
  51.0 3.3 %collective-permute-start.12 = (f32[128,256]{1,0:T(8,128)S(1)}, f32[128,256]{1,0:T(8,128)S(1)}, u32[]{:S(2)}, u32[]{:S(2)}) collective-permute-start(f32[128,256]{1,0:T(8,128)S(1)} %add.35), channel_id=1, source_target_pairs={{0,28},{1,5},{2,30},{3,7},{4,0},{5,9},{6,2},{7,11},{8,4},{9,13},{1... | collective-permute-start | bytes 393224 | tf_op jit(solution)/shard_map/ppermute | solution.py:43
  54.3 1.1 collective-permute-start.19
  55.4 0.7 collective-permute-start.23
  56.2 1.4 %collective-permute-done.22.refs_5_ = f32[128,256]{1,0:T(8,128)S(1)} collective-permute-done((f32[128,256]{1,0:T(8,128)S(1)}, f32[128,256]{1,0:T(8,128)S(1)}, u32[]{:S(2)}, u32[]{:S(2)}) %collective-permute-start.22) | collective-permute-done | bytes 131104 | tf_op jit(solution)/shard_map/ppermute | solution.py:43
  57.6 1.7 %collective-permute-done.19.refs_4_ = f32[128,256]{1,0:T(8,128)S(1)} collective-permute-done((f32[128,256]{1,0:T(8,128)S(1)}, f32[128,256]{1,0:T(8,128)S(1)}, u32[]{:S(2)}, u32[]{:S(2)}) %collective-permute-start.19) | collective-permute-done | bytes 131104 | tf_op jit(solution)/shard_map/ppermute | solution.py:43
  59.4 2.3 %collective-permute-done.23.cot_other = f32[128,256]{1,0:T(8,128)S(1)} collective-permute-done((f32[128,256]{1,0:T(8,128)S(1)}, f32[128,256]{1,0:T(8,128)S(1)}, u32[]{:S(2)}, u32[]{:S(2)}) %collective-permute-start.23) | collective-permute-done | bytes 131104 | tf_op jit(solution)/shard_map/ppermute | solution.py:466
  61.7 0.7 collective-permute-start.24
  62.4 5.7 %collective-permute-done.24.other = f32[256,256]{1,0:T(8,128)S(1)} collective-permute-done((f32[256,256]{1,0:T(8,128)S(1)}, f32[256,256]{1,0:T(8,128)S(1)}, u32[]{:S(2)}, u32[]{:S(2)}) %collective-permute-start.24) | collective-permute-done | bytes 262176 | tf_op jit(solution)/shard_map/ppermute | solution.py:470
  68.1 2.0 %middle.1 = (f32[128,256]{1,0:T(8,128)}, f32[256,256]{1,0:T(8,128)}, f32[8,40,256]{2,1,0:T(8,128)}) custom-call(s32[5]{0:T(128)S(1)} %stack.23.where, f32[256,256]{1,0:T(8,128)S(1)} %last_sum.1.mine, f32[256,256]{1,0:T(8,128)S(1)} %collective-permute-done.24.other, f32[256,256]{1,0:T(8,128)S(1)} %copy-done.2, f32[1,256]{1,0:T(1,128)S(1)} %bitcast.14, ...), custom_call_target="tpu_custom_call" | custom-call | tf_op jit(solution)/shard_map/middle/pallas_call | solution.py:224
  70.1 2.9 %collective-permute-start.26 = (f32[256,256]{1,0:T(8,128)}, f32[256,256]{1,0:T(8,128)}, u32[]{:S(2)}, u32[]{:S(2)}) collective-permute-start(f32[256,256]{1,0:T(8,128)} %get-tuple-element.80.refs_0_), channel_id=1, source_target_pairs={{0,8},{1,25},{2,10},{3,27},{4,12},{5,29},{6,14},{7,31},{8,16},{9,1... | collective-permute-start | bytes 786440 | tf_op jit(solution)/shard_map/ppermute | solution.py:43
  73.0 2.0 %collective-permute-start.32 = (f32[256,256]{1,0:T(8,128)}, f32[256,256]{1,0:T(8,128)}, u32[]{:S(2)}, u32[]{:S(2)}) collective-permute-start(f32[256,256]{1,0:T(8,128)} %get-tuple-element.80.refs_0_), channel_id=1, source_target_pairs={{0,28},{1,5},{2,30},{3,7},{4,0},{5,9},{6,2},{7,11},{8,4},{9,13},{1... | collective-permute-start | bytes 786440 | tf_op jit(solution)/shard_map/ppermute | solution.py:43
  75.0 5.2 %all-to-all-start = ((f32[8,40,256]{2,1,0:T(8,128)}), f32[8,40,256]{2,1,0:T(8,128)}, u32[]{:S(2)}, u32[]{:S(2)}) async-start(f32[8,40,256]{2,1,0:T(8,128)} %get-tuple-element.91), calls=%async_computation | async-start | bytes 655360 | tf_op jit(solution)/shard_map/all_to_all | solution.py:477
  80.2 2.3 %collective-permute-done.28.six.refs_7_ = f32[256,256]{1,0:T(8,128)} collective-permute-done((f32[256,256]{1,0:T(8,128)}, f32[256,256]{1,0:T(8,128)}, u32[]{:S(2)}, u32[]{:S(2)}) %collective-permute-start.28) | collective-permute-done | bytes 262176 | tf_op jit(solution)/shard_map/ppermute | solution.py:43
  82.5 3.3 %collective-permute-start.31 = (f32[256,256]{1,0:T(8,128)}, f32[256,256]{1,0:T(8,128)}, u32[]{:S(2)}, u32[]{:S(2)}) collective-permute-start(f32[256,256]{1,0:T(8,128)} %collective-permute-done.28.six.refs_7_), channel_id=1, source_target_pairs={{0,28},{1,5},{2,30},{3,7},{4,0},{5,9},{6,2},{7,11},{8,4},{9,13},{1... | collective-permute-start | bytes 786440 | tf_op jit(solution)/shard_map/ppermute | solution.py:43
  86.2 1.0 halves.1
  87.3 3.1 %collective-permute-start.29 = (f32[128,256]{1,0:T(8,128)S(1)}, f32[128,256]{1,0:T(8,128)S(1)}, u32[]{:S(2)}, u32[]{:S(2)}) collective-permute-start(f32[128,256]{1,0:T(8,128)S(1)} %get-tuple-element.81), channel_id=1, source_target_pairs={{0,24},{1,9},{2,26},{3,11},{4,28},{5,13},{6,30},{7,15},{8,0},{9,17... | collective-permute-start | bytes 393224 | tf_op jit(solution)/shard_map/ppermute | solution.py:43
  90.4 1.5 %collective-permute-start.30 = (f32[128,256]{1,0:T(8,128)S(1)}, f32[128,256]{1,0:T(8,128)S(1)}, u32[]{:S(2)}, u32[]{:S(2)}) collective-permute-start(f32[128,256]{1,0:T(8,128)S(1)} %get-tuple-element.82), channel_id=1, source_target_pairs={{0,8},{1,25},{2,10},{3,27},{4,12},{5,29},{6,14},{7,31},{8,16},{9,1... | collective-permute-start | bytes 393224 | tf_op jit(solution)/shard_map/ppermute | solution.py:43
  91.9 1.7 %spread.1 = f32[8,40,256]{2,1,0:T(8,128)} custom-call(f32[8,40,256]{2,1,0:T(8,128)} %all-to-all-done.parts), custom_call_target="tpu_custom_call" | custom-call | tf_op jit(solution)/shard_map/spread/pallas_call | solution.py:248
  93.6 4.3 %all-to-all-start.1 = ((f32[8,40,256]{2,1,0:T(8,128)}), f32[8,40,256]{2,1,0:T(8,128)}, u32[]{:S(2)}, u32[]{:S(2)}) async-start(f32[8,40,256]{2,1,0:T(8,128)} %spread.1), calls=%async_computation.1 | async-start | bytes 655360 | tf_op jit(solution)/shard_map/all_to_all | solution.py:478
  97.9 2.4 %collective-permute-done.30.refs_5_ = f32[128,256]{1,0:T(8,128)S(1)} collective-permute-done((f32[128,256]{1,0:T(8,128)S(1)}, f32[128,256]{1,0:T(8,128)S(1)}, u32[]{:S(2)}, u32[]{:S(2)}) %collective-permute-start.30) | collective-permute-done | bytes 131104 | tf_op jit(solution)/shard_map/ppermute | solution.py:43
  100.3 1.6 %join.1 = (f32[512,256]{1,0:T(8,128)S(1)}, f32[512,256]{1,0:T(8,128)S(1)}, f32[512,256]{1,0:T(8,128)S(1)}, f32[512,256]{1,0:T(8,128)S(1)}) custom-call(f32[256,256]{1,0:T(8,128)} %get-tuple-element.80.refs_0_, f32[256,256]{1,0:T(8,128)} %collective-permute-done.25.refs_1_, f32[256,256]{1,0:T(8,128)} %collective-permute-done.26.two.refs_2_, ...), custom_call_target="tpu_custom_call" | custom-call | flops 999999995904 | tf_op jit(solution)/shard_map/join/pallas_call | solution.py:286
  102.1 0.5 collective-permute-start.34
  103.1 0.9 collective-permute-done.33.refs_4_
  104.0 0.7 collective-permute-done.34.refs_5_
  104.7 0.7 collective-permute-done.35.refs_6_
  105.5 0.7 collective-permute-done.36.refs_7_
  106.2 2.0 %backward_tiles.1 = (f32[128,256]{1,0:T(8,128)S(1)}, f32[128,256]{1,0:T(8,128)S(1)}, f32[128,256]{1,0:T(8,128)S(1)}, f32[128,256]{1,0:T(8,128)S(1)}, f32[128,256...) custom-call(s32[12,2]{1,0:T(8,128)S(1)} %copy-done.6, ...), custom_call_target="tpu_custom_call" | custom-call | tf_op jit(solution)/shard_map/backward_tiles/pallas_call | solution.py:336
  108.3 1.2 collective-permute-start.42
  109.5 2.1 %collective-permute-start.43 = (f32[128,256]{1,0:T(8,128)S(1)}, f32[128,256]{1,0:T(8,128)S(1)}, u32[]{:S(2)}, u32[]{:S(2)}) collective-permute-start(f32[128,256]{1,0:T(8,128)S(1)} %get-tuple-element.97), channel_id=1, source_target_pairs={{0,128},{32,160},{64,192},{96,224},{128,0},{160,32},{192,64},{224,... | collective-permute-start | bytes 393224 | tf_op jit(solution)/shard_map/ppermute | solution.py:56
  111.6 1.6 %collective-permute-start.44 = (f32[128,256]{1,0:T(8,128)S(1)}, f32[128,256]{1,0:T(8,128)S(1)}, u32[]{:S(2)}, u32[]{:S(2)}) collective-permute-start(f32[128,256]{1,0:T(8,128)S(1)} %get-tuple-element.98), channel_id=1, source_target_pairs={{0,192},{32,224},{64,0},{96,32},{128,64},{160,96},{192,128},{224,1... | collective-permute-start | bytes 393224 | tf_op jit(solution)/shard_map/ppermute | solution.py:56
  113.3 1.0 total.1
  114.4 1.2 collective-permute-done.37
  115.6 5.5 %collective-permute-done.38.piece_across = f32[40,256]{1,0:T(8,128)S(1)} collective-permute-done((f32[40,256]{1,0:T(8,128)S(1)}, f32[40,256]{1,0:T(8,128)S(1)}, u32[]{:S(2)}, u32[]{:S(2)}) %collective-permute-start.38) | collective-permute-done | bytes 40992 | tf_op jit(solution)/shard_map/ppermute | solution.py:60
  121.6 2.6 %collective-permute-start.40 = (f32[208,256]{1,0:T(8,128)S(1)}, f32[208,256]{1,0:T(8,128)S(1)}, u32[]{:S(2)}, u32[]{:S(2)}) collective-permute-start(f32[208,256]{1,0:T(8,128)S(1)} %get-tuple-element.93), channel_id=1, source_target_pairs={{0,128},{32,160},{64,192},{96,224},{128,0},{160,32},{192,64},{224,... | collective-permute-start | bytes 638984 | tf_op jit(solution)/shard_map/ppermute | solution.py:56
  124.3 0.9 collective-permute-start.45
  125.2 4.2 %collective-permute-done.39.one = f32[208,256]{1,0:T(8,128)S(1)} collective-permute-done((f32[208,256]{1,0:T(8,128)S(1)}, f32[208,256]{1,0:T(8,128)S(1)}, u32[]{:S(2)}, u32[]{:S(2)}) %collective-permute-start.39) | collective-permute-done | bytes 213024 | tf_op jit(solution)/shard_map/ppermute | solution.py:56
  129.4 1.9 %collective-permute-done.40.two = f32[208,256]{1,0:T(8,128)S(1)} collective-permute-done((f32[208,256]{1,0:T(8,128)S(1)}, f32[208,256]{1,0:T(8,128)S(1)}, u32[]{:S(2)}, u32[]{:S(2)}) %collective-permute-start.40) | collective-permute-done | bytes 213024 | tf_op jit(solution)/shard_map/ppermute | solution.py:56
  131.3 2.3 %collective-permute-done.41.three = f32[208,256]{1,0:T(8,128)S(1)} collective-permute-done((f32[208,256]{1,0:T(8,128)S(1)}, f32[208,256]{1,0:T(8,128)S(1)}, u32[]{:S(2)}, u32[]{:S(2)}) %collective-permute-start.41) | collective-permute-done | bytes 213024 | tf_op jit(solution)/shard_map/ppermute | solution.py:56
  133.6 0.9 copy-done.3
  134.5 1.5 %final.1 = (f32[128,256]{1,0:T(8,128)}, f32[256,256]{1,0:T(8,128)}, f32[1,256]{1,0:T(1,128)}) custom-call(s32[5]{0:T(128)S(1)} %copy-done.8, f32[128,256]{1,0:T(8,128)S(1)} %near_sum.1.back, f32[128,256]{1,0:T(8,128)S(1)} %collective-permute-done.45.partner, f32[256,256]{1,0:T(8,128)S(1)} %copy-done.3, f32[208,256]{1,0:T(8,128)S(1)} %collective-permute-done.39.one, ...), custom_call_target="tpu_custom_call" | custom-call | tf_op jit(solution)/shard_map/final/pallas_call | solution.py:419
  (84 shorter events, 3.9 us)
Async XLA Ops:
  0.6 9.6 %collective-permute-start.3 = (f32[128,256]{1,0:T(8,128)}, f32[128,256]{1,0:T(8,128)}, u32[]{:S(2)}, u32[]{:S(2)}) collective-permute-start(f32[128,256]{1,0:T(8,128)} %refs_0_.1), channel_id=1, source_target_pairs={{0,32},{32,0},{64,96},{96,64},{128,160},{160,128},{192,224},{224,1... | collective-permute-start | bytes 393224 | tf_op jit(solution)/shard_map/ppermute | solution.py:60
  3.9 9.8 %collective-permute-start.2 = (f32[128,256]{1,0:T(8,128)}, f32[128,256]{1,0:T(8,128)S(1)}, u32[]{:S(2)}, u32[]{:S(2)}) collective-permute-start(f32[128,256]{1,0:T(8,128)} %refs_0_.1), channel_id=1, source_target_pairs={{0,64},{32,96},{64,128},{96,160},{128,192},{160,224},{192,0},{224,... | collective-permute-start | bytes 393224 | tf_op jit(solution)/shard_map/ppermute | solution.py:56
  5.4 8.4 %collective-permute-start.1 = (f32[128,256]{1,0:T(8,128)}, f32[128,256]{1,0:T(8,128)S(1)}, u32[]{:S(2)}, u32[]{:S(2)}) collective-permute-start(f32[128,256]{1,0:T(8,128)} %refs_0_.1), channel_id=1, source_target_pairs={{0,128},{32,160},{64,192},{96,224},{128,0},{160,32},{192,64},{224,... | collective-permute-start | bytes 393224 | tf_op jit(solution)/shard_map/ppermute | solution.py:56
  6.5 7.9 %collective-permute-start = (f32[128,256]{1,0:T(8,128)}, f32[128,256]{1,0:T(8,128)S(1)}, u32[]{:S(2)}, u32[]{:S(2)}) collective-permute-start(f32[128,256]{1,0:T(8,128)} %refs_0_.1), channel_id=1, source_target_pairs={{0,192},{32,224},{64,0},{96,32},{128,64},{160,96},{192,128},{224,1... | collective-permute-start | bytes 393224 | tf_op jit(solution)/shard_map/ppermute | solution.py:56
  9.3 0.7 copy-start.11
  10.1 9.7 %copy-start.5 = (s32[12,2]{1,0:T(8,128)}, s32[12,2]{1,0:T(8,128)S(1)}, u32[]{:S(2)}) copy-start(s32[12,2]{1,0:T(8,128)S(1)} %copy.11.place) | copy-start | bytes 292
  10.2 57.9 %copy-start.7 = (s32[5]{0:T(128)}, s32[5]{0:T(128)S(1)}, u32[]{:S(2)}) copy-start(s32[5]{0:T(128)S(1)} %stack.23.where) | copy-start | bytes 64
  10.2 6.0 %collective-permute-start.6 = (f32[128,256]{1,0:T(8,128)}, f32[128,256]{1,0:T(8,128)}, u32[]{:S(2)}, u32[]{:S(2)}) collective-permute-start(f32[128,256]{1,0:T(8,128)} %collective-permute-done.3.a), channel_id=1, source_target_pairs={{0,64},{32,96},{64,128},{96,160},{128,192},{160,224},{192,0},{224,... | collective-permute-start | bytes 393224 | tf_op jit(solution)/shard_map/ppermute | solution.py:56
  10.3 8.5 %collective-permute-start.5 = (f32[128,256]{1,0:T(8,128)}, f32[128,256]{1,0:T(8,128)}, u32[]{:S(2)}, u32[]{:S(2)}) collective-permute-start(f32[128,256]{1,0:T(8,128)} %collective-permute-done.3.a), channel_id=1, source_target_pairs={{0,128},{32,160},{64,192},{96,224},{128,0},{160,32},{192,64},{224,... | collective-permute-start | bytes 393224 | tf_op jit(solution)/shard_map/ppermute | solution.py:56
  13.8 6.0 %collective-permute-start.4 = (f32[128,256]{1,0:T(8,128)}, f32[128,256]{1,0:T(8,128)}, u32[]{:S(2)}, u32[]{:S(2)}) collective-permute-start(f32[128,256]{1,0:T(8,128)} %collective-permute-done.3.a), channel_id=1, source_target_pairs={{0,192},{32,224},{64,0},{96,32},{128,64},{160,96},{192,128},{224,1... | collective-permute-start | bytes 393224 | tf_op jit(solution)/shard_map/ppermute | solution.py:56
  14.4 0.9 copy-start.10
  15.3 4.5 %copy-start = (f32[1,1,12,128,128]{4,3,2,1,0:T(8,128)S(1)}, f32[1,1,12,128,128]{4,3,2,1,0:T(8,128)}, u32[]{:S(2)}) copy-start(f32[1,1,12,128,128]{4,3,2,1,0:T(8,128)} %param.10) | copy-start | bytes 2359300
  22.5 2.7 %collective-permute-start.7 = (f32[8,128,256]{2,1,0:T(8,128)S(1)}, f32[8,128,256]{2,1,0:T(8,128)S(1)}, u32[]{:S(2)}, u32[]{:S(2)}) collective-permute-start(f32[8,128,256]{2,1,0:T(8,128)S(1)} %get-tuple-element.56), channel_id=1, source_target_pairs={{0,1},{1,0},{2,3},{3,2},{4,5},{5,4},{6,7},{7,6},{8,9},{9,8},{10,11... | collective-permute-start | bytes 3145736 | tf_op jit(solution)/shard_map/ppermute | solution.py:461
  25.3 17.4 %collective-permute-start.8 = (f32[8,128,256]{2,1,0:T(8,128)S(1)}, f32[8,128,256]{2,1,0:T(8,128)S(1)}, u32[]{:S(2)}, u32[]{:S(2)}) collective-permute-start(f32[8,128,256]{2,1,0:T(8,128)S(1)} %get-tuple-element.58), channel_id=1, source_target_pairs={{0,1},{1,0},{2,3},{3,2},{4,5},{5,4},{6,7},{7,6},{8,9},{9,8},{10,11... | collective-permute-start | bytes 3145736 | tf_op jit(solution)/shard_map/ppermute | solution.py:464
  25.5 9.7 %collective-permute-start.9 = (f32[128,256]{1,0:T(8,128)S(1)}, f32[128,256]{1,0:T(8,128)S(1)}, u32[]{:S(2)}, u32[]{:S(2)}) collective-permute-start(f32[128,256]{1,0:T(8,128)S(1)} %get-tuple-element.65), channel_id=1, source_target_pairs={{0,28},{1,5},{2,30},{3,7},{4,0},{5,9},{6,2},{7,11},{8,4},{9,13},{1... | collective-permute-start | bytes 393224 | tf_op jit(solution)/shard_map/ppermute | solution.py:43
  31.5 7.6 %collective-permute-start.16 = (f32[128,256]{1,0:T(8,128)S(1)}, f32[128,256]{1,0:T(8,128)S(1)}, u32[]{:S(2)}, u32[]{:S(2)}) collective-permute-start(f32[128,256]{1,0:T(8,128)S(1)} %get-tuple-element.73), channel_id=1, source_target_pairs={{0,28},{1,5},{2,30},{3,7},{4,0},{5,9},{6,2},{7,11},{8,4},{9,13},{1... | collective-permute-start | bytes 393224 | tf_op jit(solution)/shard_map/ppermute | solution.py:43
  32.5 9.1 %collective-permute-start.13 = (f32[128,256]{1,0:T(8,128)S(1)}, f32[128,256]{1,0:T(8,128)S(1)}, u32[]{:S(2)}, u32[]{:S(2)}) collective-permute-start(f32[128,256]{1,0:T(8,128)S(1)} %get-tuple-element.68), channel_id=1, source_target_pairs={{0,4},{1,29},{2,6},{3,31},{4,8},{5,1},{6,10},{7,3},{8,12},{9,5},{1... | collective-permute-start | bytes 393224 | tf_op jit(solution)/shard_map/ppermute | solution.py:43
  33.5 8.9 %collective-permute-start.20 = (f32[128,256]{1,0:T(8,128)S(1)}, f32[128,256]{1,0:T(8,128)S(1)}, u32[]{:S(2)}, u32[]{:S(2)}) collective-permute-start(f32[128,256]{1,0:T(8,128)S(1)} %get-tuple-element.76), channel_id=1, source_target_pairs={{0,4},{1,29},{2,6},{3,31},{4,8},{5,1},{6,10},{7,3},{8,12},{9,5},{1... | collective-permute-start | bytes 393224 | tf_op jit(solution)/shard_map/ppermute | solution.py:43
  35.3 7.5 %collective-permute-start.10 = (f32[128,256]{1,0:T(8,128)S(1)}, f32[128,256]{1,0:T(8,128)S(1)}, u32[]{:S(2)}, u32[]{:S(2)}) collective-permute-start(f32[128,256]{1,0:T(8,128)S(1)} %add.33), channel_id=1, source_target_pairs={{0,28},{1,5},{2,30},{3,7},{4,0},{5,9},{6,2},{7,11},{8,4},{9,13},{1... | collective-permute-start | bytes 393224 | tf_op jit(solution)/shard_map/ppermute | solution.py:43
  39.1 6.9 %collective-permute-start.17 = (f32[128,256]{1,0:T(8,128)S(1)}, f32[128,256]{1,0:T(8,128)S(1)}, u32[]{:S(2)}, u32[]{:S(2)}) collective-permute-start(f32[128,256]{1,0:T(8,128)S(1)} %add.38), channel_id=1, source_target_pairs={{0,28},{1,5},{2,30},{3,7},{4,0},{5,9},{6,2},{7,11},{8,4},{9,13},{1... | collective-permute-start | bytes 393224 | tf_op jit(solution)/shard_map/ppermute | solution.py:43
  41.6 7.8 %collective-permute-start.14 = (f32[128,256]{1,0:T(8,128)S(1)}, f32[128,256]{1,0:T(8,128)S(1)}, u32[]{:S(2)}, u32[]{:S(2)}) collective-permute-start(f32[128,256]{1,0:T(8,128)S(1)} %add.36), channel_id=1, source_target_pairs={{0,4},{1,29},{2,6},{3,31},{4,8},{5,1},{6,10},{7,3},{8,12},{9,5},{1... | collective-permute-start | bytes 393224 | tf_op jit(solution)/shard_map/ppermute | solution.py:43
  42.4 8.4 %collective-permute-start.21 = (f32[128,256]{1,0:T(8,128)S(1)}, f32[128,256]{1,0:T(8,128)S(1)}, u32[]{:S(2)}, u32[]{:S(2)}) collective-permute-start(f32[128,256]{1,0:T(8,128)S(1)} %add.41), channel_id=1, source_target_pairs={{0,4},{1,29},{2,6},{3,31},{4,8},{5,1},{6,10},{7,3},{8,12},{9,5},{1... | collective-permute-start | bytes 393224 | tf_op jit(solution)/shard_map/ppermute | solution.py:43
  42.8 8.1 %collective-permute-start.11 = (f32[128,256]{1,0:T(8,128)S(1)}, f32[128,256]{1,0:T(8,128)S(1)}, u32[]{:S(2)}, u32[]{:S(2)}) collective-permute-start(f32[128,256]{1,0:T(8,128)S(1)} %add.34), channel_id=1, source_target_pairs={{0,28},{1,5},{2,30},{3,7},{4,0},{5,9},{6,2},{7,11},{8,4},{9,13},{1... | collective-permute-start | bytes 393224 | tf_op jit(solution)/shard_map/ppermute | solution.py:43
  46.0 8.2 %collective-permute-start.18 = (f32[128,256]{1,0:T(8,128)S(1)}, f32[128,256]{1,0:T(8,128)S(1)}, u32[]{:S(2)}, u32[]{:S(2)}) collective-permute-start(f32[128,256]{1,0:T(8,128)S(1)} %add.39), channel_id=1, source_target_pairs={{0,28},{1,5},{2,30},{3,7},{4,0},{5,9},{6,2},{7,11},{8,4},{9,13},{1... | collective-permute-start | bytes 393224 | tf_op jit(solution)/shard_map/ppermute | solution.py:43
  49.4 6.8 %collective-permute-start.15 = (f32[128,256]{1,0:T(8,128)S(1)}, f32[128,256]{1,0:T(8,128)S(1)}, u32[]{:S(2)}, u32[]{:S(2)}) collective-permute-start(f32[128,256]{1,0:T(8,128)S(1)} %add.37), channel_id=1, source_target_pairs={{0,4},{1,29},{2,6},{3,31},{4,8},{5,1},{6,10},{7,3},{8,12},{9,5},{1... | collective-permute-start | bytes 393224 | tf_op jit(solution)/shard_map/ppermute | solution.py:43
  50.8 6.8 %collective-permute-start.22 = (f32[128,256]{1,0:T(8,128)S(1)}, f32[128,256]{1,0:T(8,128)S(1)}, u32[]{:S(2)}, u32[]{:S(2)}) collective-permute-start(f32[128,256]{1,0:T(8,128)S(1)} %add.42), channel_id=1, source_target_pairs={{0,4},{1,29},{2,6},{3,31},{4,8},{5,1},{6,10},{7,3},{8,12},{9,5},{1... | collective-permute-start | bytes 393224 | tf_op jit(solution)/shard_map/ppermute | solution.py:43
  51.0 6.7 %collective-permute-start.12 = (f32[128,256]{1,0:T(8,128)S(1)}, f32[128,256]{1,0:T(8,128)S(1)}, u32[]{:S(2)}, u32[]{:S(2)}) collective-permute-start(f32[128,256]{1,0:T(8,128)S(1)} %add.35), channel_id=1, source_target_pairs={{0,28},{1,5},{2,30},{3,7},{4,0},{5,9},{6,2},{7,11},{8,4},{9,13},{1... | collective-permute-start | bytes 393224 | tf_op jit(solution)/shard_map/ppermute | solution.py:43
  54.3 1.1 copy-start.4
  54.3 5.0 %collective-permute-start.19 = (f32[128,256]{1,0:T(8,128)S(1)}, f32[128,256]{1,0:T(8,128)S(1)}, u32[]{:S(2)}, u32[]{:S(2)}) collective-permute-start(f32[128,256]{1,0:T(8,128)S(1)} %add.40), channel_id=1, source_target_pairs={{0,28},{1,5},{2,30},{3,7},{4,0},{5,9},{6,2},{7,11},{8,4},{9,13},{1... | collective-permute-start | bytes 393224 | tf_op jit(solution)/shard_map/ppermute | solution.py:43
  55.4 6.3 %collective-permute-start.23 = (f32[128,256]{1,0:T(8,128)S(1)}, f32[128,256]{1,0:T(8,128)S(1)}, u32[]{:S(2)}, u32[]{:S(2)}) collective-permute-start(f32[128,256]{1,0:T(8,128)S(1)} %copy-done.4), channel_id=1, source_target_pairs={{0,2},{1,3},{2,0},{3,1},{4,6},{5,7},{6,4},{7,5},{8,10},{9,11},{10,... | collective-permute-start | bytes 393224 | tf_op jit(solution)/shard_map/ppermute | solution.py:466
  59.3 8.8 %copy-start.2 = (f32[256,256]{1,0:T(8,128)S(1)}, f32[256,256]{1,0:T(8,128)}, u32[]{:S(2)}) copy-start(f32[256,256]{1,0:T(8,128)} %weight.3) | copy-start | bytes 786436
  59.4 8.7 %copy-start.9 = (f32[256]{0:T(256)S(1)}, f32[256]{0:T(256)}, u32[]{:S(2)}) copy-start(f32[256]{0:T(256)} %param.9) | copy-start | bytes 3076
  61.7 6.4 %collective-permute-start.24 = (f32[256,256]{1,0:T(8,128)S(1)}, f32[256,256]{1,0:T(8,128)S(1)}, u32[]{:S(2)}, u32[]{:S(2)}) collective-permute-start(f32[256,256]{1,0:T(8,128)S(1)} %last_sum.1.mine), channel_id=1, source_target_pairs={{0,2},{1,3},{2,0},{3,1},{4,6},{5,7},{6,4},{7,5},{8,10},{9,11},{10,... | collective-permute-start | bytes 786440 | tf_op jit(solution)/shard_map/ppermute | solution.py:470
  70.1 12.4 %collective-permute-start.28 = (f32[256,256]{1,0:T(8,128)}, f32[256,256]{1,0:T(8,128)}, u32[]{:S(2)}, u32[]{:S(2)}) collective-permute-start(f32[256,256]{1,0:T(8,128)} %get-tuple-element.80.refs_0_), channel_id=1, source_target_pairs={{0,24},{1,9},{2,26},{3,11},{4,28},{5,13},{6,30},{7,15},{8,0},{9,17... | collective-permute-start | bytes 786440 | tf_op jit(solution)/shard_map/ppermute | solution.py:43
  70.1 15.7 %collective-permute-start.26 = (f32[256,256]{1,0:T(8,128)}, f32[256,256]{1,0:T(8,128)}, u32[]{:S(2)}, u32[]{:S(2)}) collective-permute-start(f32[256,256]{1,0:T(8,128)} %get-tuple-element.80.refs_0_), channel_id=1, source_target_pairs={{0,8},{1,25},{2,10},{3,27},{4,12},{5,29},{6,14},{7,31},{8,16},{9,1... | collective-permute-start | bytes 786440 | tf_op jit(solution)/shard_map/ppermute | solution.py:43
  73.0 17.4 %collective-permute-start.32 = (f32[256,256]{1,0:T(8,128)}, f32[256,256]{1,0:T(8,128)}, u32[]{:S(2)}, u32[]{:S(2)}) collective-permute-start(f32[256,256]{1,0:T(8,128)} %get-tuple-element.80.refs_0_), channel_id=1, source_target_pairs={{0,28},{1,5},{2,30},{3,7},{4,0},{5,9},{6,2},{7,11},{8,4},{9,13},{1... | collective-permute-start | bytes 786440 | tf_op jit(solution)/shard_map/ppermute | solution.py:43
  75.0 22.9 %collective-permute-start.25 = (f32[256,256]{1,0:T(8,128)}, f32[256,256]{1,0:T(8,128)}, u32[]{:S(2)}, u32[]{:S(2)}) collective-permute-start(f32[256,256]{1,0:T(8,128)} %get-tuple-element.80.refs_0_), channel_id=1, source_target_pairs={{0,4},{1,29},{2,6},{3,31},{4,8},{5,1},{6,10},{7,3},{8,12},{9,5},{1... | collective-permute-start | bytes 786440 | tf_op jit(solution)/shard_map/ppermute | solution.py:43
  75.0 16.8 %all-to-all-start = ((f32[8,40,256]{2,1,0:T(8,128)}), f32[8,40,256]{2,1,0:T(8,128)}, u32[]{:S(2)}, u32[]{:S(2)}) async-start(f32[8,40,256]{2,1,0:T(8,128)} %get-tuple-element.91), calls=%async_computation | async-start | bytes 655360 | tf_op jit(solution)/shard_map/all_to_all | solution.py:477
  82.5 17.8 %collective-permute-start.31 = (f32[256,256]{1,0:T(8,128)}, f32[256,256]{1,0:T(8,128)}, u32[]{:S(2)}, u32[]{:S(2)}) collective-permute-start(f32[256,256]{1,0:T(8,128)} %collective-permute-done.28.six.refs_7_), channel_id=1, source_target_pairs={{0,28},{1,5},{2,30},{3,7},{4,0},{5,9},{6,2},{7,11},{8,4},{9,13},{1... | collective-permute-start | bytes 786440 | tf_op jit(solution)/shard_map/ppermute | solution.py:43
  85.8 14.6 %collective-permute-start.27 = (f32[256,256]{1,0:T(8,128)}, f32[256,256]{1,0:T(8,128)}, u32[]{:S(2)}, u32[]{:S(2)}) collective-permute-start(f32[256,256]{1,0:T(8,128)} %collective-permute-done.26.two.refs_2_), channel_id=1, source_target_pairs={{0,4},{1,29},{2,6},{3,31},{4,8},{5,1},{6,10},{7,3},{8,12},{9,5},{1... | collective-permute-start | bytes 786440 | tf_op jit(solution)/shard_map/ppermute | solution.py:43
  87.3 10.6 %collective-permute-start.29 = (f32[128,256]{1,0:T(8,128)S(1)}, f32[128,256]{1,0:T(8,128)S(1)}, u32[]{:S(2)}, u32[]{:S(2)}) collective-permute-start(f32[128,256]{1,0:T(8,128)S(1)} %get-tuple-element.81), channel_id=1, source_target_pairs={{0,24},{1,9},{2,26},{3,11},{4,28},{5,13},{6,30},{7,15},{8,0},{9,17... | collective-permute-start | bytes 393224 | tf_op jit(solution)/shard_map/ppermute | solution.py:43
  90.4 9.9 %collective-permute-start.30 = (f32[128,256]{1,0:T(8,128)S(1)}, f32[128,256]{1,0:T(8,128)S(1)}, u32[]{:S(2)}, u32[]{:S(2)}) collective-permute-start(f32[128,256]{1,0:T(8,128)S(1)} %get-tuple-element.82), channel_id=1, source_target_pairs={{0,8},{1,25},{2,10},{3,27},{4,12},{5,29},{6,14},{7,31},{8,16},{9,1... | collective-permute-start | bytes 393224 | tf_op jit(solution)/shard_map/ppermute | solution.py:43
  93.6 19.7 %all-to-all-start.1 = ((f32[8,40,256]{2,1,0:T(8,128)}), f32[8,40,256]{2,1,0:T(8,128)}, u32[]{:S(2)}, u32[]{:S(2)}) async-start(f32[8,40,256]{2,1,0:T(8,128)} %spread.1), calls=%async_computation.1 | async-start | bytes 655360 | tf_op jit(solution)/shard_map/all_to_all | solution.py:478
  100.3 5.9 %copy-start.1 = (f32[1,1,12,128,128]{4,3,2,1,0:T(8,128)S(1)}, f32[1,1,12,128,128]{4,3,2,1,0:T(8,128)}, u32[]{:S(2)}) copy-start(f32[1,1,12,128,128]{4,3,2,1,0:T(8,128)} %param.10) | copy-start | bytes 2359300
  102.0 4.3 %copy-start.6 = (s32[12,2]{1,0:T(8,128)S(1)}, s32[12,2]{1,0:T(8,128)}, u32[]{:S(2)}) copy-start(s32[12,2]{1,0:T(8,128)} %copy-done.5) | copy-start | bytes 292
  102.0 2.0 %collective-permute-start.33 = (f32[512,256]{1,0:T(8,128)S(1)}, f32[512,256]{1,0:T(8,128)S(1)}, u32[]{:S(2)}, u32[]{:S(2)}) collective-permute-start(f32[512,256]{1,0:T(8,128)S(1)} %get-tuple-element.83.refs_0_), channel_id=1, source_target_pairs={{0,1},{1,0},{2,3},{3,2},{4,5},{5,4},{6,7},{7,6},{8,9},{9,8},{10,11... | collective-permute-start | bytes 1572872 | tf_op jit(solution)/shard_map/ppermute | solution.py:483
  102.1 2.6 %collective-permute-start.34 = (f32[512,256]{1,0:T(8,128)S(1)}, f32[512,256]{1,0:T(8,128)S(1)}, u32[]{:S(2)}, u32[]{:S(2)}) collective-permute-start(f32[512,256]{1,0:T(8,128)S(1)} %get-tuple-element.84.refs_1_), channel_id=1, source_target_pairs={{0,1},{1,0},{2,3},{3,2},{4,5},{5,4},{6,7},{7,6},{8,9},{9,8},{10,11... | collective-permute-start | bytes 1572872 | tf_op jit(solution)/shard_map/ppermute | solution.py:483
  102.6 2.9 %collective-permute-start.35 = (f32[512,256]{1,0:T(8,128)S(1)}, f32[512,256]{1,0:T(8,128)S(1)}, u32[]{:S(2)}, u32[]{:S(2)}) collective-permute-start(f32[512,256]{1,0:T(8,128)S(1)} %get-tuple-element.85.refs_2_), channel_id=1, source_target_pairs={{0,1},{1,0},{2,3},{3,2},{4,5},{5,4},{6,7},{7,6},{8,9},{9,8},{10,11... | collective-permute-start | bytes 1572872 | tf_op jit(solution)/shard_map/ppermute | solution.py:483
  102.7 3.6 %copy-start.8 = (s32[5]{0:T(128)S(1)}, s32[5]{0:T(128)}, u32[]{:S(2)}) copy-start(s32[5]{0:T(128)} %copy-done.7) | copy-start | bytes 64
  102.7 3.5 %collective-permute-start.36 = (f32[512,256]{1,0:T(8,128)S(1)}, f32[512,256]{1,0:T(8,128)S(1)}, u32[]{:S(2)}, u32[]{:S(2)}) collective-permute-start(f32[512,256]{1,0:T(8,128)S(1)} %get-tuple-element.86.refs_3_), channel_id=1, source_target_pairs={{0,1},{1,0},{2,3},{3,2},{4,5},{5,4},{6,7},{7,6},{8,9},{9,8},{10,11... | collective-permute-start | bytes 1572872 | tf_op jit(solution)/shard_map/ppermute | solution.py:483
  108.3 15.9 %collective-permute-start.42 = (f32[128,256]{1,0:T(8,128)S(1)}, f32[128,256]{1,0:T(8,128)S(1)}, u32[]{:S(2)}, u32[]{:S(2)}) collective-permute-start(f32[128,256]{1,0:T(8,128)S(1)} %get-tuple-element.96), channel_id=1, source_target_pairs={{0,64},{32,96},{64,128},{96,160},{128,192},{160,224},{192,0},{224,... | collective-permute-start | bytes 393224 | tf_op jit(solution)/shard_map/ppermute | solution.py:56
  109.5 14.7 %collective-permute-start.43 = (f32[128,256]{1,0:T(8,128)S(1)}, f32[128,256]{1,0:T(8,128)S(1)}, u32[]{:S(2)}, u32[]{:S(2)}) collective-permute-start(f32[128,256]{1,0:T(8,128)S(1)} %get-tuple-element.97), channel_id=1, source_target_pairs={{0,128},{32,160},{64,192},{96,224},{128,0},{160,32},{192,64},{224,... | collective-permute-start | bytes 393224 | tf_op jit(solution)/shard_map/ppermute | solution.py:56
  111.6 12.6 %collective-permute-start.44 = (f32[128,256]{1,0:T(8,128)S(1)}, f32[128,256]{1,0:T(8,128)S(1)}, u32[]{:S(2)}, u32[]{:S(2)}) collective-permute-start(f32[128,256]{1,0:T(8,128)S(1)} %get-tuple-element.98), channel_id=1, source_target_pairs={{0,192},{32,224},{64,0},{96,32},{128,64},{160,96},{192,128},{224,1... | collective-permute-start | bytes 393224 | tf_op jit(solution)/shard_map/ppermute | solution.py:56
  114.2 1.3 collective-permute-start.37
  115.6 5.5 %collective-permute-start.38 = (f32[40,256]{1,0:T(8,128)S(1)}, f32[40,256]{1,0:T(8,128)S(1)}, u32[]{:S(2)}, u32[]{:S(2)}) collective-permute-start(f32[40,256]{1,0:T(8,128)S(1)} %add.43.piece), channel_id=1, source_target_pairs={{0,32},{32,0},{64,96},{96,64},{128,160},{160,128},{192,224},{224,1... | collective-permute-start | bytes 122888 | tf_op jit(solution)/shard_map/ppermute | solution.py:60
  121.1 8.3 %collective-permute-start.39 = (f32[208,256]{1,0:T(8,128)S(1)}, f32[208,256]{1,0:T(8,128)S(1)}, u32[]{:S(2)}, u32[]{:S(2)}) collective-permute-start(f32[208,256]{1,0:T(8,128)S(1)} %get-tuple-element.92), channel_id=1, source_target_pairs={{0,64},{32,96},{64,128},{96,160},{128,192},{160,224},{192,0},{224,... | collective-permute-start | bytes 638984 | tf_op jit(solution)/shard_map/ppermute | solution.py:56
  121.6 9.7 %collective-permute-start.40 = (f32[208,256]{1,0:T(8,128)S(1)}, f32[208,256]{1,0:T(8,128)S(1)}, u32[]{:S(2)}, u32[]{:S(2)}) collective-permute-start(f32[208,256]{1,0:T(8,128)S(1)} %get-tuple-element.93), channel_id=1, source_target_pairs={{0,128},{32,160},{64,192},{96,224},{128,0},{160,32},{192,64},{224,... | collective-permute-start | bytes 638984 | tf_op jit(solution)/shard_map/ppermute | solution.py:56
  124.2 9.3 %collective-permute-start.41 = (f32[208,256]{1,0:T(8,128)S(1)}, f32[208,256]{1,0:T(8,128)S(1)}, u32[]{:S(2)}, u32[]{:S(2)}) collective-permute-start(f32[208,256]{1,0:T(8,128)S(1)} %get-tuple-element.94), channel_id=1, source_target_pairs={{0,192},{32,224},{64,0},{96,32},{128,64},{160,96},{192,128},{224,1... | collective-permute-start | bytes 638984 | tf_op jit(solution)/shard_map/ppermute | solution.py:56
  124.3 9.3 %collective-permute-start.45 = (f32[128,256]{1,0:T(8,128)S(1)}, f32[128,256]{1,0:T(8,128)S(1)}, u32[]{:S(2)}, u32[]{:S(2)}) collective-permute-start(f32[128,256]{1,0:T(8,128)S(1)} %gather_sums.1), channel_id=1, source_target_pairs={{0,32},{32,0},{64,96},{96,64},{128,160},{160,128},{192,224},{224,1... | collective-permute-start | bytes 393224 | tf_op jit(solution)/shard_map/ppermute | solution.py:60
  133.5 1.0 copy-start.3
